TPU v7x, 256 devices: a whole 4x4x8 slice. The times are simulated.
256 devices in a mesh: dp: 64 (over z, y, x_hi), fsdp: 4 (over x_lo, core).
Axes of the slice: x: 4 (x_hi: 2, x_lo: 2; x = x_hi * 2 + x_lo), y: 4, z: 8, core: 2. Of those that a mesh axis runs over, the one named last changes fastest.
Arguments:
- images: float32 [256, 14, 14, 768], P(('dp', 'fsdp')), may hold values from -6 to 6
- dw_kernel: float32 [7, 7, 768], replicated, may hold values from -0.875 to 0.875
- norm_gain: float32 [768], replicated, may hold values from 0.5 to 1.5
- up_weight: float32 [768, 1536], P(None, 'fsdp'), may hold values from -0.21875 to 0.21875
- up_bias: float32 [1536], P('fsdp'), may hold values from -3 to 3
- down_weight: float32 [1536, 768], P('fsdp'), may hold values from -0.15625 to 0.15625
- layer_scale: float32 [768], replicated, may hold values from 0.5 to 1.5
- projection: float32 [768, 1152], replicated, may hold values from -0.21875 to 0.21875
- text_embed: float32 [256, 1152], P(('dp', 'fsdp')), may hold values from -0.18 to 0.18
- logit_scale: float32 [], replicated, may hold values from 4 to 12
- logit_bias: float32 [], replicated, may hold values from -4 to -2
Outputs:
- input_grad: float32 [256, 14, 14, 768], P(('dp', 'fsdp'))
- up_grad: float32 [64, 768, 1536], P('dp', None, 'fsdp')
- down_grad: float32 [64, 1536, 768], P('dp', 'fsdp')
- text_grad: float32 [256, 1152], P(('dp', 'fsdp'))
- loss_rows: float32 [256], P(('dp', 'fsdp'))
All inputs are finite; a program needn't handle non-finite values.
Results may differ from a plain program's by a relative error of at most 0.00026.
Values sent between devices are 32-bit elements; how exact they have to be, the bound alone decides.
No kernel may reach another device: no remote copies, remote signals or barrier semaphores. Data moves between devices by JAX's collectives and lax.ppermute only.
A program may use at most 128 MiB of HBM per device.

v0:
```python
import jax
import jax.numpy as jnp
from jax import lax
from jax.sharding import PartitionSpec as P


def passed_along(value, axis, by):
    peers = lax.axis_size(axis)
    return lax.ppermute(value, axis, [(i, (i + by) % peers) for i in range(peers)])


def conv_norm(images, dw_kernel, norm_gain):
    height = images.shape[1]
    width = images.shape[2]
    reach = dw_kernel.shape[0] // 2
    padded = jnp.pad(images, ((0, 0), (reach, reach), (reach, reach), (0, 0)))
    mixed = jnp.zeros_like(images)
    for row in range(dw_kernel.shape[0]):
        for column in range(dw_kernel.shape[1]):
            mixed = (
                mixed
                + padded[:, row : row + height, column : column + width, :] * dw_kernel[row, column]
            )
    center = jnp.mean(mixed, axis=-1, keepdims=True)
    spread = jnp.mean(jnp.square(mixed - center), axis=-1, keepdims=True)
    return (mixed - center) * lax.rsqrt(spread + 1e-06) * norm_gain


def pointwise(flat, first, bias_first, second):
    hidden_pre = (
        jnp.dot(flat, first, precision=lax.Precision.HIGHEST, preferred_element_type=jnp.float32)
        + bias_first
    )
    activated = jax.nn.gelu(hidden_pre, approximate=False)
    return jnp.dot(
        activated, second, precision=lax.Precision.HIGHEST, preferred_element_type=jnp.float32
    )


def pool_project(section_out, projection):
    pooled = jnp.mean(section_out, axis=(1, 2))
    return jnp.dot(
        pooled, projection, precision=lax.Precision.HIGHEST, preferred_element_type=jnp.float32
    )


def unit(vectors):
    return vectors * lax.rsqrt(jnp.sum(vectors * vectors, axis=-1, keepdims=True) + 1e-06)


def row_slopes(image_unit, text_block, my_rows, columns, logit_scale, logit_bias):
    logits = (
        logit_scale
        * jnp.dot(
            image_unit,
            text_block.T,
            precision=lax.Precision.HIGHEST,
            preferred_element_type=jnp.float32,
        )
        + logit_bias
    )
    match = (my_rows[:, None] == columns[None, :]).astype(jnp.float32)
    signs = 2.0 * match - 1.0
    losses = jnp.sum(jax.nn.softplus(-signs * logits), axis=1)
    slopes = jax.nn.sigmoid(logits) - match
    return (losses, slopes)


def pair_terms(image_unit, text_block, my_rows, columns, logit_scale, logit_bias):
    losses, slopes = row_slopes(image_unit, text_block, my_rows, columns, logit_scale, logit_bias)
    image_step = logit_scale * jnp.dot(
        slopes, text_block, precision=lax.Precision.HIGHEST, preferred_element_type=jnp.float32
    )
    text_step = logit_scale * jnp.dot(
        slopes.T, image_unit, precision=lax.Precision.HIGHEST, preferred_element_type=jnp.float32
    )
    return (losses, image_step, text_step)


def body(
    images,
    dw_kernel,
    norm_gain,
    up_weight,
    up_bias,
    down_weight,
    layer_scale,
    projection,
    text_embed,
    logit_scale,
    logit_bias,
):
    count = images.shape[0]
    channels = images.shape[3]
    normed, conv_back = jax.vjp(lambda values: conv_norm(values, dw_kernel, norm_gain), images)
    flat = normed.reshape(-1, channels)
    first, bias_first, second = (
        lax.all_gather(up_weight, "fsdp", axis=1, tiled=True),
        lax.all_gather(up_bias, "fsdp", axis=0, tiled=True),
        lax.all_gather(down_weight, "fsdp", axis=0, tiled=True),
    )
    branch, block_back = jax.vjp(
        lambda values, left, right: pointwise(values, left, bias_first, right), flat, first, second
    )
    section_out = images + layer_scale * branch.reshape(images.shape)
    features, head_back = jax.vjp(lambda values: pool_project(values, projection), section_out)
    image_unit, image_back = jax.vjp(unit, features)
    text_unit, text_back = jax.vjp(unit, text_embed)
    fsdp_size = lax.axis_size("fsdp")
    dp_size = lax.axis_size("dp")
    dp_index = lax.axis_index("dp")
    my_rows = (dp_index * fsdp_size + lax.axis_index("fsdp")) * count + jnp.arange(
        count, dtype=jnp.int32
    )
    text_block = lax.all_gather(text_unit, "fsdp", axis=0, tiled=True)
    group = text_block.shape[0]

    def visit(step, carry):
        block_now, accum, image_grad, losses = carry
        source = (dp_index - step) % dp_size
        columns = source * group + jnp.arange(group, dtype=jnp.int32)
        losses_step, image_step, text_step = pair_terms(
            image_unit, block_now, my_rows, columns, logit_scale, logit_bias
        )
        block_next, accum_next = passed_along((block_now, accum + text_step), "dp", 1)
        return (block_next, accum_next, image_grad + image_step, losses + losses_step)

    start = (
        text_block,
        jnp.zeros_like(text_block),
        jnp.zeros_like(image_unit),
        jnp.zeros((count,), jnp.float32),
    )
    finished = lax.fori_loop(0, dp_size, visit, start)
    image_grad = finished[2]
    losses = finished[3]
    text_grad_unit = lax.psum_scatter(finished[1], "fsdp", scatter_dimension=0, tiled=True)
    text_grad = text_back(text_grad_unit)[0]
    feature_grad = image_back(image_grad)[0]
    out_grad = head_back(feature_grad)[0]
    branch_grad = (layer_scale * out_grad).reshape(-1, channels)
    normed_grad, first_grad, second_grad = block_back(branch_grad)
    first_grad, second_grad = (
        lax.psum_scatter(first_grad, "fsdp", scatter_dimension=1, tiled=True),
        lax.psum_scatter(second_grad, "fsdp", scatter_dimension=0, tiled=True),
    )
    input_grad = out_grad + conv_back(normed_grad.reshape(images.shape))[0]
    return (input_grad, first_grad[None], second_grad[None], text_grad, losses)


def solution(mesh):
    placed = (
        P(("dp", "fsdp"), None, None, None),
        P(),
        P(),
        P(None, "fsdp"),
        P("fsdp"),
        P("fsdp", None),
        P(),
        P(),
        P(("dp", "fsdp"), None),
        P(),
        P(),
    )
    return jax.shard_map(
        body,
        mesh=mesh,
        in_specs=placed,
        out_specs=(
            P(("dp", "fsdp"), None, None, None),
            P("dp", None, "fsdp"),
            P("dp", "fsdp", None),
            P(("dp", "fsdp"), None),
            P(("dp", "fsdp")),
        ),
        check_vma=False,
    )
```

profile of v0, /device:TPU:1, one launch (start us, length us, event | category | flops | bytes accessed | tf_op | source)
XLA Modules:
  0.0 1352.7 jit_solution(1660978304498095065)
XLA Ops:
  10.1 8.6 all-gather.1
  20.1 5.3 all-gather
  29.0 6.4 fusion.126
  40.2 27.3 %all-gather.5.cloned.1.call-done = f32[768,1536]{1,0:T(8,128)} async-done(((f32[768,384]{1,0:T(8,128)}), f32[768,1536]{1,0:T(8,128)}) %all-gather.5.cloned.1.call-update) | async-done | bytes 4718608 | tf_op jit(solution)/shard_map/all_gather | solution.py:98
  67.5 6.8 convolution_add_fusion
  74.3 49.4 %all-gather.7.cloned.1.call-done = f32[1536,768]{1,0:T(8,128)} async-done(((f32[384,768]{1,0:T(8,128)}), f32[1536,768]{1,0:T(8,128)}) %all-gather.7.cloned.1.call-update) | async-done | bytes 4718608 | tf_op jit(solution)/shard_map/all_gather | solution.py:100
  123.7 9.5 fusion.113
  141.8 1002.9 %while.22 = (s32[]{:T(128)}, f32[4,1152]{1,0:T(4,128)}, f32[4,1152]{1,0:T(4,128)}, f32[1,1152]{1,0:T(1,128)}, f32[1]{0:T(128)}, /*index=5*/f32[]{:T(128)}, f32[1...) while((s32[]{:T(128)}, f32[4,1152]{1,0:T(4,128)}, ...), condition=%wide.region_7.8_spmd.clone, body=%wide.region_5.7_spmd.clone.sunk | while | flops 127968 | bytes 304684 | solution.py:134
  185.8 5.2 collective-permute-done.1
  263.8 5.2 collective-permute-done.1
  279.4 5.2 collective-permute-done.1
  326.2 5.2 collective-permute-done.1
  357.5 5.2 collective-permute-done.1
  373.1 5.2 collective-permute-done.1
  388.7 5.2 collective-permute-done.1
  451.1 5.4 collective-permute-done.1
  529.3 5.2 collective-permute-done.1
  544.9 5.2 collective-permute-done.1
  591.7 5.2 collective-permute-done.1
  607.3 5.6 collective-permute-done.1
  685.7 5.7 collective-permute-done.1
  826.6 5.2 collective-permute-done.1
  842.2 5.5 collective-permute-done.1
  920.5 5.4 collective-permute-done.1
  1076.7 5.6 collective-permute-done.1
  1151.8 9.2 multiply_add_fusion.1
  1160.9 5.8 fusion.129
  1168.0 8.6 fusion.112
  1178.0 7.2 multiply_reduce_fusion.3
  1196.7 8.9 pad_add_fusion
  1207.5 83.4 %all-reduce.50 = f32[4,1152]{1,0:T(4,128)} all-reduce(f32[4,1152]{1,0:T(4,128)} %get-tuple-element.252), channel_id=4, replica_groups=mesh['dp'=64,'fsdp'=4] {'fsdp'}, use_global_device_ids=true, to_apply=%region_14.15.clone | all-reduce | flops 4608 | bytes 36864
  1295.4 49.5 %reduce-scatter.5.cloned.1.call-done = f32[384,768]{1,0:T(8,128)} async-done(((f32[1536,768]{1,0:T(8,128)}), f32[384,768]{1,0:T(8,128)}) %reduce-scatter.5.cloned.1.call-update) | async-done | bytes 1179664 | tf_op jit(solution)/shard_map/reduce_scatter | solution.py:145
  (1065 shorter events, 919.8 us)
Async XLA Ops:
  7.2 60.3 %all-gather.5.cloned.1.call-start = ((), (), s32[]{:S(2)}) async-start(), calls=%async_computation.2 | async-start | bytes 5898240 | tf_op jit(solution)/shard_map/all_gather | solution.py:98
  7.9 115.8 %all-gather.7.cloned.1.call-start = ((), (), s32[]{:S(2)}) async-start(), calls=%async_computation.3 | async-start | bytes 5898240 | tf_op jit(solution)/shard_map/all_gather | solution.py:100
  8.7 1286.7 %reduce-scatter.3.cloned.1.call-start = ((), (), s32[]{:S(2)}) async-start(), calls=%async_computation.4 | async-start | bytes 5898240 | tf_op jit(solution)/shard_map/reduce_scatter | solution.py:144
  143.1 16.7 %collective-permute-start = (f32[4,1152]{1,0:T(4,128)}, f32[4,1152]{1,0:T(4,128)}, u32[]{:S(2)}, u32[]{:S(2)}) collective-permute-start(f32[4,1152]{1,0:T(4,128)} %copy.40), channel_id=1, source_target_pairs={{0,4},{4,8},{8,12},{12,16},{16,20},{20,24},{24,28},{28,32},{32,36}... | collective-permute-start | bytes 55304 | tf_op jit(solution)/shard_map/while/body/eval_jaxpr/ppermute | solution.py:9
  176.7 14.3 %collective-permute-start = (f32[4,1152]{1,0:T(4,128)}, f32[4,1152]{1,0:T(4,128)}, u32[]{:S(2)}, u32[]{:S(2)}) collective-permute-start(f32[4,1152]{1,0:T(4,128)} %copy.40), channel_id=1, source_target_pairs={{0,4},{4,8},{8,12},{12,16},{16,20},{20,24},{24,28},{28,32},{32,36}... | collective-permute-start | bytes 55304 | tf_op jit(solution)/shard_map/while/body/eval_jaxpr/ppermute | solution.py:9
  207.9 14.3 %collective-permute-start = (f32[4,1152]{1,0:T(4,128)}, f32[4,1152]{1,0:T(4,128)}, u32[]{:S(2)}, u32[]{:S(2)}) collective-permute-start(f32[4,1152]{1,0:T(4,128)} %copy.40), channel_id=1, source_target_pairs={{0,4},{4,8},{8,12},{12,16},{16,20},{20,24},{24,28},{28,32},{32,36}... | collective-permute-start | bytes 55304 | tf_op jit(solution)/shard_map/while/body/eval_jaxpr/ppermute | solution.py:9
  239.2 14.3 %collective-permute-start = (f32[4,1152]{1,0:T(4,128)}, f32[4,1152]{1,0:T(4,128)}, u32[]{:S(2)}, u32[]{:S(2)}) collective-permute-start(f32[4,1152]{1,0:T(4,128)} %copy.40), channel_id=1, source_target_pairs={{0,4},{4,8},{8,12},{12,16},{16,20},{20,24},{24,28},{28,32},{32,36}... | collective-permute-start | bytes 55304 | tf_op jit(solution)/shard_map/while/body/eval_jaxpr/ppermute | solution.py:9
  254.8 14.3 %collective-permute-start = (f32[4,1152]{1,0:T(4,128)}, f32[4,1152]{1,0:T(4,128)}, u32[]{:S(2)}, u32[]{:S(2)}) collective-permute-start(f32[4,1152]{1,0:T(4,128)} %copy.40), channel_id=1, source_target_pairs={{0,4},{4,8},{8,12},{12,16},{16,20},{20,24},{24,28},{28,32},{32,36}... | collective-permute-start | bytes 55304 | tf_op jit(solution)/shard_map/while/body/eval_jaxpr/ppermute | solution.py:9
  270.4 14.3 %collective-permute-start = (f32[4,1152]{1,0:T(4,128)}, f32[4,1152]{1,0:T(4,128)}, u32[]{:S(2)}, u32[]{:S(2)}) collective-permute-start(f32[4,1152]{1,0:T(4,128)} %copy.40), channel_id=1, source_target_pairs={{0,4},{4,8},{8,12},{12,16},{16,20},{20,24},{24,28},{28,32},{32,36}... | collective-permute-start | bytes 55304 | tf_op jit(solution)/shard_map/while/body/eval_jaxpr/ppermute | solution.py:9
  286.0 14.3 %collective-permute-start = (f32[4,1152]{1,0:T(4,128)}, f32[4,1152]{1,0:T(4,128)}, u32[]{:S(2)}, u32[]{:S(2)}) collective-permute-start(f32[4,1152]{1,0:T(4,128)} %copy.40), channel_id=1, source_target_pairs={{0,4},{4,8},{8,12},{12,16},{16,20},{20,24},{24,28},{28,32},{32,36}... | collective-permute-start | bytes 55304 | tf_op jit(solution)/shard_map/while/body/eval_jaxpr/ppermute | solution.py:9
  301.6 14.3 %collective-permute-start = (f32[4,1152]{1,0:T(4,128)}, f32[4,1152]{1,0:T(4,128)}, u32[]{:S(2)}, u32[]{:S(2)}) collective-permute-start(f32[4,1152]{1,0:T(4,128)} %copy.40), channel_id=1, source_target_pairs={{0,4},{4,8},{8,12},{12,16},{16,20},{20,24},{24,28},{28,32},{32,36}... | collective-permute-start | bytes 55304 | tf_op jit(solution)/shard_map/while/body/eval_jaxpr/ppermute | solution.py:9
  317.2 14.3 %collective-permute-start = (f32[4,1152]{1,0:T(4,128)}, f32[4,1152]{1,0:T(4,128)}, u32[]{:S(2)}, u32[]{:S(2)}) collective-permute-start(f32[4,1152]{1,0:T(4,128)} %copy.40), channel_id=1, source_target_pairs={{0,4},{4,8},{8,12},{12,16},{16,20},{20,24},{24,28},{28,32},{32,36}... | collective-permute-start | bytes 55304 | tf_op jit(solution)/shard_map/while/body/eval_jaxpr/ppermute | solution.py:9
  332.8 14.3 %collective-permute-start = (f32[4,1152]{1,0:T(4,128)}, f32[4,1152]{1,0:T(4,128)}, u32[]{:S(2)}, u32[]{:S(2)}) collective-permute-start(f32[4,1152]{1,0:T(4,128)} %copy.40), channel_id=1, source_target_pairs={{0,4},{4,8},{8,12},{12,16},{16,20},{20,24},{24,28},{28,32},{32,36}... | collective-permute-start | bytes 55304 | tf_op jit(solution)/shard_map/while/body/eval_jaxpr/ppermute | solution.py:9
  348.4 14.3 %collective-permute-start = (f32[4,1152]{1,0:T(4,128)}, f32[4,1152]{1,0:T(4,128)}, u32[]{:S(2)}, u32[]{:S(2)}) collective-permute-start(f32[4,1152]{1,0:T(4,128)} %copy.40), channel_id=1, source_target_pairs={{0,4},{4,8},{8,12},{12,16},{16,20},{20,24},{24,28},{28,32},{32,36}... | collective-permute-start | bytes 55304 | tf_op jit(solution)/shard_map/while/body/eval_jaxpr/ppermute | solution.py:9
  364.0 14.3 %collective-permute-start = (f32[4,1152]{1,0:T(4,128)}, f32[4,1152]{1,0:T(4,128)}, u32[]{:S(2)}, u32[]{:S(2)}) collective-permute-start(f32[4,1152]{1,0:T(4,128)} %copy.40), channel_id=1, source_target_pairs={{0,4},{4,8},{8,12},{12,16},{16,20},{20,24},{24,28},{28,32},{32,36}... | collective-permute-start | bytes 55304 | tf_op jit(solution)/shard_map/while/body/eval_jaxpr/ppermute | solution.py:9
  379.6 14.3 %collective-permute-start = (f32[4,1152]{1,0:T(4,128)}, f32[4,1152]{1,0:T(4,128)}, u32[]{:S(2)}, u32[]{:S(2)}) collective-permute-start(f32[4,1152]{1,0:T(4,128)} %copy.40), channel_id=1, source_target_pairs={{0,4},{4,8},{8,12},{12,16},{16,20},{20,24},{24,28},{28,32},{32,36}... | collective-permute-start | bytes 55304 | tf_op jit(solution)/shard_map/while/body/eval_jaxpr/ppermute | solution.py:9
  410.8 14.3 %collective-permute-start = (f32[4,1152]{1,0:T(4,128)}, f32[4,1152]{1,0:T(4,128)}, u32[]{:S(2)}, u32[]{:S(2)}) collective-permute-start(f32[4,1152]{1,0:T(4,128)} %copy.40), channel_id=1, source_target_pairs={{0,4},{4,8},{8,12},{12,16},{16,20},{20,24},{24,28},{28,32},{32,36}... | collective-permute-start | bytes 55304 | tf_op jit(solution)/shard_map/while/body/eval_jaxpr/ppermute | solution.py:9
  442.0 14.4 %collective-permute-start = (f32[4,1152]{1,0:T(4,128)}, f32[4,1152]{1,0:T(4,128)}, u32[]{:S(2)}, u32[]{:S(2)}) collective-permute-start(f32[4,1152]{1,0:T(4,128)} %copy.40), channel_id=1, source_target_pairs={{0,4},{4,8},{8,12},{12,16},{16,20},{20,24},{24,28},{28,32},{32,36}... | collective-permute-start | bytes 55304 | tf_op jit(solution)/shard_map/while/body/eval_jaxpr/ppermute | solution.py:9
  457.8 14.3 %collective-permute-start = (f32[4,1152]{1,0:T(4,128)}, f32[4,1152]{1,0:T(4,128)}, u32[]{:S(2)}, u32[]{:S(2)}) collective-permute-start(f32[4,1152]{1,0:T(4,128)} %copy.40), channel_id=1, source_target_pairs={{0,4},{4,8},{8,12},{12,16},{16,20},{20,24},{24,28},{28,32},{32,36}... | collective-permute-start | bytes 55304 | tf_op jit(solution)/shard_map/while/body/eval_jaxpr/ppermute | solution.py:9
  473.4 14.3 %collective-permute-start = (f32[4,1152]{1,0:T(4,128)}, f32[4,1152]{1,0:T(4,128)}, u32[]{:S(2)}, u32[]{:S(2)}) collective-permute-start(f32[4,1152]{1,0:T(4,128)} %copy.40), channel_id=1, source_target_pairs={{0,4},{4,8},{8,12},{12,16},{16,20},{20,24},{24,28},{28,32},{32,36}... | collective-permute-start | bytes 55304 | tf_op jit(solution)/shard_map/while/body/eval_jaxpr/ppermute | solution.py:9
  504.6 14.3 %collective-permute-start = (f32[4,1152]{1,0:T(4,128)}, f32[4,1152]{1,0:T(4,128)}, u32[]{:S(2)}, u32[]{:S(2)}) collective-permute-start(f32[4,1152]{1,0:T(4,128)} %copy.40), channel_id=1, source_target_pairs={{0,4},{4,8},{8,12},{12,16},{16,20},{20,24},{24,28},{28,32},{32,36}... | collective-permute-start | bytes 55304 | tf_op jit(solution)/shard_map/while/body/eval_jaxpr/ppermute | solution.py:9
  535.8 14.3 %collective-permute-start = (f32[4,1152]{1,0:T(4,128)}, f32[4,1152]{1,0:T(4,128)}, u32[]{:S(2)}, u32[]{:S(2)}) collective-permute-start(f32[4,1152]{1,0:T(4,128)} %copy.40), channel_id=1, source_target_pairs={{0,4},{4,8},{8,12},{12,16},{16,20},{20,24},{24,28},{28,32},{32,36}... | collective-permute-start | bytes 55304 | tf_op jit(solution)/shard_map/while/body/eval_jaxpr/ppermute | solution.py:9
  567.0 14.3 %collective-permute-start = (f32[4,1152]{1,0:T(4,128)}, f32[4,1152]{1,0:T(4,128)}, u32[]{:S(2)}, u32[]{:S(2)}) collective-permute-start(f32[4,1152]{1,0:T(4,128)} %copy.40), channel_id=1, source_target_pairs={{0,4},{4,8},{8,12},{12,16},{16,20},{20,24},{24,28},{28,32},{32,36}... | collective-permute-start | bytes 55304 | tf_op jit(solution)/shard_map/while/body/eval_jaxpr/ppermute | solution.py:9
  582.6 14.3 %collective-permute-start = (f32[4,1152]{1,0:T(4,128)}, f32[4,1152]{1,0:T(4,128)}, u32[]{:S(2)}, u32[]{:S(2)}) collective-permute-start(f32[4,1152]{1,0:T(4,128)} %copy.40), channel_id=1, source_target_pairs={{0,4},{4,8},{8,12},{12,16},{16,20},{20,24},{24,28},{28,32},{32,36}... | collective-permute-start | bytes 55304 | tf_op jit(solution)/shard_map/while/body/eval_jaxpr/ppermute | solution.py:9
  598.3 14.6 %collective-permute-start = (f32[4,1152]{1,0:T(4,128)}, f32[4,1152]{1,0:T(4,128)}, u32[]{:S(2)}, u32[]{:S(2)}) collective-permute-start(f32[4,1152]{1,0:T(4,128)} %copy.40), channel_id=1, source_target_pairs={{0,4},{4,8},{8,12},{12,16},{16,20},{20,24},{24,28},{28,32},{32,36}... | collective-permute-start | bytes 55304 | tf_op jit(solution)/shard_map/while/body/eval_jaxpr/ppermute | solution.py:9
  614.2 14.3 %collective-permute-start = (f32[4,1152]{1,0:T(4,128)}, f32[4,1152]{1,0:T(4,128)}, u32[]{:S(2)}, u32[]{:S(2)}) collective-permute-start(f32[4,1152]{1,0:T(4,128)} %copy.40), channel_id=1, source_target_pairs={{0,4},{4,8},{8,12},{12,16},{16,20},{20,24},{24,28},{28,32},{32,36}... | collective-permute-start | bytes 55304 | tf_op jit(solution)/shard_map/while/body/eval_jaxpr/ppermute | solution.py:9
  645.4 14.3 %collective-permute-start = (f32[4,1152]{1,0:T(4,128)}, f32[4,1152]{1,0:T(4,128)}, u32[]{:S(2)}, u32[]{:S(2)}) collective-permute-start(f32[4,1152]{1,0:T(4,128)} %copy.40), channel_id=1, source_target_pairs={{0,4},{4,8},{8,12},{12,16},{16,20},{20,24},{24,28},{28,32},{32,36}... | collective-permute-start | bytes 55304 | tf_op jit(solution)/shard_map/while/body/eval_jaxpr/ppermute | solution.py:9
  676.6 14.7 %collective-permute-start = (f32[4,1152]{1,0:T(4,128)}, f32[4,1152]{1,0:T(4,128)}, u32[]{:S(2)}, u32[]{:S(2)}) collective-permute-start(f32[4,1152]{1,0:T(4,128)} %copy.40), channel_id=1, source_target_pairs={{0,4},{4,8},{8,12},{12,16},{16,20},{20,24},{24,28},{28,32},{32,36}... | collective-permute-start | bytes 55304 | tf_op jit(solution)/shard_map/while/body/eval_jaxpr/ppermute | solution.py:9
  833.1 14.6 %collective-permute-start = (f32[4,1152]{1,0:T(4,128)}, f32[4,1152]{1,0:T(4,128)}, u32[]{:S(2)}, u32[]{:S(2)}) collective-permute-start(f32[4,1152]{1,0:T(4,128)} %copy.40), channel_id=1, source_target_pairs={{0,4},{4,8},{8,12},{12,16},{16,20},{20,24},{24,28},{28,32},{32,36}... | collective-permute-start | bytes 55304 | tf_op jit(solution)/shard_map/while/body/eval_jaxpr/ppermute | solution.py:9
  911.4 14.4 %collective-permute-start = (f32[4,1152]{1,0:T(4,128)}, f32[4,1152]{1,0:T(4,128)}, u32[]{:S(2)}, u32[]{:S(2)}) collective-permute-start(f32[4,1152]{1,0:T(4,128)} %copy.40), channel_id=1, source_target_pairs={{0,4},{4,8},{8,12},{12,16},{16,20},{20,24},{24,28},{28,32},{32,36}... | collective-permute-start | bytes 55304 | tf_op jit(solution)/shard_map/while/body/eval_jaxpr/ppermute | solution.py:9
  1067.7 14.6 %collective-permute-start = (f32[4,1152]{1,0:T(4,128)}, f32[4,1152]{1,0:T(4,128)}, u32[]{:S(2)}, u32[]{:S(2)}) collective-permute-start(f32[4,1152]{1,0:T(4,128)} %copy.40), channel_id=1, source_target_pairs={{0,4},{4,8},{8,12},{12,16},{16,20},{20,24},{24,28},{28,32},{32,36}... | collective-permute-start | bytes 55304 | tf_op jit(solution)/shard_map/while/body/eval_jaxpr/ppermute | solution.py:9
  1166.8 178.1 %reduce-scatter.5.cloned.1.call-start = ((), (), s32[]{:S(2)}) async-start(), calls=%async_computation.5 | async-start | bytes 5898240 | tf_op jit(solution)/shard_map/reduce_scatter | solution.py:145
  (261 other events, 2014.4 us)
Sparse Core Ops, SparseCore 0:
  9.8 57.6 all-gather.4
  69.3 54.3 all-gather.6
  1166.9 121.4 reduce-scatter.2
  1291.4 53.4 reduce-scatter.4
where the time goes:
time: 1380 us; the launch traced here: 1350 us
  waiting for transfers between devices  462 us (33%)
  other arithmetic  336 us (24%)
  matrix products  294 us (21%)
  local copies, waits for them, and re-layouts  101 us (7%)
  blocking collectives  97.3 us (7%)
  loops' own time  37.4 us (3%)
  between operations  19.3 us (1%)
    ppermute x128, waiting for transfers between devices, passed_along(): lax.ppermute(value, axis, [(i, (i + by) % peers) for i in range(peers)])  334 us
    dot_general x64, matrix products, row_slopes(): jnp.dot(image_unit, text_block.T, precision=lax.Precision.HIGHEST, prefer...  183 us
    add x64, other arithmetic, visit(): accum + text_step  131 us
    while x192, local copies, waits for them, and re-layouts  85.4 us
    unnamed x1, blocking collectives  83.4 us
    add x64, other arithmetic, visit(): image_grad + image_step  82.1 us
    dot_general x64, matrix products, pair_terms(): jnp.dot(slopes, text_block, precision=lax.Precision.HIGHEST, preferred_el...  58.2 us
    reduce_scatter x1, waiting for transfers between devices, body(): lax.psum_scatter(second_grad, 'fsdp', scatter_dimension=0, tiled=True)  49.5 us
  transfers between devices with their start and end apart: 132, of which 67 were waited for; matrix products, arithmetic and copies ran while one was open for 45% of the time, Pallas kernels for 0%

commit v1 on v0

v1 whole, which is shorter than its diff:
```python
import functools

import jax
import jax.numpy as jnp
from jax import lax
from jax.experimental import pallas as pl
from jax.experimental.pallas import tpu as pltpu
from jax.sharding import PartitionSpec as P

LANES = 128
HIGH = lax.Precision.HIGH
HIGHEST = lax.Precision.HIGHEST
VMEM = pl.BlockSpec(memory_space=pltpu.VMEM)
SMEM = pl.BlockSpec(memory_space=pltpu.SMEM)
F32 = jnp.float32


HBM = pl.BlockSpec(memory_space=pltpu.HBM)


def call(kernel, outs, specs, scratch=(), mib=24, flops=0, moved=0):
    return pl.pallas_call(
        kernel,
        out_shape=[jax.ShapeDtypeStruct(shape, F32) for shape in outs],
        in_specs=specs,
        out_specs=[VMEM] * len(outs),
        scratch_shapes=list(scratch),
        compiler_params=pltpu.CompilerParams(vmem_limit_bytes=mib << 20),
        cost_estimate=pl.CostEstimate(flops=flops, bytes_accessed=moved, transcendentals=0),
    )


def fetch(pairs, sems):
    copies = [
        pltpu.make_async_copy(source, target, sems.at[i])
        for i, (source, target) in enumerate(pairs)
    ]
    for copy in copies:
        copy.start()
    return copies


def dot(left, right, precision, dims=((1,), (0,))):
    return lax.dot_general(
        left, right, (dims, ((), ())), precision=precision, preferred_element_type=F32
    )


def lanes_of(tile):
    return pl.ds(pl.multiple_of(tile * LANES, LANES), LANES)


def convolve(pad, w_ref, tile, side, flip):
    taps = w_ref.shape[0]
    halves = []
    for half in range(2):
        total = jnp.zeros((side, 8, LANES), F32)
        for q in range(taps):
            column = pad[tile, :, pl.ds(q + 8 * half, 8), :]
            for p in range(taps):
                row = taps - 1 - p if flip else p
                col = taps - 1 - q if flip else q
                total = total + column[p : p + side] * w_ref[row, pl.ds(col, 1), lanes_of(tile)]
        halves.append(total)
    return halves


def front_kernel(
    x_hbm, w_hbm, gain_hbm, normed_ref, unit_ref, rstd_ref, sum_ref, x_ref, w_ref, gain_ref, pad, mixed, sems
):
    tiles, side = unit_ref.shape[0], unit_ref.shape[1]
    reach = w_ref.shape[0] // 2
    channels = tiles * LANES
    copies = fetch(((x_hbm, x_ref), (w_hbm, w_ref), (gain_hbm, gain_ref.at[0])), sems)
    pad[...] = jnp.zeros_like(pad)
    for copy in copies:
        copy.wait()
    for tile in range(tiles):
        total = jnp.zeros((side, LANES), F32)
        for h in range(side):
            row = x_ref[pl.ds(h * side * tiles + tile, side, stride=tiles), :]
            pad[tile, reach + h, pl.ds(reach, side), :] = row
            total = total + row
        sum_ref[:, tile * LANES : (tile + 1) * LANES] = jnp.sum(total, axis=0, keepdims=True)

    @pl.loop(0, tiles)
    def _(tile):
        low, high = convolve(pad, w_ref, tile, side, False)
        mixed[tile, :, 0:8, :] = low
        mixed[tile, :, 8:16, :] = high

    total = mixed[0]
    for tile in range(1, tiles):
        total = total + mixed[tile]
    mean = jnp.sum(total, axis=-1, keepdims=True) * (1.0 / channels)
    square = jnp.zeros((side, 16, LANES), F32)
    for tile in range(tiles):
        off = mixed[tile] - mean
        square = square + off * off
    rstd = lax.rsqrt(jnp.sum(square, axis=-1, keepdims=True) * (1.0 / channels) + 1e-06)
    rstd_ref[...] = jnp.broadcast_to(rstd, rstd_ref.shape)
    for tile in range(tiles):
        lanes = slice(tile * LANES, (tile + 1) * LANES)
        unit = (mixed[tile] - mean) * rstd
        unit_ref[tile] = unit
        out = unit * gain_ref[:, lanes]
        for h in range(side):
            normed_ref[h * side : (h + 1) * side, lanes] = out[h, :side]


def front(images, dw_kernel, norm_gain):
    side, taps = images.shape[1], dw_kernel.shape[0]
    channels = images.shape[3]
    tiles = channels // LANES
    return call(
        front_kernel,
        [(side * side, channels), (tiles, side, 16, LANES), (side, 16, LANES), (1, channels)],
        [HBM] * 3,
        [
            pltpu.VMEM((side * side * tiles, LANES), F32),
            pltpu.VMEM(dw_kernel.shape, F32),
            pltpu.VMEM((1, channels), F32),
            pltpu.VMEM((tiles, side + taps - 1, 24, LANES), F32),
            pltpu.VMEM((tiles, side, 16, LANES), F32),
            pltpu.SemaphoreType.DMA((3,)),
        ],
        mib=16,
        flops=side * side * channels * 2 * taps * taps,
        moved=8 * images.size,
    )(images.reshape(-1, LANES), dw_kernel, norm_gain)


def mlp_kernel(
    own_ref, across_ref, up_hbm, up_sib_ref, bias_hbm, bias_sib_hbm, down_hbm, down_sib_ref, scale_hbm, sum_ref,
    slope_ref, hidden_ref, part_ref, up_ref, bias_ref, down_ref, scale_ref, sems,
):
    positions = slope_ref.shape[2]
    width = up_ref.shape[1]
    copies = fetch(
        (
            (up_hbm, up_ref),
            (bias_hbm, bias_ref.at[0]),
            (bias_sib_hbm, bias_ref.at[1]),
            (down_hbm, down_ref),
            (scale_hbm, scale_ref.at[0]),
        ),
        sems,
    )
    for copy in copies[:3]:
        copy.wait()
    for k, normed in enumerate((own_ref, across_ref)):
        for s, weight in enumerate((up_ref, up_sib_ref)):
            pre = dot(normed[...], weight[...], HIGH) + bias_ref[pl.ds(s, 1), :]
            cdf = 0.5 * (1.0 + lax.erf(pre * (0.5**0.5)))
            slope_ref[k, s] = cdf + pre * (jnp.exp(-0.5 * pre * pre) * 0.3989422804014327)
            hidden_ref[pl.ds(k, 1), s * width : (s + 1) * width] = jnp.sum(
                pre * cdf, axis=0, keepdims=True
            )
    for copy in copies[3:]:
        copy.wait()
    hidden = hidden_ref[...]
    part = dot(hidden[:, :width], down_ref[...], HIGH) + dot(hidden[:, width:], down_sib_ref[...], HIGH)
    part = part * scale_ref[...]
    own = lax.broadcasted_iota(jnp.int32, part.shape, 0) == 0
    part = part + jnp.where(own, sum_ref[...], 0.0)
    part_ref[...] = part * (1.0 / positions)


def mlp(own, across, up, up_sib, bias, bias_sib, down, down_sib, scale, image_sum):
    positions, channels = own.shape
    hidden = up.shape[1]
    return call(
        mlp_kernel,
        [(2, 2, positions, hidden), (2, 2 * hidden), (2, channels)],
        [VMEM, VMEM, HBM, VMEM, HBM, HBM, HBM, VMEM, HBM, VMEM],
        [
            pltpu.VMEM(up.shape, F32),
            pltpu.VMEM((2, hidden), F32),
            pltpu.VMEM(down.shape, F32),
            pltpu.VMEM((1, channels), F32),
            pltpu.SemaphoreType.DMA((5,)),
        ],
        mib=24,
        flops=24 * positions * channels * hidden,
        moved=4 * (2 * positions * (channels + 2 * hidden) + 4 * channels * hidden),
    )(own, across, up, up_sib, bias, bias_sib, down, down_sib, scale, image_sum)


def normal(rows):
    inverse = lax.rsqrt(jnp.sum(rows * rows, axis=-1, keepdims=True) + 1e-06)
    return rows * inverse, inverse


def pair_kernel(
    mine_ref, other_ref, proj_hbm, texts_ref, texts_sib_ref, dp_ref, scale_ref, shift_ref,
    unit_ref, spread_ref, inverse_ref, packed_ref, proj_ref, pooled, sems,
):
    copies = fetch(((proj_hbm, proj_ref),), sems)
    embed = unit_ref.shape[1]
    text, _ = normal(texts_ref[...])
    text_sib, _ = normal(texts_sib_ref[...])
    pooled[pl.ds(0, 1), :] = mine_ref[pl.ds(0, 1), :] + other_ref[pl.ds(1, 1), :]
    pooled[pl.ds(1, 1), :] = mine_ref[pl.ds(1, 1), :] + other_ref[pl.ds(0, 1), :]
    for copy in copies:
        copy.wait()
    unit, inverse = normal(dot(pooled[...], proj_ref[...], HIGH))
    unit_ref[...] = unit
    inverse_ref[...] = jnp.broadcast_to(inverse, inverse_ref.shape)
    spread_ref[...] = jnp.broadcast_to(unit[0:1], spread_ref.shape)
    step = jnp.zeros(unit.shape, F32)
    losses = jnp.zeros((2, 1), F32)
    for s, block in enumerate((text, text_sib)):
        logits = scale_ref[0] * dot(unit, block, HIGH, ((1,), (1,))) + shift_ref[0]
        if s == 0:
            columns = lax.broadcasted_iota(jnp.int32, logits.shape, 1)
            place = lax.broadcasted_iota(jnp.int32, logits.shape, 0)
            match = jnp.where((place == 0) & (columns == dp_ref[0]), 1.0, 0.0)
        else:
            match = jnp.zeros(logits.shape, F32)
        flipped = (1.0 - 2.0 * match) * logits
        tail = jnp.log1p(jnp.exp(-jnp.abs(flipped)))
        losses = losses + jnp.sum(jnp.maximum(flipped, 0.0) + tail, axis=1, keepdims=True)
        slopes = 1.0 / (1.0 + jnp.exp(-logits)) - match
        step = step + dot(slopes, block, HIGH)
    packed_ref[:, :embed] = step * scale_ref[0]
    packed_ref[:, embed:] = jnp.broadcast_to(losses, (2, LANES))


def pairs(mine, other, projection, texts, texts_sib, dp, scale, shift):
    embed = projection.shape[1]
    return call(
        pair_kernel,
        [(2, embed), texts.shape, (2, LANES), (2, embed + LANES)],
        [VMEM, VMEM, HBM, VMEM, VMEM, SMEM, SMEM, SMEM],
        [
            pltpu.VMEM(projection.shape, F32),
            pltpu.VMEM(mine.shape, F32),
            pltpu.SemaphoreType.DMA((1,)),
        ],
        mib=16,
        flops=6 * 256 * projection.size,
        moved=4 * projection.size,
    )(mine, other, projection, texts, texts_sib, dp, scale, shift)


def slope_kernel(
    packed_ref, other_ref, unit_ref, inverse_ref, proj_hbm, scale_hbm, down_hbm, down_sib_ref, up_hbm, up_sib_ref,
    slope_ref, loss_ref, const_ref, branch_ref, grad_ref, out_ref,
    proj_ref, scale_ref, down_ref, up_ref, sums, sems,
):
    copies = fetch(
        ((proj_hbm, proj_ref), (scale_hbm, scale_ref.at[0]), (down_hbm, down_ref), (up_hbm, up_ref)), sems
    )
    embed = unit_ref.shape[1]
    width = down_ref.shape[0]
    positions = slope_ref.shape[2]
    sums[pl.ds(0, 1), :] = packed_ref[pl.ds(0, 1), :] + other_ref[pl.ds(1, 1), :]
    sums[pl.ds(1, 1), :] = packed_ref[pl.ds(1, 1), :] + other_ref[pl.ds(0, 1), :]
    loss_ref[...] = sums[0:1, embed:]
    step = sums[:, :embed]
    unit = unit_ref[...]
    grad = inverse_ref[:, 0:1] * (step - unit * jnp.sum(unit * step, axis=-1, keepdims=True))
    copies[0].wait()
    const = dot(grad, proj_ref[...], HIGH, ((1,), (1,))) * (1.0 / positions)
    const_ref[...] = const[0:1]
    copies[1].wait()
    branch = const * scale_ref[...]
    branch_ref[...] = branch
    copies[2].wait()
    grad_ref[:, :width] = dot(branch, down_ref[...], HIGH, ((1,), (1,)))
    grad_ref[:, width:] = dot(branch, down_sib_ref[...], HIGH, ((1,), (1,)))
    copies[3].wait()
    out_ref[...] = dot(
        slope_ref[1, 0] * grad_ref[1:2, :width], up_ref[...], HIGH, ((1,), (1,))
    ) + dot(slope_ref[1, 1] * grad_ref[1:2, width:], up_sib_ref[...], HIGH, ((1,), (1,)))


def slopes_of(packed, other, unit, inverse, projection, scale, down, down_sib, up, up_sib, slope):
    channels, embed = projection.shape
    positions, hidden = slope.shape[2], slope.shape[3]
    return call(
        slope_kernel,
        [(1, LANES), (1, channels), (2, channels), (2, 2 * hidden), (positions, channels)],
        [VMEM] * 4 + [HBM, HBM, HBM, VMEM, HBM, VMEM, VMEM],
        [
            pltpu.VMEM(projection.shape, F32),
            pltpu.VMEM((1, channels), F32),
            pltpu.VMEM(down.shape, F32),
            pltpu.VMEM(up.shape, F32),
            pltpu.VMEM(packed.shape, F32),
            pltpu.SemaphoreType.DMA((4,)),
        ],
        mib=24,
        flops=12 * positions * channels * hidden,
        moved=4 * projection.size,
    )(packed, other, unit, inverse, projection, scale, down, down_sib, up, up_sib, slope)


def weight_kernel(own_ref, across_ref, slope_ref, grad_ref, out_ref, *, shard):
    width = out_ref.shape[1]
    lanes = slice(shard * width, (shard + 1) * width)
    out_ref[...] = dot(own_ref[...], slope_ref[0, shard] * grad_ref[0:1, lanes], HIGH, ((0,), (0,)))
    out_ref[...] += dot(across_ref[...], slope_ref[1, shard] * grad_ref[1:2, lanes], HIGH, ((0,), (0,)))


def weight_grad(own, across, slope, grad, shard):
    positions, channels = own.shape
    hidden = slope.shape[3]
    return call(
        functools.partial(weight_kernel, shard=shard),
        [(channels, hidden)],
        [VMEM] * 4,
        mib=24,
        flops=12 * positions * channels * hidden,
        moved=4 * channels * hidden,
    )(own, across, slope, grad)[0]


def last_kernel(
    own_ref, across_ref, slope_ref, grad_ref, moved_ref, hidden_ref, hidden_sib_ref, branch_ref, branch_sib_ref,
    up_out, down_out,
):
    width = up_out.shape[1]
    up_out[...] = moved_ref[...] + dot(
        own_ref[...], slope_ref[0, 0] * grad_ref[0:1, :width], HIGH, ((0,), (0,))
    )
    up_out[...] += dot(across_ref[...], slope_ref[1, 0] * grad_ref[1:2, :width], HIGH, ((0,), (0,)))
    down_out[...] = dot(hidden_ref[:, :width], branch_ref[...], HIGH, ((0,), (0,))) + dot(
        hidden_sib_ref[:, width:], branch_sib_ref[...], HIGH, ((0,), (0,))
    )


def last_grads(own, across, slope, grad, moved, hidden, hidden_sib, branch, branch_sib):
    positions, channels = own.shape
    width = slope.shape[3]
    return call(
        last_kernel,
        [(channels, width), (width, channels)],
        [VMEM] * 9,
        mib=24,
        flops=12 * positions * channels * width,
        moved=12 * channels * width,
    )(own, across, slope, grad, moved, hidden, hidden_sib, branch, branch_sib)


def back_kernel(
    other_ref, slope_ref, grad_ref, up_hbm, up_sib_ref, unit_ref, rstd_ref, w_hbm, gain_hbm, const_ref,
    out_ref, up_ref, w_ref, gain_ref, pad, slope, normed, sems,
):
    tiles, side = unit_ref.shape[0], unit_ref.shape[1]
    reach = w_ref.shape[0] // 2
    channels = tiles * LANES
    width = up_ref.shape[1]
    copies = fetch(((up_hbm, up_ref), (w_hbm, w_ref), (gain_hbm, gain_ref.at[0])), sems)
    pad[...] = jnp.zeros_like(pad)
    slope[...] = jnp.zeros_like(slope)
    for copy in copies:
        copy.wait()
    normed[...] = other_ref[...] + (
        dot(slope_ref[0, 0] * grad_ref[0:1, :width], up_ref[...], HIGH, ((1,), (1,)))
        + dot(slope_ref[0, 1] * grad_ref[0:1, width:], up_sib_ref[...], HIGH, ((1,), (1,)))
    )
    first = jnp.zeros((side, 16, LANES), F32)
    second = jnp.zeros((side, 16, LANES), F32)
    for tile in range(tiles):
        lanes = slice(tile * LANES, (tile + 1) * LANES)
        for h in range(side):
            slope[tile, h, 0:side, :] = normed[h * side : (h + 1) * side, lanes] * gain_ref[:, lanes]
        first = first + slope[tile]
        second = second + slope[tile] * unit_ref[tile]
    first = jnp.sum(first, axis=-1, keepdims=True) * (1.0 / channels)
    second = jnp.sum(second, axis=-1, keepdims=True) * (1.0 / channels)
    rstd = rstd_ref[...]
    for tile in range(tiles):
        grad = rstd * (slope[tile] - first - unit_ref[tile] * second)
        for h in range(side):
            pad[tile, reach + h, pl.ds(reach, side), :] = grad[h, :side]

    @pl.loop(0, tiles)
    def _(tile):
        low, high = convolve(pad, w_ref, tile, side, True)
        slope[tile, :, 0:8, :] = low
        slope[tile, :, 8:16, :] = high

    for tile in range(tiles):
        const = const_ref[:, tile * LANES : (tile + 1) * LANES]
        for h in range(side):
            out_ref[pl.ds(h * side * tiles + tile, side, stride=tiles), :] = (
                slope[tile, h, 0:side, :] + const
            )


def back(other, slope, grad, up, up_sib, unit, rstd, dw_kernel, norm_gain, const):
    tiles, side = unit.shape[0], unit.shape[1]
    taps = dw_kernel.shape[0]
    channels = tiles * LANES
    return call(
        back_kernel,
        [(side * side * tiles, LANES)],
        [VMEM, VMEM, VMEM, HBM, VMEM, VMEM, VMEM, HBM, HBM, VMEM],
        [
            pltpu.VMEM(up.shape, F32),
            pltpu.VMEM(dw_kernel.shape, F32),
            pltpu.VMEM((1, channels), F32),
            pltpu.VMEM((tiles, side + taps - 1, 24, LANES), F32),
            pltpu.VMEM((tiles, side, 16, LANES), F32),
            pltpu.VMEM((side * side, channels), F32),
            pltpu.SemaphoreType.DMA((3,)),
        ],
        mib=24,
        flops=side * side * channels * 2 * taps * taps,
        moved=12 * side * side * channels,
    )(other, slope, grad, up, up_sib, unit, rstd, dw_kernel, norm_gain, const)[0]


def column_kernel(images_ref, t0_ref, t1_ref, t2_ref, t3_ref, dp_ref, scale_ref, shift_ref, o0, o1, o2, o3):
    images = images_ref[...]
    for k, (text, out) in enumerate(((t0_ref, o0), (t1_ref, o1), (t2_ref, o2), (t3_ref, o3))):
        unit, _ = normal(text[...])
        logits = scale_ref[0] * jnp.sum(images * unit, axis=-1, keepdims=True) + shift_ref[0]
        slopes = 1.0 / (1.0 + jnp.exp(-logits))
        if k == 0:
            rows = lax.broadcasted_iota(jnp.int32, logits.shape, 0)
            slopes = slopes - jnp.where(rows == dp_ref[0], 1.0, 0.0)
        out[...] = jnp.sum(images * (scale_ref[0] * slopes), axis=0, keepdims=True)


def columns_of(images, texts, dp, scale, shift):
    return call(
        column_kernel,
        [texts[0].shape] * 4,
        [VMEM] * 5 + [SMEM] * 3,
        mib=8,
        flops=16 * images.size,
        moved=4 * images.size,
    )(images, *texts, dp, scale, shift)


def text_kernel(text_ref, a_ref, b_ref, c_ref, d_ref, out_ref):
    unit, inverse = normal(text_ref[...])
    step = a_ref[...] + b_ref[...] + (c_ref[...] + d_ref[...])
    out_ref[...] = inverse * (step - unit * jnp.sum(unit * step, axis=-1, keepdims=True))


def text_grads(text, parts):
    return call(text_kernel, [text.shape], [VMEM] * 5, mib=8)(text, *parts)[0]


def swapped(value, by):
    peers = lax.axis_size("fsdp")
    return lax.ppermute(value, "fsdp", [(i, i ^ by) for i in range(peers)])


def spread_out(rows):
    return lax.all_to_all(rows, "dp", 0, 0, tiled=True)


def body(
    images,
    dw_kernel,
    norm_gain,
    up_weight,
    up_bias,
    down_weight,
    layer_scale,
    projection,
    text_embed,
    logit_scale,
    logit_bias,
):
    dp = lax.axis_index("dp").astype(jnp.int32)[None]
    scale, shift = logit_scale[None], logit_bias[None]
    up_sib, down_sib, bias_sib = swapped(up_weight, 1), swapped(down_weight, 1), swapped(up_bias, 1)
    group_texts = (text_embed,) + tuple(swapped(text_embed, k) for k in (1, 2, 3))

    normed, unit, rstd, image_sum = front(images, dw_kernel, norm_gain)
    across = swapped(normed, 2)
    texts = spread_out(jnp.broadcast_to(text_embed, (lax.axis_size("dp"), text_embed.shape[1])))
    texts_sib = swapped(texts, 1)
    slope, hidden, part = mlp(
        normed, across, up_weight, up_sib, up_bias, bias_sib, down_weight, down_sib, layer_scale, image_sum
    )
    image_unit, spread, inverse, packed = pairs(
        part, swapped(part, 2), projection, texts, texts_sib, dp, scale, shift
    )
    losses, const, branch, grad, across_grad = slopes_of(
        packed, swapped(packed, 2), image_unit, inverse, projection, layer_scale,
        down_weight, down_sib, up_weight, up_sib, slope,
    )
    other_grad = swapped(across_grad, 2)
    moved = swapped(weight_grad(normed, across, slope, grad, 1), 1)
    image_units = spread_out(spread)
    input_grad = back(
        other_grad, slope, grad, up_weight, up_sib, unit, rstd, dw_kernel, norm_gain, const
    )
    steps = columns_of(image_units, group_texts, dp, scale, shift)
    up_grad, down_grad = last_grads(
        normed, across, slope, grad, moved, hidden, swapped(hidden, 1), branch, swapped(branch, 1)
    )
    text_grad = text_grads(
        text_embed, (steps[0],) + tuple(swapped(steps[k], k) for k in (1, 2, 3))
    )
    return (
        input_grad.reshape(images.shape),
        up_grad[None],
        down_grad[None],
        text_grad,
        losses[0, :1],
    )


def solution(mesh):
    placed = (
        P(("dp", "fsdp"), None, None, None),
        P(),
        P(),
        P(None, "fsdp"),
        P("fsdp"),
        P("fsdp", None),
        P(),
        P(),
        P(("dp", "fsdp"), None),
        P(),
        P(),
    )
    return jax.shard_map(
        body,
        mesh=mesh,
        in_specs=placed,
        out_specs=(
            P(("dp", "fsdp"), None, None, None),
            P("dp", None, "fsdp"),
            P("dp", "fsdp", None),
            P(("dp", "fsdp"), None),
            P(("dp", "fsdp")),
        ),
        check_vma=False,
    )
```

time: 1380 us -> 128 us (0.09); the launches traced: 1350 us -> 127 us
  waiting for transfers between devices: 462 us -> 24.5 us
  other arithmetic: 336 us -> 0.71 us
  matrix products: 294 us -> 0 us
  blocking collectives: 97.3 us -> 0 us
  local copies, waits for them, and re-layouts: 101 us -> 16.3 us
  starting transfers between devices: 4.95 us -> 45.9 us
  Pallas kernels: 0 us -> 37.6 us
  loops' own time: 37.4 us -> 0 us
  between operations: 19.3 us -> 2.14 us
    ppermute x128 -> x17, waiting for transfers between devices: 334 us -> 8.96 us  [swapped(): return lax.ppermute(value, 'fsdp', [(i, i ^ by) for i in range(peers)])]
    dot_general x136 -> x0, matrix products: 294 us -> none  [the longest x64 183 us: row_slopes(): jnp.dot(image_unit, text_block.T, precision=lax.Precision.HIGHEST, prefer...]
    add x129 -> x0, other arithmetic: 214 us -> none  [the longest x64 131 us: visit(): accum + text_step]
    while x192 -> x0, local copies, waits for them, and re-layouts: 85.4 us -> none
    unnamed x1 -> x0, blocking collectives: 83.4 us -> none
    all_gather x2 -> x0, waiting for transfers between devices: 76.7 us -> none  [the longest x1 49.4 us: body(): lax.all_gather(down_weight, 'fsdp', axis=0, tiled=True)]
    mul x72 -> x0, other arithmetic: 52.5 us -> none  [the longest x64 41.6 us: pair_terms(): logit_scale * jnp.dot(slopes, text_block, precision=lax.Precision.HIGHEST...]
    reduce_scatter x2 -> x0, waiting for transfers between devices: 49.5 us -> none  [the longest x1 49.5 us: body(): lax.psum_scatter(second_grad, 'fsdp', scatter_dimension=0, tiled=True)]
  transfers between devices with their start and end apart: 132 -> 19, of which waited for: 67 -> 7; matrix products, arithmetic and copies ran while one was open for 45% -> 4% of each run, Pallas kernels for 0% -> 14%
where the time goes in v1:
time: 128 us; the launch traced here: 127 us
  starting transfers between devices  45.9 us (36%)
  Pallas kernels  37.6 us (29%)
  waiting for transfers between devices  24.5 us (19%)
  local copies, waits for them, and re-layouts  16.3 us (13%)
  between operations  2.14 us (2%)
    all_to_all x2, starting transfers between devices, spread_out(): return lax.all_to_all(rows, 'dp', 0, 0, tiled=True)  25.5 us
    ppermute x17, starting transfers between devices, swapped(): return lax.ppermute(value, 'fsdp', [(i, i ^ by) for i in range(peers)])  20.4 us
    all_to_all x2, waiting for transfers between devices, spread_out(): return lax.all_to_all(rows, 'dp', 0, 0, tiled=True)  15.6 us
    unnamed x40, local copies, waits for them, and re-layouts  14.4 us
    ppermute x17, waiting for transfers between devices, swapped(): return lax.ppermute(value, 'fsdp', [(i, i ^ by) for i in range(peers)])  8.96 us
    pallas_call x1, Pallas kernels, slopes_of(): call(slope_kernel, [(1, LANES), (1, channels), (2, channels), (2, 2 * hid...  8.26 us
    pallas_call x1, Pallas kernels, back(): call(back_kernel, [(side * side * tiles, LANES)], [VMEM, VMEM, VMEM, HBM,...  7.16 us
    pallas_call x1, Pallas kernels, mlp(): call(mlp_kernel, [(2, 2, positions, hidden), (2, 2 * hidden), (2, channel...  5.27 us
  transfers between devices with their start and end apart: 19, of which 7 were waited for; matrix products, arithmetic and copies ran while one was open for 4% of the time, Pallas kernels for 14%

profile of v1, /device:TPU:1, one launch (start us, length us, event | category | flops | bytes accessed | tf_op | source)
XLA Modules:
  0.0 127.3 jit_solution(4920377264776693123)
XLA Ops:
  0.6 3.3 %collective-permute-start.3 = (f32[384,768]{1,0:T(8,128)}, f32[384,768]{1,0:T(8,128)}, u32[]{:S(2)}, u32[]{:S(2)}) collective-permute-start(f32[384,768]{1,0:T(8,128)} %down_hbm.3), channel_id=1, source_target_pairs={{0,1},{1,0},{2,3},{3,2},{4,5},{5,4},{6,7},{7,6},{8,9},{9,8},{10,11... | collective-permute-start | bytes 3538952 | tf_op jit(solution)/shard_map/ppermute | solution.py:451
  5.6 12.8 %all-to-all-start = ((f32[64,1,1152]{2,1,0:T(1,128)}), f32[64,1,1152]{2,1,0:T(1,128)}, u32[]{:S(2)}, u32[]{:S(2)}) async-start(f32[64,1,1152]{2,1,0:T(1,128)} %broadcast_in_dim.20), calls=%async_computation | async-start | bytes 589824 | tf_op jit(solution)/shard_map/all_to_all | solution.py:455
  18.4 0.9 copy-done.9
  19.4 1.1 copy-done.13
  21.1 4.1 %shard_map.149 = (f32[196,768]{1,0:T(8,128)S(1)}, f32[6,14,16,128]{3,2,1,0:T(8,128)S(1)}, f32[14,16,128]{2,1,0:T(8,128)S(1)}, f32[1,768]{1,0:T(1,128)S(1)}) custom-call(f32[1176,128]{1,0:T(8,128)S(1)} %bitcast.21, f32[7,7,768]{2,1,0:T(8,128)S(1)} %copy-done.9, f32[768]{0:T(1024)S(1)} %copy-done.16), custom_call_target="tpu_custom_call" | custom-call | flops 14751744 | bytes 1204224 | tf_op jit(solution)/shard_map/pallas_call | solution.py:115
  26.4 4.9 %all-to-all-done = f32[64,1,1152]{2,1,0:T(1,128)} async-done(((f32[64,1,1152]{2,1,0:T(1,128)}), f32[64,1,1152]{2,1,0:T(1,128)}, u32[]{:S(2)}, u32[]{:S(2)}) %all-to-all-start) | async-done | bytes 294944 | tf_op jit(solution)/shard_map/all_to_all | solution.py:455
  31.3 1.0 copy.25
  32.3 2.8 %collective-permute-start.5 = (f32[64,1152]{1,0:T(8,128)S(1)}, f32[64,1152]{1,0:T(8,128)}, u32[]{:S(2)}, u32[]{:S(2)}) collective-permute-start(f32[64,1152]{1,0:T(8,128)S(1)} %bitcast.22), channel_id=1, source_target_pairs={{0,1},{1,0},{2,3},{3,2},{4,5},{5,4},{6,7},{7,6},{8,9},{9,8},{10,11... | collective-permute-start | bytes 884744 | tf_op jit(solution)/shard_map/ppermute | solution.py:451
  35.2 1.1 collective-permute-done.2.bias_sib_hbm
  36.3 4.7 %collective-permute-done.across_ref = f32[196,768]{1,0:T(8,128)} collective-permute-done((f32[196,768]{1,0:T(8,128)S(1)}, f32[196,768]{1,0:T(8,128)}, u32[]{:S(2)}, u32[]{:S(2)}) %collective-permute-start) | collective-permute-done | bytes 602144 | tf_op jit(solution)/shard_map/ppermute | solution.py:451
  41.0 1.0 copy-done.1
  42.0 1.3 copy-done.2
  43.3 1.3 copy-done.5
  44.5 5.3 %shard_map.150 = (f32[2,2,196,384]{3,2,1,0:T(8,128)S(1)}, f32[2,768]{1,0:T(2,128)S(1)}, f32[2,768]{1,0:T(2,128)S(1)}) custom-call(f32[196,768]{1,0:T(8,128)S(1)} %get-tuple-element.27.own_ref, f32[196,768]{1,0:T(8,128)} %collective-permute-done.across_ref, f32[768,384]{1,0:T(8,128)S(1)} %copy-done, f32[768,384]{1,0:T(8,128)S(1)} %copy-done.2, ...), custom_call_target="tpu_custom_call" | custom-call | flops 1387266048 | bytes 7127040 | tf_op jit(solution)/shard_map/pallas_call | solution.py:172
  52.4 2.0 %copy-done.7 = f32[768,1152]{1,0:T(8,128)S(1)} copy-done((f32[768,1152]{1,0:T(8,128)S(1)}, f32[768,1152]{1,0:T(8,128)}, u32[]{:S(2)}) %copy-start.7) | copy-done | bytes 3538968
  54.4 3.4 %shard_map.151 = (f32[2,1152]{1,0:T(2,128)S(1)}, f32[64,1152]{1,0:T(8,128)S(1)}, f32[2,128]{1,0:T(2,128)S(1)}, f32[2,1280]{1,0:T(2,128)S(1)}) custom-call(f32[2,768]{1,0:T(2,128)S(1)} %get-tuple-element.29.mine_ref, f32[2,768]{1,0:T(2,128)S(1)} %collective-permute-done.4.other_ref, f32[768,1152]{1,0:T(8,128)S(1)} %copy-done.7, f32[64,1152]{1,0:T(8,128)S(1)} %bitcast.23, ...), custom_call_target="tpu_custom_call" | custom-call | flops 1358954496 | bytes 3538944 | tf_op jit(solution)/shard_map/pallas_call | solution.py:231
  58.6 2.0 %collective-permute-done.6.other_ref = f32[2,1280]{1,0:T(2,128)S(1)} collective-permute-done((f32[2,1280]{1,0:T(2,128)S(1)}, f32[2,1280]{1,0:T(2,128)S(1)}, u32[]{:S(2)}, u32[]{:S(2)}) %collective-permute-start.6) | collective-permute-done | bytes 10272 | tf_op jit(solution)/shard_map/ppermute | solution.py:451
  60.6 2.0 %copy-done.8 = f32[768,1152]{1,0:T(8,128)S(1)} copy-done((f32[768,1152]{1,0:T(8,128)S(1)}, f32[768,1152]{1,0:T(8,128)}, u32[]{:S(2)}) %copy-start.8) | copy-done | bytes 3538968
  62.6 8.3 %shard_map.152 = (f32[1,128]{1,0:T(1,128)}, f32[1,768]{1,0:T(1,128)S(1)}, f32[2,768]{1,0:T(2,128)S(1)}, f32[2,768]{1,0:T(2,128)S(1)}, f32[196,768]{1,0:T(8,128)}) custom-call(f32[2,1280]{1,0:T(2,128)S(1)} %get-tuple-element.30.packed_ref, f32[2,1280]{1,0:T(2,128)S(1)} %collective-permute-done.6.other_ref, f32[2,1152]{1,0:T(2,128)S(1)} %get-tuple-element.31.unit_ref, ...), custom_call_target="tpu_custom_call" | custom-call | flops 693633024 | bytes 3538944 | tf_op jit(solution)/shard_map/pallas_call | solution.py:281
  70.8 3.5 %shard_map.154 = f32[768,384]{1,0:T(8,128)} custom-call(f32[196,768]{1,0:T(8,128)S(1)} %get-tuple-element.27.own_ref, f32[196,768]{1,0:T(8,128)} %collective-permute-done.across_ref, f32[2,2,196,384]{3,2,1,0:T(8,128)S(1)} %get-tuple-element.33.slope_ref, f32[2,768]{1,0:T(2,128)S(1)} %get-tuple-element.35.grad_ref), custom_call_target="tpu_custom_call" | custom-call | flops 693633024 | bytes 1179648 | tf_op jit(solution)/shard_map/pallas_call | solution.py:309
  74.4 3.8 %collective-permute-start.8 = (f32[768,384]{1,0:T(8,128)}, f32[768,384]{1,0:T(8,128)}, u32[]{:S(2)}, u32[]{:S(2)}) collective-permute-start(f32[768,384]{1,0:T(8,128)} %shard_map.154), channel_id=1, source_target_pairs={{0,1},{1,0},{2,3},{3,2},{4,5},{5,4},{6,7},{7,6},{8,9},{9,8},{10,11... | collective-permute-start | bytes 3538952 | tf_op jit(solution)/shard_map/ppermute | solution.py:451
  78.6 1.0 copy.18
  79.7 12.7 %all-to-all-start.1 = ((f32[64,1,1152]{2,1,0:T(1,128)}), f32[64,1,1152]{2,1,0:T(1,128)}, u32[]{:S(2)}, u32[]{:S(2)}) async-start(f32[64,1,1152]{2,1,0:T(1,128)} %copy.18), calls=%async_computation.1 | async-start | bytes 589824 | tf_op jit(solution)/shard_map/all_to_all | solution.py:455
  93.0 1.5 %collective-permute-start.12 = (f32[1,1152]{1,0:T(1,128)S(1)}, f32[1,1152]{1,0:T(1,128)S(1)}, u32[]{:S(2)}, u32[]{:S(2)}) collective-permute-start(f32[1,1152]{1,0:T(1,128)S(1)} %copy-done.14), channel_id=1, source_target_pairs={{0,2},{1,3},{2,0},{3,1},{4,6},{5,7},{6,4},{7,5},{8,10},{9,11},{10,... | collective-permute-start | bytes 13832 | tf_op jit(solution)/shard_map/ppermute | solution.py:451
  94.6 10.6 %all-to-all-done.1 = f32[64,1,1152]{2,1,0:T(1,128)} async-done(((f32[64,1,1152]{2,1,0:T(1,128)}), f32[64,1,1152]{2,1,0:T(1,128)}, u32[]{:S(2)}, u32[]{:S(2)}) %all-to-all-start.1) | async-done | bytes 294944 | tf_op jit(solution)/shard_map/all_to_all | solution.py:455
  105.3 1.0 copy.24
  106.7 2.7 %collective-permute-start.14 = (f32[1,1152]{1,0:T(1,128)S(1)}, f32[1,1152]{1,0:T(1,128)S(1)}, u32[]{:S(2)}, u32[]{:S(2)}) collective-permute-start(f32[1,1152]{1,0:T(1,128)S(1)} %get-tuple-element.45), channel_id=1, source_target_pairs={{0,1},{1,0},{2,3},{3,2},{4,5},{5,4},{6,7},{7,6},{8,9},{9,8},{10,11... | collective-permute-start | bytes 13832 | tf_op jit(solution)/shard_map/ppermute | solution.py:451
  109.4 1.7 %collective-permute-start.16 = (f32[1,1152]{1,0:T(1,128)S(1)}, f32[1,1152]{1,0:T(1,128)S(1)}, u32[]{:S(2)}, u32[]{:S(2)}) collective-permute-start(f32[1,1152]{1,0:T(1,128)S(1)} %get-tuple-element.47), channel_id=1, source_target_pairs={{0,3},{1,2},{2,1},{3,0},{4,7},{5,6},{6,5},{7,4},{8,11},{9,10},{10,... | collective-permute-start | bytes 13832 | tf_op jit(solution)/shard_map/ppermute | solution.py:451
  111.9 1.2 collective-permute-start.10
  114.0 1.3 copy-done.4
  115.2 7.2 %shard_map.153 = f32[1176,128]{1,0:T(8,128)} custom-call(f32[196,768]{1,0:T(8,128)} %collective-permute-done.7.other_ref, f32[2,2,196,384]{3,2,1,0:T(8,128)S(1)} %get-tuple-element.33.slope_ref, f32[2,768]{1,0:T(2,128)S(1)} %get-tuple-element.35.grad_ref, f32[768,384]{1,0:T(8,128)S(1)} %copy-done, f32[768,384]{1,0:T(8,128)S(1)} %copy-done.4, ...), custom_call_target="tpu_custom_call" | custom-call | flops 14751744 | bytes 1806336 | tf_op jit(solution)/shard_map/pallas_call | solution.py:397
  122.4 4.8 %shard_map.155 = (f32[768,384]{1,0:T(8,128)}, f32[384,768]{1,0:T(8,128)}) custom-call(f32[196,768]{1,0:T(8,128)S(1)} %get-tuple-element.27.own_ref, f32[196,768]{1,0:T(8,128)} %collective-permute-done.across_ref, f32[2,2,196,384]{3,2,1,0:T(8,128)S(1)} %get-tuple-element.33.slope_ref, f32[2,768]{1,0:T(2,128)S(1)} %get-tuple-element.35.grad_ref, ...), custom_call_target="tpu_custom_call" | custom-call | flops 693633024 | bytes 3538944 | tf_op jit(solution)/shard_map/pallas_call | solution.py:336
  (58 shorter events, 8.9 us)
Async XLA Ops:
  0.6 41.4 %copy-start = (f32[768,384]{1,0:T(8,128)S(1)}, f32[768,384]{1,0:T(8,128)}, u32[]{:S(2)}) copy-start(f32[768,384]{1,0:T(8,128)} %up_hbm.5) | copy-start | bytes 3538948
  0.6 40.3 %collective-permute-start.3 = (f32[384,768]{1,0:T(8,128)}, f32[384,768]{1,0:T(8,128)}, u32[]{:S(2)}, u32[]{:S(2)}) collective-permute-start(f32[384,768]{1,0:T(8,128)} %down_hbm.3), channel_id=1, source_target_pairs={{0,1},{1,0},{2,3},{3,2},{4,5},{5,4},{6,7},{7,6},{8,9},{9,8},{10,11... | collective-permute-start | bytes 3538952 | tf_op jit(solution)/shard_map/ppermute | solution.py:451
  4.0 37.0 %collective-permute-start.1 = (f32[768,384]{1,0:T(8,128)}, f32[768,384]{1,0:T(8,128)S(1)}, u32[]{:S(2)}, u32[]{:S(2)}) collective-permute-start(f32[768,384]{1,0:T(8,128)} %up_hbm.5), channel_id=1, source_target_pairs={{0,1},{1,0},{2,3},{3,2},{4,5},{5,4},{6,7},{7,6},{8,9},{9,8},{10,11... | collective-permute-start | bytes 3538952 | tf_op jit(solution)/shard_map/ppermute | solution.py:451
  5.6 25.7 %all-to-all-start = ((f32[64,1,1152]{2,1,0:T(1,128)}), f32[64,1,1152]{2,1,0:T(1,128)}, u32[]{:S(2)}, u32[]{:S(2)}) async-start(f32[64,1,1152]{2,1,0:T(1,128)} %broadcast_in_dim.20), calls=%async_computation | async-start | bytes 589824 | tf_op jit(solution)/shard_map/all_to_all | solution.py:455
  21.1 14.0 %copy-start.18 = (f32[384]{0:T(512)S(1)}, f32[384]{0:T(512)}, u32[]{:S(2)}) copy-start(f32[384]{0:T(512)} %bias_hbm.1) | copy-start | bytes 4612
  21.1 20.9 %copy-start.15 = (f32[768]{0:T(1024)S(1)}, f32[768]{0:T(1024)}, u32[]{:S(2)}) copy-start(f32[768]{0:T(1024)} %scale_hbm.3) | copy-start | bytes 9220
  26.0 14.9 %collective-permute-start = (f32[196,768]{1,0:T(8,128)S(1)}, f32[196,768]{1,0:T(8,128)}, u32[]{:S(2)}, u32[]{:S(2)}) collective-permute-start(f32[196,768]{1,0:T(8,128)S(1)} %get-tuple-element.27.own_ref), channel_id=1, source_target_pairs={{0,2},{1,3},{2,0},{3,1},{4,6},{5,7},{6,4},{7,5},{8,10},{9,11},{10,... | collective-permute-start | bytes 1806344 | tf_op jit(solution)/shard_map/ppermute | solution.py:451
  32.3 19.5 %collective-permute-start.5 = (f32[64,1152]{1,0:T(8,128)S(1)}, f32[64,1152]{1,0:T(8,128)}, u32[]{:S(2)}, u32[]{:S(2)}) collective-permute-start(f32[64,1152]{1,0:T(8,128)S(1)} %bitcast.22), channel_id=1, source_target_pairs={{0,1},{1,0},{2,3},{3,2},{4,5},{5,4},{6,7},{7,6},{8,9},{9,8},{10,11... | collective-permute-start | bytes 884744 | tf_op jit(solution)/shard_map/ppermute | solution.py:451
  35.1 1.2 collective-permute-start.2
  42.0 1.3 copy-start.2
  49.8 2.6 %collective-permute-start.4 = (f32[2,768]{1,0:T(2,128)S(1)}, f32[2,768]{1,0:T(2,128)S(1)}, u32[]{:S(2)}, u32[]{:S(2)}) collective-permute-start(f32[2,768]{1,0:T(2,128)S(1)} %get-tuple-element.29.mine_ref), channel_id=1, source_target_pairs={{0,2},{1,3},{2,0},{3,1},{4,6},{5,7},{6,4},{7,5},{8,10},{9,11},{10,... | collective-permute-start | bytes 18440 | tf_op jit(solution)/shard_map/ppermute | solution.py:451
  52.4 2.0 %copy-start.7 = (f32[768,1152]{1,0:T(8,128)S(1)}, f32[768,1152]{1,0:T(8,128)}, u32[]{:S(2)}) copy-start(f32[768,1152]{1,0:T(8,128)} %proj_hbm.3) | copy-start | bytes 10616836
  54.4 6.2 %copy-start.3 = (f32[768,384]{1,0:T(8,128)S(1)}, f32[768,384]{1,0:T(8,128)}, u32[]{:S(2)}) copy-start(f32[768,384]{1,0:T(8,128)} %copy-done.1) | copy-start | bytes 3538948
  54.4 6.2 %copy-start.6 = (f32[384,768]{1,0:T(8,128)S(1)}, f32[384,768]{1,0:T(8,128)}, u32[]{:S(2)}) copy-start(f32[384,768]{1,0:T(8,128)} %down_hbm.3) | copy-start | bytes 3538948
  57.8 2.8 %collective-permute-start.6 = (f32[2,1280]{1,0:T(2,128)S(1)}, f32[2,1280]{1,0:T(2,128)S(1)}, u32[]{:S(2)}, u32[]{:S(2)}) collective-permute-start(f32[2,1280]{1,0:T(2,128)S(1)} %get-tuple-element.30.packed_ref), channel_id=1, source_target_pairs={{0,2},{1,3},{2,0},{3,1},{4,6},{5,7},{6,4},{7,5},{8,10},{9,11},{10,... | collective-permute-start | bytes 30728 | tf_op jit(solution)/shard_map/ppermute | solution.py:451
  60.6 2.0 %copy-start.8 = (f32[768,1152]{1,0:T(8,128)S(1)}, f32[768,1152]{1,0:T(8,128)}, u32[]{:S(2)}) copy-start(f32[768,1152]{1,0:T(8,128)} %proj_hbm.3) | copy-start | bytes 10616836
  74.3 18.0 %copy-start.14 = (f32[1,1152]{1,0:T(1,128)S(1)}, f32[1,1152]{1,0:T(1,128)}, u32[]{:S(2)}) copy-start(f32[1,1152]{1,0:T(1,128)} %text_ref.1) | copy-start | bytes 13828
  74.4 39.6 %copy-start.10 = (f32[7,7,768]{2,1,0:T(8,128)S(1)}, f32[7,7,768]{2,1,0:T(8,128)}, u32[]{:S(2)}) copy-start(f32[7,7,768]{2,1,0:T(8,128)} %w_hbm.3) | copy-start | bytes 451588
  74.4 39.6 %copy-start.17 = (f32[768]{0:T(1024)S(1)}, f32[768]{0:T(1024)}, u32[]{:S(2)}) copy-start(f32[768]{0:T(1024)} %gain_hbm.3) | copy-start | bytes 9220
  74.4 48.1 %collective-permute-start.8 = (f32[768,384]{1,0:T(8,128)}, f32[768,384]{1,0:T(8,128)}, u32[]{:S(2)}, u32[]{:S(2)}) collective-permute-start(f32[768,384]{1,0:T(8,128)} %shard_map.154), channel_id=1, source_target_pairs={{0,1},{1,0},{2,3},{3,2},{4,5},{5,4},{6,7},{7,6},{8,9},{9,8},{10,11... | collective-permute-start | bytes 3538952 | tf_op jit(solution)/shard_map/ppermute | solution.py:451
  78.2 35.8 %collective-permute-start.7 = (f32[196,768]{1,0:T(8,128)}, f32[196,768]{1,0:T(8,128)}, u32[]{:S(2)}, u32[]{:S(2)}) collective-permute-start(f32[196,768]{1,0:T(8,128)} %get-tuple-element.34), channel_id=1, source_target_pairs={{0,2},{1,3},{2,0},{3,1},{4,6},{5,7},{6,4},{7,5},{8,10},{9,11},{10,... | collective-permute-start | bytes 1806344 | tf_op jit(solution)/shard_map/ppermute | solution.py:451
  79.7 25.6 %all-to-all-start.1 = ((f32[64,1,1152]{2,1,0:T(1,128)}), f32[64,1,1152]{2,1,0:T(1,128)}, u32[]{:S(2)}, u32[]{:S(2)}) async-start(f32[64,1,1152]{2,1,0:T(1,128)} %copy.18), calls=%async_computation.1 | async-start | bytes 589824 | tf_op jit(solution)/shard_map/all_to_all | solution.py:455
  92.4 13.9 %collective-permute-start.13 = (f32[1,1152]{1,0:T(1,128)S(1)}, f32[1,1152]{1,0:T(1,128)S(1)}, u32[]{:S(2)}, u32[]{:S(2)}) collective-permute-start(f32[1,1152]{1,0:T(1,128)S(1)} %copy-done.14), channel_id=1, source_target_pairs={{0,3},{1,2},{2,1},{3,0},{4,7},{5,6},{6,5},{7,4},{8,11},{9,10},{10,... | collective-permute-start | bytes 13832 | tf_op jit(solution)/shard_map/ppermute | solution.py:451
  93.0 13.4 %collective-permute-start.12 = (f32[1,1152]{1,0:T(1,128)S(1)}, f32[1,1152]{1,0:T(1,128)S(1)}, u32[]{:S(2)}, u32[]{:S(2)}) collective-permute-start(f32[1,1152]{1,0:T(1,128)S(1)} %copy-done.14), channel_id=1, source_target_pairs={{0,2},{1,3},{2,0},{3,1},{4,6},{5,7},{6,4},{7,5},{8,10},{9,11},{10,... | collective-permute-start | bytes 13832 | tf_op jit(solution)/shard_map/ppermute | solution.py:451
  94.5 11.9 %collective-permute-start.11 = (f32[1,1152]{1,0:T(1,128)S(1)}, f32[1,1152]{1,0:T(1,128)S(1)}, u32[]{:S(2)}, u32[]{:S(2)}) collective-permute-start(f32[1,1152]{1,0:T(1,128)S(1)} %copy-done.14), channel_id=1, source_target_pairs={{0,1},{1,0},{2,3},{3,2},{4,5},{5,4},{6,7},{7,6},{8,9},{9,8},{10,11... | collective-permute-start | bytes 13832 | tf_op jit(solution)/shard_map/ppermute | solution.py:451
  105.3 8.7 %copy-start.12 = (f32[6,14,16,128]{3,2,1,0:T(8,128)S(1)}, f32[6,14,16,128]{3,2,1,0:T(8,128)}, u32[]{:S(2)}) copy-start(f32[6,14,16,128]{3,2,1,0:T(8,128)} %copy-done.11) | copy-start | bytes 2064388
  106.7 4.4 %collective-permute-start.14 = (f32[1,1152]{1,0:T(1,128)S(1)}, f32[1,1152]{1,0:T(1,128)S(1)}, u32[]{:S(2)}, u32[]{:S(2)}) collective-permute-start(f32[1,1152]{1,0:T(1,128)S(1)} %get-tuple-element.45), channel_id=1, source_target_pairs={{0,1},{1,0},{2,3},{3,2},{4,5},{5,4},{6,7},{7,6},{8,9},{9,8},{10,11... | collective-permute-start | bytes 13832 | tf_op jit(solution)/shard_map/ppermute | solution.py:451
  109.4 2.5 %collective-permute-start.15 = (f32[1,1152]{1,0:T(1,128)S(1)}, f32[1,1152]{1,0:T(1,128)S(1)}, u32[]{:S(2)}, u32[]{:S(2)}) collective-permute-start(f32[1,1152]{1,0:T(1,128)S(1)} %get-tuple-element.46), channel_id=1, source_target_pairs={{0,2},{1,3},{2,0},{3,1},{4,6},{5,7},{6,4},{7,5},{8,10},{9,11},{10,... | collective-permute-start | bytes 13832 | tf_op jit(solution)/shard_map/ppermute | solution.py:451
  109.4 3.7 %collective-permute-start.16 = (f32[1,1152]{1,0:T(1,128)S(1)}, f32[1,1152]{1,0:T(1,128)S(1)}, u32[]{:S(2)}, u32[]{:S(2)}) collective-permute-start(f32[1,1152]{1,0:T(1,128)S(1)} %get-tuple-element.47), channel_id=1, source_target_pairs={{0,3},{1,2},{2,1},{3,0},{4,7},{5,6},{6,5},{7,4},{8,11},{9,10},{10,... | collective-permute-start | bytes 13832 | tf_op jit(solution)/shard_map/ppermute | solution.py:451
  111.2 11.2 %collective-permute-start.9 = (f32[2,768]{1,0:T(2,128)S(1)}, f32[2,768]{1,0:T(2,128)S(1)}, u32[]{:S(2)}, u32[]{:S(2)}) collective-permute-start(f32[2,768]{1,0:T(2,128)S(1)} %get-tuple-element.39.hidden_ref), channel_id=1, source_target_pairs={{0,1},{1,0},{2,3},{3,2},{4,5},{5,4},{6,7},{7,6},{8,9},{9,8},{10,11... | collective-permute-start | bytes 18440 | tf_op jit(solution)/shard_map/ppermute | solution.py:451
  111.9 10.5 %collective-permute-start.10 = (f32[2,768]{1,0:T(2,128)S(1)}, f32[2,768]{1,0:T(2,128)S(1)}, u32[]{:S(2)}, u32[]{:S(2)}) collective-permute-start(f32[2,768]{1,0:T(2,128)S(1)} %get-tuple-element.40.branch_ref), channel_id=1, source_target_pairs={{0,1},{1,0},{2,3},{3,2},{4,5},{5,4},{6,7},{7,6},{8,9},{9,8},{10,11... | collective-permute-start | bytes 18440 | tf_op jit(solution)/shard_map/ppermute | solution.py:451
  113.9 1.3 %copy-start.4 = (f32[768,384]{1,0:T(8,128)S(1)}, f32[768,384]{1,0:T(8,128)}, u32[]{:S(2)}) copy-start(f32[768,384]{1,0:T(8,128)} %copy-done.1) | copy-start | bytes 3538948
  (6 other events, 5.8 us)

commit v2 on v1

v2 whole, which is shorter than its diff:
```python
import functools

import jax
import jax.numpy as jnp
from jax import lax
from jax.experimental import pallas as pl
from jax.experimental.pallas import tpu as pltpu
from jax.sharding import PartitionSpec as P

LANES = 128
HIGH = lax.Precision.HIGH
VMEM = pl.BlockSpec(memory_space=pltpu.VMEM)
SMEM = pl.BlockSpec(memory_space=pltpu.SMEM)
ANY = pl.BlockSpec(memory_space=pl.ANY)
F32 = jnp.float32
WIDE = 58


def call(kernel, outs, specs, scratch=(), us=1.0, mib=12):
    return pl.pallas_call(
        kernel,
        out_shape=[jax.ShapeDtypeStruct(shape, F32) for shape in outs],
        in_specs=specs,
        out_specs=[VMEM] * len(outs),
        scratch_shapes=list(scratch),
        compiler_params=pltpu.CompilerParams(vmem_limit_bytes=mib << 20),
        cost_estimate=pl.CostEstimate(
            flops=int(us * 1.15e9), bytes_accessed=int(us * 3.0e6), transcendentals=0
        ),
    )


def fetch(sems, *pairs):
    copies = [
        pltpu.make_async_copy(source, target, sems.at[i])
        for i, (source, target) in enumerate(pairs)
    ]
    for copy in copies:
        copy.start()
    return copies


def dot(left, right, dims=((1,), (0,))):
    return lax.dot_general(
        left, right, (dims, ((), ())), precision=HIGH, preferred_element_type=F32
    )


def row_dots(matrix_ref, vectors):
    count, width = matrix_ref.shape
    rows = [[] for _ in vectors]
    for block in range(count // LANES):
        for i, vector in enumerate(vectors):
            total = jnp.zeros((LANES, LANES), F32)
            for tile in range(width // LANES):
                lanes = slice(tile * LANES, (tile + 1) * LANES)
                total = total + matrix_ref[block * LANES : (block + 1) * LANES, lanes] * vector[:, lanes]
            rows[i].append(jnp.sum(total.T, axis=0, keepdims=True))
    return [jnp.concatenate(row, axis=1) for row in rows]


def gathered_rows(flat_ref, rows_ref):
    tiles = rows_ref.shape[1] // LANES
    count = rows_ref.shape[0]
    for tile in range(tiles):
        rows_ref[:, tile * LANES : (tile + 1) * LANES] = flat_ref[pl.ds(tile, count, stride=tiles), :]


def lanes_of(tile):
    return pl.ds(pl.multiple_of(tile * LANES, LANES), LANES)


def convolve(pad, w_ref, tile, side, flip):
    taps = w_ref.shape[0]
    halves = []
    for half in range(2):
        total = jnp.zeros((side, 8, LANES), F32)
        for q in range(taps):
            column = pad[tile, :, pl.ds(q + 8 * half, 8), :]
            for p in range(taps):
                row = taps - 1 - p if flip else p
                col = taps - 1 - q if flip else q
                total = total + column[p : p + side] * w_ref[row, pl.ds(col, 1), lanes_of(tile)]
        halves.append(total)
    return halves


def front_kernel(
    x_any, w_any, gain_any, normed_ref, rstd_ref, sum_ref, gain_ref, x_ref, w_ref, pad, mixed, sems
):
    tiles, side = mixed.shape[0], mixed.shape[1]
    reach = w_ref.shape[0] // 2
    channels = tiles * LANES
    copies = fetch(sems, (x_any, x_ref), (w_any, w_ref), (gain_any, gain_ref.at[0]))
    pad[...] = jnp.zeros_like(pad)
    for copy in copies:
        copy.wait()
    for tile in range(tiles):
        total = jnp.zeros((side, LANES), F32)
        for h in range(side):
            row = x_ref[pl.ds(h * side * tiles + tile, side, stride=tiles), :]
            pad[tile, reach + h, pl.ds(reach, side), :] = row
            total = total + row
        sum_ref[:, tile * LANES : (tile + 1) * LANES] = jnp.sum(total, axis=0, keepdims=True)

    @pl.loop(0, tiles)
    def _(tile):
        low, high = convolve(pad, w_ref, tile, side, False)
        mixed[tile, :, 0:8, :] = low
        mixed[tile, :, 8:16, :] = high

    total = mixed[0]
    for tile in range(1, tiles):
        total = total + mixed[tile]
    mean = jnp.sum(total, axis=-1, keepdims=True) * (1.0 / channels)
    square = jnp.zeros((side, 16, LANES), F32)
    for tile in range(tiles):
        off = mixed[tile] - mean
        square = square + off * off
    rstd = lax.rsqrt(jnp.sum(square, axis=-1, keepdims=True) * (1.0 / channels) + 1e-06)
    rstd_ref[...] = jnp.broadcast_to(rstd, rstd_ref.shape)
    for tile in range(tiles):
        lanes = slice(tile * LANES, (tile + 1) * LANES)
        out = (mixed[tile] - mean) * rstd * gain_ref[:, lanes]
        for h in range(side):
            normed_ref[h * side : (h + 1) * side, lanes] = out[h, :side]
    rest = normed_ref.shape[0] - side * side
    normed_ref[side * side :, :] = jnp.zeros((rest, channels), F32)


def front(images, dw_kernel, norm_gain):
    side, taps = images.shape[1], dw_kernel.shape[0]
    channels = images.shape[3]
    tiles = channels // LANES
    return call(
        front_kernel,
        [
            (pl.cdiv(side * side, 8) * 8, channels),
            (side, 16, LANES),
            (1, channels),
            (1, channels),
        ],
        [ANY] * 3,
        [
            pltpu.VMEM((side * side * tiles, LANES), F32),
            pltpu.VMEM(dw_kernel.shape, F32),
            pltpu.VMEM((tiles, side + taps - 1, 24, LANES), F32),
            pltpu.VMEM((tiles, side, 16, LANES), F32),
            pltpu.SemaphoreType.DMA((3,)),
        ],
        us=4.0,
        mib=WIDE,
    )(images.reshape(-1, LANES), dw_kernel, norm_gain)


def spread_kernel(row_ref, other_ref, out_ref):
    tiles = row_ref.shape[1] // LANES
    copies = out_ref.shape[0] // (2 * tiles)
    for k, row in enumerate((row_ref, other_ref)):
        for tile in range(tiles):
            out_ref[pl.ds(k * tiles + tile, copies, stride=2 * tiles), :] = jnp.broadcast_to(
                row[0:1, tile * LANES : (tile + 1) * LANES], (copies, LANES)
            )


def spread_pair(row, other, peers):
    flat = (peers * row.shape[1] // LANES, LANES)
    return call(spread_kernel, [flat], [VMEM] * 2, us=0.5)(row, other)[0]


def mlp_kernel(
    own_any, across_any, up_any, up_sib_any, bias_any, bias_sib_any, down_any, down_sib_any, scale_any, proj_any,
    sum_any, both_ref, slope_ref, slope_sib_ref, hidden_ref, part_ref,
    up_ref, up_sib_ref, bias_ref, down_ref, down_sib_ref, scale_ref, proj_ref, sum_ref, sems, *, positions,
):
    offset = own_any.shape[0]
    width = up_ref.shape[1]
    copies = fetch(
        sems,
        (own_any, both_ref.at[pl.ds(0, offset)]),
        (across_any, both_ref.at[pl.ds(offset, offset)]),
        (up_any, up_ref),
        (bias_any, bias_ref.at[0]),
        (bias_sib_any, bias_ref.at[1]),
        (up_sib_any, up_sib_ref),
        (scale_any, scale_ref.at[0]),
        (sum_any, sum_ref),
        (down_any, down_ref),
        (down_sib_any, down_sib_ref),
        (proj_any, proj_ref),
    )
    for copy in copies[:5]:
        copy.wait()
    for s, (weight, out) in enumerate(((up_ref, slope_ref), (up_sib_ref, slope_sib_ref))):
        if s == 1:
            copies[5].wait()
        pre = dot(both_ref[...], weight[...]) + bias_ref[pl.ds(s, 1), :]
        cdf = 0.5 * (1.0 + lax.erf(pre * (0.5**0.5)))
        out[...] = cdf + pre * (jnp.exp(-0.5 * pre * pre) * 0.3989422804014327)
        act = pre * cdf
        for k in range(2):
            hidden_ref[pl.ds(k, 1), s * width : (s + 1) * width] = jnp.sum(
                act[k * offset : k * offset + positions], axis=0, keepdims=True
            )
    hidden = hidden_ref[...]
    for copy in copies[6:10]:
        copy.wait()
    part = dot(hidden[:, :width], down_ref[...]) + dot(hidden[:, width:], down_sib_ref[...])
    part = part * scale_ref[...]
    own = lax.broadcasted_iota(jnp.int32, part.shape, 0) == 0
    part = part + jnp.where(own, sum_ref[...], 0.0)
    copies[10].wait()
    part_ref[...] = dot(part * (1.0 / positions), proj_ref[...])


def mlp(own, across, up, up_sib, bias, bias_sib, down, down_sib, scale, projection, image_sum, positions):
    channels = own.shape[1]
    hidden = up.shape[1]
    rows = 2 * own.shape[0]
    return call(
        functools.partial(mlp_kernel, positions=positions),
        [
            (rows, channels), (rows, hidden), (rows, hidden), (2, 2 * hidden),
            (2, projection.shape[1]),
        ],
        [ANY] * 11,
        [
            pltpu.VMEM(up.shape, F32),
            pltpu.VMEM(up.shape, F32),
            pltpu.VMEM((2, hidden), F32),
            pltpu.VMEM(down.shape, F32),
            pltpu.VMEM(down.shape, F32),
            pltpu.VMEM((1, channels), F32),
            pltpu.VMEM(projection.shape, F32),
            pltpu.VMEM(image_sum.shape, F32),
            pltpu.SemaphoreType.DMA((11,)),
        ],
        us=5.0,
        mib=WIDE,
    )(own, across, up, up_sib, bias, bias_sib, down, down_sib, scale, projection, image_sum)


def normal(rows):
    inverse = lax.rsqrt(jnp.sum(rows * rows, axis=-1, keepdims=True) + 1e-06)
    return rows * inverse, inverse


def pair_kernel(
    mine_ref, other_ref, texts_ref, texts_sib_ref, dp_ref, scale_ref, shift_ref,
    unit_ref, inverse_ref, packed_ref, features, text, text_sib,
):
    embed = unit_ref.shape[1]
    gathered_rows(texts_ref, text)
    gathered_rows(texts_sib_ref, text_sib)
    features[pl.ds(0, 1), :] = mine_ref[pl.ds(0, 1), :] + other_ref[pl.ds(1, 1), :]
    features[pl.ds(1, 1), :] = mine_ref[pl.ds(1, 1), :] + other_ref[pl.ds(0, 1), :]
    unit, inverse = normal(features[...])
    inverse_ref[...] = jnp.broadcast_to(inverse, inverse_ref.shape)
    unit_ref[...] = unit
    step = jnp.zeros(unit.shape, F32)
    losses = jnp.zeros((2, 1), F32)
    for s, block_ref in enumerate((text, text_sib)):
        block, _ = normal(block_ref[...])
        logits = scale_ref[0] * dot(unit, block, ((1,), (1,))) + shift_ref[0]
        if s == 0:
            columns = lax.broadcasted_iota(jnp.int32, logits.shape, 1)
            place = lax.broadcasted_iota(jnp.int32, logits.shape, 0)
            match = jnp.where((place == 0) & (columns == dp_ref[0]), 1.0, 0.0)
        else:
            match = jnp.zeros(logits.shape, F32)
        flipped = (1.0 - 2.0 * match) * logits
        tail = jnp.log1p(jnp.exp(-jnp.abs(flipped)))
        losses = losses + jnp.sum(jnp.maximum(flipped, 0.0) + tail, axis=1, keepdims=True)
        slopes = 1.0 / (1.0 + jnp.exp(-logits)) - match
        step = step + dot(slopes, block)
    packed_ref[:, :embed] = step * scale_ref[0]
    packed_ref[:, embed:] = jnp.broadcast_to(losses, (2, LANES))


def pairs(mine, other, texts, texts_sib, dp, scale, shift):
    embed = mine.shape[1]
    count = texts.size // embed
    return call(
        pair_kernel,
        [(2, embed), (2, LANES), (2, embed + LANES)],
        [VMEM] * 4 + [SMEM] * 3,
        [
            pltpu.VMEM(mine.shape, F32),
            pltpu.VMEM((count, embed), F32),
            pltpu.VMEM((count, embed), F32),
        ],
        us=6.0,
    )(mine, other, texts, texts_sib, dp, scale, shift)


def scaled(slope_ref, rows):
    second = lax.broadcasted_iota(jnp.int32, slope_ref.shape, 0) >= slope_ref.shape[0] // 2
    return slope_ref[...] * jnp.where(second, rows[1:2], rows[0:1])


def slope_kernel(
    packed_ref, other_ref, unit_ref, inverse_ref, proj_ref, scale_ref, down_ref, down_sib_ref, up_ref, up_sib_ref,
    slope_ref, slope_sib_ref, loss_ref, const_ref, grad_ref, own_ref, across_ref, sums,
):
    embed = unit_ref.shape[1]
    width = down_ref.shape[0]
    positions = own_ref.shape[0]
    offset = slope_ref.shape[0] // 2
    sums[pl.ds(0, 1), :] = packed_ref[pl.ds(0, 1), :] + other_ref[pl.ds(1, 1), :]
    sums[pl.ds(1, 1), :] = packed_ref[pl.ds(1, 1), :] + other_ref[pl.ds(0, 1), :]
    loss_ref[...] = sums[0:1, embed:]
    step, unit = sums[:, :embed], unit_ref[...]
    grad = step - unit * jnp.sum(unit * step, axis=-1, keepdims=True)
    grad = grad * (inverse_ref[:, 0:1] * (1.0 / positions))
    rows = row_dots(proj_ref, (grad[0:1], grad[1:2]))
    const_ref[...] = rows[0]
    for k in range(2):
        grad_ref[pl.ds(2 + k, 1), :] = rows[k] * scale_ref[...]
    branch = grad_ref[2:4, :]
    for s, weight in enumerate((down_ref, down_sib_ref)):
        for k, row in enumerate(row_dots(weight, (branch[0:1], branch[1:2]))):
            grad_ref[pl.ds(k, 1), s * width : (s + 1) * width] = row
    rows = grad_ref[...]
    total = dot(scaled(slope_ref, rows[:, :width]), up_ref[...], ((1,), (1,)))
    total = total + dot(scaled(slope_sib_ref, rows[:, width:]), up_sib_ref[...], ((1,), (1,)))
    own_ref[...] = total[:positions]
    across_ref[...] = total[offset : offset + positions]


def slopes_of(packed, other, unit, inverse, projection, scale, down, down_sib, up, up_sib, slope, slope_sib, positions):
    channels = up.shape[0]
    return call(
        slope_kernel,
        [(1, LANES), (1, channels), (4, channels), (positions, channels), (positions, channels)],
        [VMEM] * 12,
        [pltpu.VMEM(packed.shape, F32)],
        us=4.0,
        mib=16,
    )(packed, other, unit, inverse, projection, scale[None], down, down_sib, up, up_sib, slope, slope_sib)


def last_kernel(
    both_ref, both_sib_ref, slope_ref, slope_sib_ref, grad_ref, grad_sib_ref, hidden_ref, hidden_sib_ref,
    up_out, down_out,
):
    width = up_out.shape[1]
    rows, rows_sib = grad_ref[...], grad_sib_ref[...]
    up_out[...] = dot(both_ref[...], scaled(slope_ref, rows[:, :width]), ((0,), (0,)))
    up_out[...] += dot(both_sib_ref[...], scaled(slope_sib_ref, rows_sib[:, width:]), ((0,), (0,)))
    down_out[...] = dot(hidden_ref[:, :width], rows[2:4], ((0,), (0,))) + dot(
        hidden_sib_ref[:, width:], rows_sib[2:4], ((0,), (0,))
    )


def last_grads(both, both_sib, slope, slope_sib, grad, grad_sib, hidden, hidden_sib):
    channels, width = both.shape[1], slope.shape[1]
    return call(
        last_kernel, [(channels, width), (width, channels)], [VMEM] * 8, us=0.2, mib=16
    )(both, both_sib, slope, slope_sib, grad, grad_sib, hidden, hidden_sib)


def back_kernel(
    mine_ref, other_ref, both_ref, rstd_ref, w_ref, gain_ref, const_ref, out_ref, pad, slope, unit
):
    tiles, side = slope.shape[0], slope.shape[1]
    reach = w_ref.shape[0] // 2
    channels = tiles * LANES
    pad[...] = jnp.zeros_like(pad)
    unit[...] = jnp.zeros_like(unit)
    slope[...] = jnp.zeros_like(slope)
    first = jnp.zeros((side, 16, LANES), F32)
    second = jnp.zeros((side, 16, LANES), F32)
    for tile in range(tiles):
        lanes = slice(tile * LANES, (tile + 1) * LANES)
        invert = 1.0 / gain_ref[:, lanes]
        for h in range(side):
            rows = slice(h * side, (h + 1) * side)
            unit[tile, h, 0:side, :] = both_ref[rows, lanes] * invert
            slope[tile, h, 0:side, :] = (mine_ref[rows, lanes] + other_ref[rows, lanes]) * gain_ref[:, lanes]
        first = first + slope[tile]
        second = second + slope[tile] * unit[tile]
    first = jnp.sum(first, axis=-1, keepdims=True) * (1.0 / channels)
    second = jnp.sum(second, axis=-1, keepdims=True) * (1.0 / channels)
    rstd = rstd_ref[...]
    for tile in range(tiles):
        grad = rstd * (slope[tile] - first - unit[tile] * second)
        for h in range(side):
            pad[tile, reach + h, pl.ds(reach, side), :] = grad[h, :side]

    @pl.loop(0, tiles)
    def _(tile):
        low, high = convolve(pad, w_ref, tile, side, True)
        slope[tile, :, 0:8, :] = low
        slope[tile, :, 8:16, :] = high

    for tile in range(tiles):
        const = const_ref[:, tile * LANES : (tile + 1) * LANES]
        for h in range(side):
            out_ref[pl.ds(h * side * tiles + tile, side, stride=tiles), :] = (
                slope[tile, h, 0:side, :] + const
            )


def back(mine, other, both, rstd, dw_kernel, norm_gain, const, side):
    taps, channels = dw_kernel.shape[0], dw_kernel.shape[2]
    tiles = channels // LANES
    return call(
        back_kernel,
        [(side * side * tiles, LANES)],
        [VMEM] * 7,
        [
            pltpu.VMEM((tiles, side + taps - 1, 24, LANES), F32),
            pltpu.VMEM((tiles, side, 16, LANES), F32),
            pltpu.VMEM((tiles, side, 16, LANES), F32),
        ],
        us=4.0,
    )(mine, other, both, rstd, dw_kernel, norm_gain, const)[0]


def column_kernel(
    flat_ref, t0_ref, t1_ref, t2_ref, t3_ref, dp_ref, scale_ref, shift_ref, o0, o1, o2, o3, images_ref
):
    gathered_rows(flat_ref, images_ref)
    images = images_ref[...]
    for k, (text, out) in enumerate(((t0_ref, o0), (t1_ref, o1), (t2_ref, o2), (t3_ref, o3))):
        unit, _ = normal(text[...])
        logits = scale_ref[0] * jnp.sum(images * unit, axis=-1, keepdims=True) + shift_ref[0]
        slopes = 1.0 / (1.0 + jnp.exp(-logits))
        if k == 0:
            rows = lax.broadcasted_iota(jnp.int32, logits.shape, 0)
            slopes = slopes - jnp.where(rows == dp_ref[0], 1.0, 0.0)
        out[...] = jnp.sum(images * (scale_ref[0] * slopes), axis=0, keepdims=True)


def columns_of(images, texts, dp, scale, shift):
    embed = texts[0].shape[1]
    return call(
        column_kernel,
        [texts[0].shape] * 4,
        [VMEM] * 5 + [SMEM] * 3,
        [pltpu.VMEM((images.size // embed, embed), F32)],
        us=0.5,
    )(images, *texts, dp, scale, shift)


def text_kernel(text_ref, a_ref, b_ref, c_ref, d_ref, out_ref):
    unit, inverse = normal(text_ref[...])
    step = a_ref[...] + b_ref[...] + (c_ref[...] + d_ref[...])
    out_ref[...] = inverse * (step - unit * jnp.sum(unit * step, axis=-1, keepdims=True))


def text_grads(text, parts):
    return call(text_kernel, [text.shape], [VMEM] * 5, us=0.5)(text, *parts)[0]


def swapped(value, by):
    peers = lax.axis_size("fsdp")
    return lax.ppermute(value, "fsdp", [(i, i ^ by) for i in range(peers)])


def mirrored(value):
    peers = lax.axis_size("dp")
    return lax.ppermute(value, "dp", [(i, i ^ 1) for i in range(peers)])


def spread_out(flat):
    peers = lax.axis_size("dp")
    groups = [list(range(start, peers, 2)) for start in range(2)]
    rows = flat.reshape(peers // 2, 1, -1)
    return lax.all_to_all(
        rows, "dp", 0, 0, axis_index_groups=groups, tiled=True
    ).reshape(flat.shape)


def body(
    images,
    dw_kernel,
    norm_gain,
    up_weight,
    up_bias,
    down_weight,
    layer_scale,
    projection,
    text_embed,
    logit_scale,
    logit_bias,
):
    positions = images.shape[1] * images.shape[2]
    peers = lax.axis_size("dp")
    place = (lax.axis_index("dp") // 2 * 2).astype(jnp.int32)[None]
    scale, shift = logit_scale[None], logit_bias[None]
    text_other = mirrored(text_embed)
    up_sib, down_sib, bias_sib = swapped(up_weight, 1), swapped(down_weight, 1), swapped(up_bias, 1)

    normed, rstd, image_sum, gain = front(images, dw_kernel, norm_gain)
    text_other, normed = lax.optimization_barrier((text_other, normed))
    across = swapped(normed, 2)
    texts = spread_out(spread_pair(text_embed, text_other, peers))
    group_texts = tuple(swapped(text_embed, k) for k in (1, 2, 3))
    across, group_texts = lax.optimization_barrier((across, group_texts))
    both, slope, slope_sib, hidden, part = mlp(
        normed, across, up_weight, up_sib, up_bias, bias_sib, down_weight, down_sib, layer_scale,
        projection, image_sum, images.shape[1] * images.shape[2],
    )
    part_other = swapped(part, 2)
    texts, hidden = lax.optimization_barrier((texts, hidden))
    texts_sib = swapped(texts, 1)
    image_unit, inverse, packed = pairs(
        part, part_other, texts, texts_sib, place, scale, shift
    )
    packed_other = swapped(packed, 2)
    unit_other = mirrored(image_unit)
    packed_other, unit_other = lax.optimization_barrier((packed_other, unit_other))
    losses, const, grad, own_grad, across_grad = slopes_of(
        packed, packed_other, image_unit, inverse, projection, layer_scale,
        down_weight, down_sib, up_weight, up_sib, slope, slope_sib, images.shape[1] * images.shape[2],
    )
    grad, both, slope_sib, hidden = lax.optimization_barrier((grad, both, slope_sib, hidden))
    both_sib, slope_back, hidden_sib = swapped(both, 1), swapped(slope_sib, 1), swapped(hidden, 1)
    across_grad, image_unit, unit_other = lax.optimization_barrier((across_grad, image_unit, unit_other))
    other_grad = swapped(across_grad, 2)
    image_units = spread_out(spread_pair(image_unit, unit_other, peers))
    up_grad, down_grad = last_grads(
        both, both_sib, slope, slope_back, grad, swapped(grad, 1), hidden, hidden_sib
    )
    image_units, up_grad = lax.optimization_barrier((image_units, up_grad))
    steps = columns_of(image_units, (text_embed,) + group_texts, place, scale, shift)
    input_grad = back(own_grad, other_grad, both, rstd, dw_kernel, gain, const, images.shape[1])
    first_step, input_grad = lax.optimization_barrier((steps[0], input_grad))
    text_grad = text_grads(
        text_embed, (first_step,) + tuple(swapped(steps[k], k) for k in (1, 2, 3))
    )
    return (
        input_grad.reshape(images.shape),
        up_grad[None],
        down_grad[None],
        text_grad,
        losses[0, :1],
    )


def solution(mesh):
    placed = (
        P(("dp", "fsdp"), None, None, None),
        P(),
        P(),
        P(None, "fsdp"),
        P("fsdp"),
        P("fsdp", None),
        P(),
        P(),
        P(("dp", "fsdp"), None),
        P(),
        P(),
    )
    return jax.shard_map(
        body,
        mesh=mesh,
        in_specs=placed,
        out_specs=(
            P(("dp", "fsdp"), None, None, None),
            P("dp", None, "fsdp"),
            P("dp", "fsdp", None),
            P(("dp", "fsdp"), None),
            P(("dp", "fsdp")),
        ),
        check_vma=False,
    )
```

time: 128 us -> 87.9 us (0.69)
  waiting for transfers between devices: 24.5 us -> 7.88 us
  local copies, waits for them, and re-layouts: 16.3 us -> 3.04 us
  Pallas kernels: 37.6 us -> 30.4 us
  starting transfers between devices: 45.9 us -> 44 us
    all_to_all x2, waiting for transfers between devices: 15.6 us -> 2.13 us  [spread_out(): lax.all_to_all(rows, 'dp', 0, 0, axis_index_groups=groups, tiled=True)]
    unnamed x40 -> x46, local copies, waits for them, and re-layouts: 14.4 us -> 3.04 us
    pallas_call x9 -> x10, Pallas kernels: 37.6 us -> 30.4 us  [the longest x1 6.75 us: mlp(): call(functools.partial(mlp_kernel, positions=positions), [(rows, channels...]
    ppermute x17 -> x18, waiting for transfers between devices: 8.96 us -> 2.56 us  [swapped(): return lax.ppermute(value, 'fsdp', [(i, i ^ by) for i in range(peers)])]
    all_to_all x2, starting transfers between devices: 25.5 us -> 20.8 us  [spread_out(): lax.all_to_all(rows, 'dp', 0, 0, axis_index_groups=groups, tiled=True)]
    ppermute x0 -> x2, waiting for transfers between devices: none -> 3.19 us  [mirrored(): return lax.ppermute(value, 'dp', [(i, i ^ 1) for i in range(peers)])]
    ppermute x0 -> x2, starting transfers between devices: none -> 1.83 us  [mirrored(): return lax.ppermute(value, 'dp', [(i, i ^ 1) for i in range(peers)])]
    ppermute x17 -> x18, starting transfers between devices: 20.4 us -> 21.4 us  [swapped(): return lax.ppermute(value, 'fsdp', [(i, i ^ by) for i in range(peers)])]
  transfers between devices with their start and end apart: 19 -> 22, of which waited for: 7 -> 6; matrix products, arithmetic and copies ran while one was open for 4% -> 0% of each run, Pallas kernels for 14% -> 28%
where the time goes in v2:
time: 87.9 us; the launch traced here: 87.5 us
  starting transfers between devices  44 us (50%)
  Pallas kernels  30.4 us (35%)
  waiting for transfers between devices  7.88 us (9%)
  local copies, waits for them, and re-layouts  3.04 us (3%)
  between operations  2.18 us (2%)
    ppermute x18, starting transfers between devices, swapped(): return lax.ppermute(value, 'fsdp', [(i, i ^ by) for i in range(peers)])  21.4 us
    all_to_all x2, starting transfers between devices, spread_out(): lax.all_to_all(rows, 'dp', 0, 0, axis_index_groups=groups, tiled=True)  20.8 us
    pallas_call x1, Pallas kernels, mlp(): call(functools.partial(mlp_kernel, positions=positions), [(rows, channels...  6.75 us
    pallas_call x1, Pallas kernels, last_grads(): call(last_kernel, [(channels, width), (width, channels)], [VMEM] * 8, us=...  5.67 us
    pallas_call x1, Pallas kernels, front(): call(front_kernel, [(pl.cdiv(side * side, 8) * 8, channels), (side, 16, L...  5.38 us
    pallas_call x1, Pallas kernels, back(): call(back_kernel, [(side * side * tiles, LANES)], [VMEM] * 7, [pltpu.VMEM...  5.23 us
    pallas_call x1, Pallas kernels, slopes_of(): call(slope_kernel, [(1, LANES), (1, channels), (4, channels), (positions,...  4.69 us
    ppermute x2, waiting for transfers between devices, mirrored(): return lax.ppermute(value, 'dp', [(i, i ^ 1) for i in range(peers)])  3.19 us
  transfers between devices with their start and end apart: 22, of which 6 were waited for; matrix products, arithmetic and copies ran while one was open for 0% of the time, Pallas kernels for 28%

profile of v2, /device:TPU:1, one launch (start us, length us, event | category | flops | bytes accessed | tf_op | source)
XLA Modules:
  0.0 87.5 jit_solution(2711051988675171159)
XLA Ops:
  0.6 3.3 %collective-permute-start.5 = (f32[768,384]{1,0:T(8,128)}, f32[768,384]{1,0:T(8,128)S(1)}, u32[]{:S(2)}, u32[]{:S(2)}) collective-permute-start(f32[768,384]{1,0:T(8,128)} %up_ref.1), channel_id=1, source_target_pairs={{0,1},{1,0},{2,3},{3,2},{4,5},{5,4},{6,7},{7,6},{8,9},{9,8},{10,11... | collective-permute-start | bytes 3538952 | tf_op jit(solution)/shard_map/ppermute | solution.py:458
  4.1 1.0 %collective-permute-start = (f32[1,1152]{1,0:T(1,128)}, f32[1,1152]{1,0:T(1,128)S(1)}, u32[]{:S(2)}, u32[]{:S(2)}) collective-permute-start(f32[1,1152]{1,0:T(1,128)} %text_ref.1), channel_id=1, source_target_pairs={{0,4},{4,0},{8,12},{12,8},{16,20},{20,16},{24,28},{28,24},{32,36},... | collective-permute-start | bytes 13832 | tf_op jit(solution)/shard_map/ppermute | solution.py:463
  5.1 5.4 %shard_map.146 = (f32[200,768]{1,0:T(8,128)}, f32[14,16,128]{2,1,0:T(8,128)}, f32[1,768]{1,0:T(1,128)}, f32[1,768]{1,0:T(1,128)}) custom-call(f32[1176,128]{1,0:T(8,128)} %bitcast.23, f32[7,7,768]{2,1,0:T(8,128)} %w_ref.1, f32[768]{0:T(1024)} %gain_any.1), custom_call_target="tpu_custom_call" | custom-call | flops 4600000000 | bytes 12000000 | tf_op jit(solution)/shard_map/pallas_call | solution.py:135
  10.9 0.7 shard_map.148
  11.6 11.2 %all-to-all-start = ((f32[32,1,2304]{2,1,0:T(1,128)}), f32[32,1,2304]{2,1,0:T(1,128)S(1)}, u32[]{:S(2)}, u32[]{:S(2)}) async-start(f32[32,1,2304]{2,1,0:T(1,128)} %bitcast.1), calls=%async_computation | async-start | bytes 589824 | tf_op jit(solution)/shard_map/all_to_all | solution.py:470
  22.8 1.3 %collective-permute-start.2 = (f32[1,1152]{1,0:T(1,128)S(1)}, f32[1,1152]{1,0:T(1,128)S(1)}, u32[]{:S(2)}, u32[]{:S(2)}) collective-permute-start(f32[1,1152]{1,0:T(1,128)S(1)} %copy-done.14), channel_id=1, source_target_pairs={{0,1},{1,0},{2,3},{3,2},{4,5},{5,4},{6,7},{7,6},{8,9},{9,8},{10,11... | collective-permute-start | bytes 13832 | tf_op jit(solution)/shard_map/ppermute | solution.py:458
  24.2 1.2 %collective-permute-start.3 = (f32[1,1152]{1,0:T(1,128)S(1)}, f32[1,1152]{1,0:T(1,128)S(1)}, u32[]{:S(2)}, u32[]{:S(2)}) collective-permute-start(f32[1,1152]{1,0:T(1,128)S(1)} %copy-done.14), channel_id=1, source_target_pairs={{0,2},{1,3},{2,0},{3,1},{4,6},{5,7},{6,4},{7,5},{8,10},{9,11},{10,... | collective-permute-start | bytes 13832 | tf_op jit(solution)/shard_map/ppermute | solution.py:458
  25.3 1.0 %collective-permute-start.4 = (f32[1,1152]{1,0:T(1,128)S(1)}, f32[1,1152]{1,0:T(1,128)S(1)}, u32[]{:S(2)}, u32[]{:S(2)}) collective-permute-start(f32[1,1152]{1,0:T(1,128)S(1)} %copy-done.14), channel_id=1, source_target_pairs={{0,3},{1,2},{2,1},{3,0},{4,7},{5,6},{6,5},{7,4},{8,11},{9,10},{10,... | collective-permute-start | bytes 13832 | tf_op jit(solution)/shard_map/ppermute | solution.py:458
  26.7 1.2 %collective-permute-start.6 = (f32[384]{0:T(512)S(1)}, f32[384]{0:T(512)S(1)}, u32[]{:S(2)}, u32[]{:S(2)}) collective-permute-start(f32[384]{0:T(512)S(1)} %copy-done.21), channel_id=1, source_target_pairs={{0,1},{1,0},{2,3},{3,2},{4,5},{5,4},{6,7},{7,6},{8,9},{9,8},{10,11... | collective-permute-start | bytes 4616 | tf_op jit(solution)/shard_map/ppermute | solution.py:458
  27.9 0.8 collective-permute-done.4.t3_ref
  28.7 0.8 copy-done.20
  30.3 6.7 %shard_map.147 = (f32[400,768]{1,0:T(8,128)}, f32[400,384]{1,0:T(8,128)}, f32[400,384]{1,0:T(8,128)}, f32[2,768]{1,0:T(2,128)}, f32[2,1152]{1,0:T(2,128)}) custom-call(f32[200,768]{1,0:T(8,128)} %get-tuple-element.50.own_any, f32[200,768]{1,0:T(8,128)} %copy-done.20, f32[768,384]{1,0:T(8,128)} %up_ref.1, f32[768,384]{1,0:T(8,128)} %copy-done.7, ...), custom_call_target="tpu_custom_call" | custom-call | flops 5750000128 | bytes 15000000 | tf_op jit(solution)/shard_map/pallas_call | solution.py:220
  37.3 1.2 %collective-permute-start.8 = (f32[2,1152]{1,0:T(2,128)}, f32[2,1152]{1,0:T(2,128)S(1)}, u32[]{:S(2)}, u32[]{:S(2)}) collective-permute-start(f32[2,1152]{1,0:T(2,128)} %get-tuple-element.53.mine_ref), channel_id=1, source_target_pairs={{0,2},{1,3},{2,0},{3,1},{4,6},{5,7},{6,4},{7,5},{8,10},{9,11},{10,... | collective-permute-start | bytes 27656 | tf_op jit(solution)/shard_map/ppermute | solution.py:458
  40.0 0.7 copy-done.13
  40.8 0.8 shard_map.149
  41.5 1.4 %collective-permute-start.10 = (f32[2,1280]{1,0:T(2,128)S(1)}, f32[2,1280]{1,0:T(2,128)S(1)}, u32[]{:S(2)}, u32[]{:S(2)}) collective-permute-start(f32[2,1280]{1,0:T(2,128)S(1)} %get-tuple-element.57.packed_ref), channel_id=1, source_target_pairs={{0,2},{1,3},{2,0},{3,1},{4,6},{5,7},{6,4},{7,5},{8,10},{9,11},{10,... | collective-permute-start | bytes 30728 | tf_op jit(solution)/shard_map/ppermute | solution.py:458
  42.9 0.8 collective-permute-start.11
  43.8 3.2 %collective-permute-done.11.other_ref = f32[2,1152]{1,0:T(2,128)S(1)} collective-permute-done((f32[2,1152]{1,0:T(2,128)S(1)}, f32[2,1152]{1,0:T(2,128)S(1)}, u32[]{:S(2)}, u32[]{:S(2)}) %collective-permute-start.11) | collective-permute-done | bytes 9248 | tf_op jit(solution)/shard_map/ppermute | solution.py:463
  47.0 4.7 %shard_map.150 = (f32[1,128]{1,0:T(1,128)}, f32[1,768]{1,0:T(1,128)S(1)}, f32[4,768]{1,0:T(4,128)S(1)}, f32[196,768]{1,0:T(8,128)S(1)}, f32[196,768]{1,0:T(8,128)S(1)}) custom-call(f32[2,1280]{1,0:T(2,128)S(1)} %get-tuple-element.57.packed_ref, f32[2,1280]{1,0:T(2,128)S(1)} %collective-permute-done.10.other_ref, ...), custom_call_target="tpu_custom_call" | custom-call | flops 4600000000 | bytes 12000000 | tf_op jit(solution)/shard_map/pallas_call | solution.py:332
  51.7 2.8 %collective-permute-start.12 = (f32[400,768]{1,0:T(8,128)S(1)}, f32[400,768]{1,0:T(8,128)S(1)}, u32[]{:S(2)}, u32[]{:S(2)}) collective-permute-start(f32[400,768]{1,0:T(8,128)S(1)} %copy-done), channel_id=1, source_target_pairs={{0,1},{1,0},{2,3},{3,2},{4,5},{5,4},{6,7},{7,6},{8,9},{9,8},{10,11... | collective-permute-start | bytes 3686408 | tf_op jit(solution)/shard_map/ppermute | solution.py:458
  54.6 0.7 copy-done.2
  55.3 9.6 %all-to-all-start.1 = ((f32[32,1,2304]{2,1,0:T(1,128)}), f32[32,1,2304]{2,1,0:T(1,128)S(1)}, u32[]{:S(2)}, u32[]{:S(2)}) async-start(f32[32,1,2304]{2,1,0:T(1,128)} %bitcast.20), calls=%async_computation.1 | async-start | bytes 589824 | tf_op jit(solution)/shard_map/all_to_all | solution.py:470
  65.0 1.3 %collective-permute-start.16 = (f32[196,768]{1,0:T(8,128)}, f32[196,768]{1,0:T(8,128)}, u32[]{:S(2)}, u32[]{:S(2)}) collective-permute-start(f32[196,768]{1,0:T(8,128)} %copy-done.11), channel_id=1, source_target_pairs={{0,2},{1,3},{2,0},{3,1},{4,6},{5,7},{6,4},{7,5},{8,10},{9,11},{10,... | collective-permute-start | bytes 1806344 | tf_op jit(solution)/shard_map/ppermute | solution.py:458
  66.3 1.4 %collective-permute-start.14 = (f32[4,768]{1,0:T(4,128)S(1)}, f32[4,768]{1,0:T(4,128)S(1)}, u32[]{:S(2)}, u32[]{:S(2)}) collective-permute-start(f32[4,768]{1,0:T(4,128)S(1)} %get-tuple-element.72.grad_ref), channel_id=1, source_target_pairs={{0,1},{1,0},{2,3},{3,2},{4,5},{5,4},{6,7},{7,6},{8,9},{9,8},{10,11... | collective-permute-start | bytes 36872 | tf_op jit(solution)/shard_map/ppermute | solution.py:458
  67.7 1.2 %collective-permute-done.15.hidden_sib_ref = f32[2,768]{1,0:T(2,128)S(1)} collective-permute-done((f32[2,768]{1,0:T(2,128)S(1)}, f32[2,768]{1,0:T(2,128)S(1)}, u32[]{:S(2)}, u32[]{:S(2)}) %collective-permute-start.15) | collective-permute-done | bytes 6176 | tf_op jit(solution)/shard_map/ppermute | solution.py:458
  68.9 5.7 %shard_map.152 = (f32[768,384]{1,0:T(8,128)}, f32[384,768]{1,0:T(8,128)}) custom-call(f32[400,768]{1,0:T(8,128)S(1)} %copy-done, f32[400,768]{1,0:T(8,128)S(1)} %collective-permute-done.12.both_sib_ref, f32[400,384]{1,0:T(8,128)S(1)} %copy-done.1, f32[400,384]{1,0:T(8,128)} %collective-permute-done.13.slope_sib_ref, ...), custom_call_target="tpu_custom_call" | custom-call | flops 230000000 | bytes 600000 | tf_op jit(solution)/shard_map/pallas_call | solution.py:357
  74.5 2.1 %all-to-all-done.1 = f32[32,1,2304]{2,1,0:T(1,128)S(1)} async-done(((f32[32,1,2304]{2,1,0:T(1,128)}), f32[32,1,2304]{2,1,0:T(1,128)S(1)}, u32[]{:S(2)}, u32[]{:S(2)}) %all-to-all-start.1) | async-done | bytes 294944 | tf_op jit(solution)/shard_map/all_to_all | solution.py:470
  77.0 2.7 %collective-permute-start.17 = (f32[1,1152]{1,0:T(1,128)S(1)}, f32[1,1152]{1,0:T(1,128)S(1)}, u32[]{:S(2)}, u32[]{:S(2)}) collective-permute-start(f32[1,1152]{1,0:T(1,128)S(1)} %get-tuple-element.89), channel_id=1, source_target_pairs={{0,1},{1,0},{2,3},{3,2},{4,5},{5,4},{6,7},{7,6},{8,9},{9,8},{10,11... | collective-permute-start | bytes 13832 | tf_op jit(solution)/shard_map/ppermute | solution.py:458
  79.7 1.2 %collective-permute-start.18 = (f32[1,1152]{1,0:T(1,128)S(1)}, f32[1,1152]{1,0:T(1,128)S(1)}, u32[]{:S(2)}, u32[]{:S(2)}) collective-permute-start(f32[1,1152]{1,0:T(1,128)S(1)} %get-tuple-element.90), channel_id=1, source_target_pairs={{0,2},{1,3},{2,0},{3,1},{4,6},{5,7},{6,4},{7,5},{8,10},{9,11},{10,... | collective-permute-start | bytes 13832 | tf_op jit(solution)/shard_map/ppermute | solution.py:458
  80.9 0.5 collective-permute-start.19
  81.5 5.2 %shard_map.154 = f32[1176,128]{1,0:T(8,128)} custom-call(f32[196,768]{1,0:T(8,128)S(1)} %copy-done.16, f32[196,768]{1,0:T(8,128)} %collective-permute-done.16.other_ref, f32[400,768]{1,0:T(8,128)S(1)} %copy-done, f32[14,16,128]{2,1,0:T(8,128)S(1)} %copy-done.17, f32[7,7,768]{2,1,0:T(8,128)S(1)} %copy-done.12, f32[1,768]{1,0:T(1,128)S(1)} %copy-done.18, ...), custom_call_target="tpu_custom_call" | custom-call | flops 4600000000 | bytes 12000000 | tf_op jit(solution)/shard_map/pallas_call | solution.py:407
  86.7 0.8 shard_map.155
  (69 shorter events, 2.7 us)
Async XLA Ops:
  0.6 28.1 %collective-permute-start.5 = (f32[768,384]{1,0:T(8,128)}, f32[768,384]{1,0:T(8,128)S(1)}, u32[]{:S(2)}, u32[]{:S(2)}) collective-permute-start(f32[768,384]{1,0:T(8,128)} %up_ref.1), channel_id=1, source_target_pairs={{0,1},{1,0},{2,3},{3,2},{4,5},{5,4},{6,7},{7,6},{8,9},{9,8},{10,11... | collective-permute-start | bytes 3538952 | tf_op jit(solution)/shard_map/ppermute | solution.py:458
  4.0 24.8 %collective-permute-start.7 = (f32[384,768]{1,0:T(8,128)}, f32[384,768]{1,0:T(8,128)S(1)}, u32[]{:S(2)}, u32[]{:S(2)}) collective-permute-start(f32[384,768]{1,0:T(8,128)} %down_ref.1), channel_id=1, source_target_pairs={{0,1},{1,0},{2,3},{3,2},{4,5},{5,4},{6,7},{7,6},{8,9},{9,8},{10,11... | collective-permute-start | bytes 3538952 | tf_op jit(solution)/shard_map/ppermute | solution.py:458
  4.1 6.4 %collective-permute-start = (f32[1,1152]{1,0:T(1,128)}, f32[1,1152]{1,0:T(1,128)S(1)}, u32[]{:S(2)}, u32[]{:S(2)}) collective-permute-start(f32[1,1152]{1,0:T(1,128)} %text_ref.1), channel_id=1, source_target_pairs={{0,4},{4,0},{8,12},{12,8},{16,20},{20,16},{24,28},{28,24},{32,36},... | collective-permute-start | bytes 13832 | tf_op jit(solution)/shard_map/ppermute | solution.py:463
  10.5 16.2 %copy-start.21 = (f32[384]{0:T(512)S(1)}, f32[384]{0:T(512)}, u32[]{:S(2)}) copy-start(f32[384]{0:T(512)} %bias_any.1) | copy-start | bytes 4612
  10.5 18.2 %collective-permute-start.1 = (f32[200,768]{1,0:T(8,128)}, f32[200,768]{1,0:T(8,128)S(1)}, u32[]{:S(2)}, u32[]{:S(2)}) collective-permute-start(f32[200,768]{1,0:T(8,128)} %get-tuple-element.50.own_any), channel_id=1, source_target_pairs={{0,2},{1,3},{2,0},{3,1},{4,6},{5,7},{6,4},{7,5},{8,10},{9,11},{10,... | collective-permute-start | bytes 1843208 | tf_op jit(solution)/shard_map/ppermute | solution.py:458
  11.6 25.4 %all-to-all-start = ((f32[32,1,2304]{2,1,0:T(1,128)}), f32[32,1,2304]{2,1,0:T(1,128)S(1)}, u32[]{:S(2)}, u32[]{:S(2)}) async-start(f32[32,1,2304]{2,1,0:T(1,128)} %bitcast.1), calls=%async_computation | async-start | bytes 589824 | tf_op jit(solution)/shard_map/all_to_all | solution.py:470
  22.8 2.5 %collective-permute-start.2 = (f32[1,1152]{1,0:T(1,128)S(1)}, f32[1,1152]{1,0:T(1,128)S(1)}, u32[]{:S(2)}, u32[]{:S(2)}) collective-permute-start(f32[1,1152]{1,0:T(1,128)S(1)} %copy-done.14), channel_id=1, source_target_pairs={{0,1},{1,0},{2,3},{3,2},{4,5},{5,4},{6,7},{7,6},{8,9},{9,8},{10,11... | collective-permute-start | bytes 13832 | tf_op jit(solution)/shard_map/ppermute | solution.py:458
  24.2 2.5 %collective-permute-start.3 = (f32[1,1152]{1,0:T(1,128)S(1)}, f32[1,1152]{1,0:T(1,128)S(1)}, u32[]{:S(2)}, u32[]{:S(2)}) collective-permute-start(f32[1,1152]{1,0:T(1,128)S(1)} %copy-done.14), channel_id=1, source_target_pairs={{0,2},{1,3},{2,0},{3,1},{4,6},{5,7},{6,4},{7,5},{8,10},{9,11},{10,... | collective-permute-start | bytes 13832 | tf_op jit(solution)/shard_map/ppermute | solution.py:458
  25.3 3.3 %collective-permute-start.4 = (f32[1,1152]{1,0:T(1,128)S(1)}, f32[1,1152]{1,0:T(1,128)S(1)}, u32[]{:S(2)}, u32[]{:S(2)}) collective-permute-start(f32[1,1152]{1,0:T(1,128)S(1)} %copy-done.14), channel_id=1, source_target_pairs={{0,3},{1,2},{2,1},{3,0},{4,7},{5,6},{6,5},{7,4},{8,11},{9,10},{10,... | collective-permute-start | bytes 13832 | tf_op jit(solution)/shard_map/ppermute | solution.py:458
  26.7 2.0 %collective-permute-start.6 = (f32[384]{0:T(512)S(1)}, f32[384]{0:T(512)S(1)}, u32[]{:S(2)}, u32[]{:S(2)}) collective-permute-start(f32[384]{0:T(512)S(1)} %copy-done.21), channel_id=1, source_target_pairs={{0,1},{1,0},{2,3},{3,2},{4,5},{5,4},{6,7},{7,6},{8,9},{9,8},{10,11... | collective-permute-start | bytes 4616 | tf_op jit(solution)/shard_map/ppermute | solution.py:458
  37.1 3.0 %collective-permute-start.9 = (f32[576,128]{1,0:T(8,128)S(1)}, f32[576,128]{1,0:T(8,128)S(1)}, u32[]{:S(2)}, u32[]{:S(2)}) collective-permute-start(f32[576,128]{1,0:T(8,128)S(1)} %bitcast.17), channel_id=1, source_target_pairs={{0,1},{1,0},{2,3},{3,2},{4,5},{5,4},{6,7},{7,6},{8,9},{9,8},{10,11... | collective-permute-start | bytes 884744 | tf_op jit(solution)/shard_map/ppermute | solution.py:458
  37.3 2.7 %collective-permute-start.8 = (f32[2,1152]{1,0:T(2,128)}, f32[2,1152]{1,0:T(2,128)S(1)}, u32[]{:S(2)}, u32[]{:S(2)}) collective-permute-start(f32[2,1152]{1,0:T(2,128)} %get-tuple-element.53.mine_ref), channel_id=1, source_target_pairs={{0,2},{1,3},{2,0},{3,1},{4,6},{5,7},{6,4},{7,5},{8,10},{9,11},{10,... | collective-permute-start | bytes 27656 | tf_op jit(solution)/shard_map/ppermute | solution.py:458
  40.7 6.2 %copy-start.5 = (f32[768,384]{1,0:T(8,128)S(1)}, f32[768,384]{1,0:T(8,128)}, u32[]{:S(2)}) copy-start(f32[768,384]{1,0:T(8,128)} %up_ref.1) | copy-start | bytes 3538948
  40.7 6.2 %copy-start.6 = (f32[384,768]{1,0:T(8,128)S(1)}, f32[384,768]{1,0:T(8,128)}, u32[]{:S(2)}) copy-start(f32[384,768]{1,0:T(8,128)} %down_ref.1) | copy-start | bytes 3538948
  40.8 6.2 %copy-start.8 = (f32[768,384]{1,0:T(8,128)S(1)}, f32[768,384]{1,0:T(8,128)}, u32[]{:S(2)}) copy-start(f32[768,384]{1,0:T(8,128)} %copy-done.7) | copy-start | bytes 3538948
  40.8 6.2 %copy-start.10 = (f32[384,768]{1,0:T(8,128)S(1)}, f32[384,768]{1,0:T(8,128)}, u32[]{:S(2)}) copy-start(f32[384,768]{1,0:T(8,128)} %copy-done.9) | copy-start | bytes 3538948
  41.5 5.4 %collective-permute-start.10 = (f32[2,1280]{1,0:T(2,128)S(1)}, f32[2,1280]{1,0:T(2,128)S(1)}, u32[]{:S(2)}, u32[]{:S(2)}) collective-permute-start(f32[2,1280]{1,0:T(2,128)S(1)} %get-tuple-element.57.packed_ref), channel_id=1, source_target_pairs={{0,2},{1,3},{2,0},{3,1},{4,6},{5,7},{6,4},{7,5},{8,10},{9,11},{10,... | collective-permute-start | bytes 30728 | tf_op jit(solution)/shard_map/ppermute | solution.py:458
  42.9 4.0 %collective-permute-start.11 = (f32[2,1152]{1,0:T(2,128)S(1)}, f32[2,1152]{1,0:T(2,128)S(1)}, u32[]{:S(2)}, u32[]{:S(2)}) collective-permute-start(f32[2,1152]{1,0:T(2,128)S(1)} %get-tuple-element.65.unit_ref.row_ref), channel_id=1, source_target_pairs={{0,4},{4,0},{8,12},{12,8},{16,20},{20,16},{24,28},{28,24},{32,36},... | collective-permute-start | bytes 27656 | tf_op jit(solution)/shard_map/ppermute | solution.py:463
  51.7 17.1 %collective-permute-start.12 = (f32[400,768]{1,0:T(8,128)S(1)}, f32[400,768]{1,0:T(8,128)S(1)}, u32[]{:S(2)}, u32[]{:S(2)}) collective-permute-start(f32[400,768]{1,0:T(8,128)S(1)} %copy-done), channel_id=1, source_target_pairs={{0,1},{1,0},{2,3},{3,2},{4,5},{5,4},{6,7},{7,6},{8,9},{9,8},{10,11... | collective-permute-start | bytes 3686408 | tf_op jit(solution)/shard_map/ppermute | solution.py:458
  54.5 14.4 %collective-permute-start.13 = (f32[400,384]{1,0:T(8,128)}, f32[400,384]{1,0:T(8,128)}, u32[]{:S(2)}, u32[]{:S(2)}) collective-permute-start(f32[400,384]{1,0:T(8,128)} %get-tuple-element.71.slope_sib_ref), channel_id=1, source_target_pairs={{0,1},{1,0},{2,3},{3,2},{4,5},{5,4},{6,7},{7,6},{8,9},{9,8},{10,11... | collective-permute-start | bytes 1843208 | tf_op jit(solution)/shard_map/ppermute | solution.py:458
  54.6 13.1 %copy-start.3 = (f32[2,768]{1,0:T(2,128)S(1)}, f32[2,768]{1,0:T(2,128)}, u32[]{:S(2)}) copy-start(f32[2,768]{1,0:T(2,128)} %get-tuple-element.73.hidden_ref) | copy-start | bytes 18436
  55.3 21.4 %all-to-all-start.1 = ((f32[32,1,2304]{2,1,0:T(1,128)}), f32[32,1,2304]{2,1,0:T(1,128)S(1)}, u32[]{:S(2)}, u32[]{:S(2)}) async-start(f32[32,1,2304]{2,1,0:T(1,128)} %bitcast.20), calls=%async_computation.1 | async-start | bytes 589824 | tf_op jit(solution)/shard_map/all_to_all | solution.py:470
  65.0 16.5 %collective-permute-start.16 = (f32[196,768]{1,0:T(8,128)}, f32[196,768]{1,0:T(8,128)}, u32[]{:S(2)}, u32[]{:S(2)}) collective-permute-start(f32[196,768]{1,0:T(8,128)} %copy-done.11), channel_id=1, source_target_pairs={{0,2},{1,3},{2,0},{3,1},{4,6},{5,7},{6,4},{7,5},{8,10},{9,11},{10,... | collective-permute-start | bytes 1806344 | tf_op jit(solution)/shard_map/ppermute | solution.py:458
  66.3 2.6 %collective-permute-start.14 = (f32[4,768]{1,0:T(4,128)S(1)}, f32[4,768]{1,0:T(4,128)S(1)}, u32[]{:S(2)}, u32[]{:S(2)}) collective-permute-start(f32[4,768]{1,0:T(4,128)S(1)} %get-tuple-element.72.grad_ref), channel_id=1, source_target_pairs={{0,1},{1,0},{2,3},{3,2},{4,5},{5,4},{6,7},{7,6},{8,9},{9,8},{10,11... | collective-permute-start | bytes 36872 | tf_op jit(solution)/shard_map/ppermute | solution.py:458
  67.7 1.2 %collective-permute-start.15 = (f32[2,768]{1,0:T(2,128)S(1)}, f32[2,768]{1,0:T(2,128)S(1)}, u32[]{:S(2)}, u32[]{:S(2)}) collective-permute-start(f32[2,768]{1,0:T(2,128)S(1)} %copy-done.3), channel_id=1, source_target_pairs={{0,1},{1,0},{2,3},{3,2},{4,5},{5,4},{6,7},{7,6},{8,9},{9,8},{10,11... | collective-permute-start | bytes 18440 | tf_op jit(solution)/shard_map/ppermute | solution.py:458
  74.5 6.9 %copy-start.12 = (f32[7,7,768]{2,1,0:T(8,128)S(1)}, f32[7,7,768]{2,1,0:T(8,128)}, u32[]{:S(2)}) copy-start(f32[7,7,768]{2,1,0:T(8,128)} %w_ref.1) | copy-start | bytes 451588
  74.5 6.9 %copy-start.16 = (f32[196,768]{1,0:T(8,128)S(1)}, f32[196,768]{1,0:T(8,128)}, u32[]{:S(2)}) copy-start(f32[196,768]{1,0:T(8,128)} %copy-done.15) | copy-start | bytes 1806340
  74.5 6.9 %copy-start.17 = (f32[14,16,128]{2,1,0:T(8,128)S(1)}, f32[14,16,128]{2,1,0:T(8,128)}, u32[]{:S(2)}) copy-start(f32[14,16,128]{2,1,0:T(8,128)} %get-tuple-element.82.rstd_ref) | copy-start | bytes 344068
  74.5 6.9 %copy-start.18 = (f32[1,768]{1,0:T(1,128)S(1)}, f32[1,768]{1,0:T(1,128)}, u32[]{:S(2)}) copy-start(f32[1,768]{1,0:T(1,128)} %get-tuple-element.83.gain_ref) | copy-start | bytes 9220
  77.0 9.7 %collective-permute-start.17 = (f32[1,1152]{1,0:T(1,128)S(1)}, f32[1,1152]{1,0:T(1,128)S(1)}, u32[]{:S(2)}, u32[]{:S(2)}) collective-permute-start(f32[1,1152]{1,0:T(1,128)S(1)} %get-tuple-element.89), channel_id=1, source_target_pairs={{0,1},{1,0},{2,3},{3,2},{4,5},{5,4},{6,7},{7,6},{8,9},{9,8},{10,11... | collective-permute-start | bytes 13832 | tf_op jit(solution)/shard_map/ppermute | solution.py:458
  79.7 7.0 %collective-permute-start.18 = (f32[1,1152]{1,0:T(1,128)S(1)}, f32[1,1152]{1,0:T(1,128)S(1)}, u32[]{:S(2)}, u32[]{:S(2)}) collective-permute-start(f32[1,1152]{1,0:T(1,128)S(1)} %get-tuple-element.90), channel_id=1, source_target_pairs={{0,2},{1,3},{2,0},{3,1},{4,6},{5,7},{6,4},{7,5},{8,10},{9,11},{10,... | collective-permute-start | bytes 13832 | tf_op jit(solution)/shard_map/ppermute | solution.py:458
  80.9 5.8 %collective-permute-start.19 = (f32[1,1152]{1,0:T(1,128)S(1)}, f32[1,1152]{1,0:T(1,128)S(1)}, u32[]{:S(2)}, u32[]{:S(2)}) collective-permute-start(f32[1,1152]{1,0:T(1,128)S(1)} %get-tuple-element.91), channel_id=1, source_target_pairs={{0,3},{1,2},{2,1},{3,0},{4,7},{5,6},{6,5},{7,4},{8,11},{9,10},{10,... | collective-permute-start | bytes 13832 | tf_op jit(solution)/shard_map/ppermute | solution.py:458
  (13 other events, 37.5 us)

commit v3 on v2

--- a/solution.py
+++ b/solution.py
@@ -57,6 +57,24 @@
                 total = total + matrix_ref[block * LANES : (block + 1) * LANES, lanes] * vector[:, lanes]
             rows[i].append(jnp.sum(total.T, axis=0, keepdims=True))
     return [jnp.concatenate(row, axis=1) for row in rows]
+
+
+def column_dots(vectors, matrix_ref):
+    count, width = matrix_ref.shape
+    totals = [[None] * (width // LANES) for _ in vectors]
+    for block in range(count // LANES):
+        rows = slice(block * LANES, (block + 1) * LANES)
+        for i, vector in enumerate(vectors):
+            column = jnp.broadcast_to(vector[:, rows], (LANES, LANES)).T
+            for tile in range(width // LANES):
+                term = matrix_ref[rows, tile * LANES : (tile + 1) * LANES] * column
+                term = jnp.sum(term.reshape(LANES // 8, 8, LANES), axis=0)
+                old = totals[i][tile]
+                totals[i][tile] = term if old is None else old + term
+    return [
+        jnp.concatenate([jnp.sum(part, axis=0, keepdims=True) for part in total], axis=1)
+        for total in totals
+    ]
 
 
 def gathered_rows(flat_ref, rows_ref):
@@ -153,14 +171,18 @@
     )(images.reshape(-1, LANES), dw_kernel, norm_gain)
 
 
+def spread_rows(row, out_ref, place):
+    tiles = row.shape[1] // LANES
+    copies = out_ref.shape[0] // (2 * tiles)
+    for tile in range(tiles):
+        out_ref[pl.ds(place * tiles + tile, copies, stride=2 * tiles), :] = jnp.broadcast_to(
+            row[:, tile * LANES : (tile + 1) * LANES], (copies, LANES)
+        )
+
+
 def spread_kernel(row_ref, other_ref, out_ref):
-    tiles = row_ref.shape[1] // LANES
-    copies = out_ref.shape[0] // (2 * tiles)
-    for k, row in enumerate((row_ref, other_ref)):
-        for tile in range(tiles):
-            out_ref[pl.ds(k * tiles + tile, copies, stride=2 * tiles), :] = jnp.broadcast_to(
-                row[0:1, tile * LANES : (tile + 1) * LANES], (copies, LANES)
-            )
+    spread_rows(row_ref[...], out_ref, 0)
+    spread_rows(other_ref[...], out_ref, 1)
 
 
 def spread_pair(row, other, peers):
@@ -171,7 +193,8 @@
 def mlp_kernel(
     own_any, across_any, up_any, up_sib_any, bias_any, bias_sib_any, down_any, down_sib_any, scale_any, proj_any,
     sum_any, both_ref, slope_ref, slope_sib_ref, hidden_ref, part_ref,
-    up_ref, up_sib_ref, bias_ref, down_ref, down_sib_ref, scale_ref, proj_ref, sum_ref, sems, *, positions,
+    up_ref, up_sib_ref, bias_ref, down_ref, down_sib_ref, scale_ref, proj_ref, sum_ref, sems, late_sems,
+    *, positions,
 ):
     offset = own_any.shape[0]
     width = up_ref.shape[1]
@@ -183,14 +206,17 @@
         (bias_any, bias_ref.at[0]),
         (bias_sib_any, bias_ref.at[1]),
         (up_sib_any, up_sib_ref),
+    )
+    for copy in copies[:5]:
+        copy.wait()
+    late = fetch(
+        late_sems,
         (scale_any, scale_ref.at[0]),
         (sum_any, sum_ref),
         (down_any, down_ref),
         (down_sib_any, down_sib_ref),
         (proj_any, proj_ref),
     )
-    for copy in copies[:5]:
-        copy.wait()
     for s, (weight, out) in enumerate(((up_ref, slope_ref), (up_sib_ref, slope_sib_ref))):
         if s == 1:
             copies[5].wait()
@@ -203,14 +229,17 @@
                 act[k * offset : k * offset + positions], axis=0, keepdims=True
             )
     hidden = hidden_ref[...]
-    for copy in copies[6:10]:
+    for copy in late[:4]:
         copy.wait()
-    part = dot(hidden[:, :width], down_ref[...]) + dot(hidden[:, width:], down_sib_ref[...])
-    part = part * scale_ref[...]
-    own = lax.broadcasted_iota(jnp.int32, part.shape, 0) == 0
-    part = part + jnp.where(own, sum_ref[...], 0.0)
-    copies[10].wait()
-    part_ref[...] = dot(part * (1.0 / positions), proj_ref[...])
+    first = column_dots((hidden[0:1, :width], hidden[1:2, :width]), down_ref)
+    second = column_dots((hidden[0:1, width:], hidden[1:2, width:]), down_sib_ref)
+    pooled = []
+    for k in range(2):
+        row = (first[k] + second[k]) * scale_ref[...]
+        pooled.append((row + sum_ref[...] if k == 0 else row) * (1.0 / positions))
+    late[4].wait()
+    for k, row in enumerate(column_dots(pooled, proj_ref)):
+        part_ref[pl.ds(k, 1), :] = row
 
 
 def mlp(own, across, up, up_sib, bias, bias_sib, down, down_sib, scale, projection, image_sum, positions):
@@ -233,7 +262,8 @@
             pltpu.VMEM((1, channels), F32),
             pltpu.VMEM(projection.shape, F32),
             pltpu.VMEM(image_sum.shape, F32),
-            pltpu.SemaphoreType.DMA((11,)),
+            pltpu.SemaphoreType.DMA((6,)),
+            pltpu.SemaphoreType.DMA((5,)),
         ],
         us=5.0,
         mib=WIDE,
@@ -247,7 +277,7 @@
 
 def pair_kernel(
     mine_ref, other_ref, texts_ref, texts_sib_ref, dp_ref, scale_ref, shift_ref,
-    unit_ref, inverse_ref, packed_ref, features, text, text_sib,
+    unit_ref, inverse_ref, packed_ref, spread_ref, features, text, text_sib,
 ):
     embed = unit_ref.shape[1]
     gathered_rows(texts_ref, text)
@@ -257,6 +287,8 @@
     unit, inverse = normal(features[...])
     inverse_ref[...] = jnp.broadcast_to(inverse, inverse_ref.shape)
     unit_ref[...] = unit
+    spread_rows(unit[0:1], spread_ref, 0)
+    spread_rows(unit[1:2], spread_ref, 1)
     step = jnp.zeros(unit.shape, F32)
     losses = jnp.zeros((2, 1), F32)
     for s, block_ref in enumerate((text, text_sib)):
@@ -282,7 +314,7 @@
     count = texts.size // embed
     return call(
         pair_kernel,
-        [(2, embed), (2, LANES), (2, embed + LANES)],
+        [(2, embed), (2, LANES), (2, embed + LANES), texts.shape],
         [VMEM] * 4 + [SMEM] * 3,
         [
             pltpu.VMEM(mine.shape, F32),
@@ -360,14 +392,17 @@
 
 
 def back_kernel(
-    mine_ref, other_ref, both_ref, rstd_ref, w_ref, gain_ref, const_ref, out_ref, pad, slope, unit
-):
+    mine_ref, other_any, both_ref, rstd_ref, w_ref, gain_ref, const_ref, out_ref, pad, slope, unit,
+    other_ref, sems,
+):
+    copies = fetch(sems, (other_any, other_ref))
     tiles, side = slope.shape[0], slope.shape[1]
     reach = w_ref.shape[0] // 2
     channels = tiles * LANES
     pad[...] = jnp.zeros_like(pad)
     unit[...] = jnp.zeros_like(unit)
     slope[...] = jnp.zeros_like(slope)
+    copies[0].wait()
     first = jnp.zeros((side, 16, LANES), F32)
     second = jnp.zeros((side, 16, LANES), F32)
     for tile in range(tiles):
@@ -407,18 +442,20 @@
     return call(
         back_kernel,
         [(side * side * tiles, LANES)],
-        [VMEM] * 7,
+        [VMEM, ANY] + [VMEM] * 5,
         [
             pltpu.VMEM((tiles, side + taps - 1, 24, LANES), F32),
             pltpu.VMEM((tiles, side, 16, LANES), F32),
             pltpu.VMEM((tiles, side, 16, LANES), F32),
+            pltpu.VMEM(other.shape, F32),
+            pltpu.SemaphoreType.DMA((1,)),
         ],
         us=4.0,
     )(mine, other, both, rstd, dw_kernel, norm_gain, const)[0]
 
 
 def column_kernel(
-    flat_ref, t0_ref, t1_ref, t2_ref, t3_ref, dp_ref, scale_ref, shift_ref, o0, o1, o2, o3, images_ref
+    flat_ref, t0_ref, t1_ref, t2_ref, t3_ref, place_ref, scale_ref, shift_ref, o0, o1, o2, o3, images_ref
 ):
     gathered_rows(flat_ref, images_ref)
     images = images_ref[...]
@@ -428,11 +465,11 @@
         slopes = 1.0 / (1.0 + jnp.exp(-logits))
         if k == 0:
             rows = lax.broadcasted_iota(jnp.int32, logits.shape, 0)
-            slopes = slopes - jnp.where(rows == dp_ref[0], 1.0, 0.0)
+            slopes = slopes - jnp.where(rows == place_ref[0], 1.0, 0.0)
         out[...] = jnp.sum(images * (scale_ref[0] * slopes), axis=0, keepdims=True)
 
 
-def columns_of(images, texts, dp, scale, shift):
+def columns_of(images, texts, place, scale, shift):
     embed = texts[0].shape[1]
     return call(
         column_kernel,
@@ -440,7 +477,7 @@
         [VMEM] * 5 + [SMEM] * 3,
         [pltpu.VMEM((images.size // embed, embed), F32)],
         us=0.5,
-    )(images, *texts, dp, scale, shift)
+    )(images, *texts, place, scale, shift)
 
 
 def text_kernel(text_ref, a_ref, b_ref, c_ref, d_ref, out_ref):
@@ -461,6 +498,14 @@
 def mirrored(value):
     peers = lax.axis_size("dp")
     return lax.ppermute(value, "dp", [(i, i ^ 1) for i in range(peers)])
+
+
+def cornered(value):
+    peers, cores = lax.axis_size("dp"), lax.axis_size("fsdp")
+    moves = [
+        (i * cores + j, (i ^ 1) * cores + (j ^ 1)) for i in range(peers) for j in range(cores)
+    ]
+    return lax.ppermute(value, ("dp", "fsdp"), moves)
 
 
 def spread_out(flat):
@@ -490,45 +535,46 @@
     place = (lax.axis_index("dp") // 2 * 2).astype(jnp.int32)[None]
     scale, shift = logit_scale[None], logit_bias[None]
     text_other = mirrored(text_embed)
-    up_sib, down_sib, bias_sib = swapped(up_weight, 1), swapped(down_weight, 1), swapped(up_bias, 1)
-
     normed, rstd, image_sum, gain = front(images, dw_kernel, norm_gain)
-    text_other, normed = lax.optimization_barrier((text_other, normed))
+    text_other, normed, own_up, own_down, own_bias = lax.optimization_barrier(
+        (text_other, normed, up_weight, down_weight, up_bias)
+    )
     across = swapped(normed, 2)
+    up_sib, down_sib, bias_sib = swapped(own_up, 1), swapped(own_down, 1), swapped(own_bias, 1)
     texts = spread_out(spread_pair(text_embed, text_other, peers))
-    group_texts = tuple(swapped(text_embed, k) for k in (1, 2, 3))
+    positions = images.shape[1] * images.shape[2]
+    group_texts = (swapped(text_embed, 1), text_other, swapped(text_other, 1))
     across, group_texts = lax.optimization_barrier((across, group_texts))
     both, slope, slope_sib, hidden, part = mlp(
         normed, across, up_weight, up_sib, up_bias, bias_sib, down_weight, down_sib, layer_scale,
-        projection, image_sum, images.shape[1] * images.shape[2],
+        projection, image_sum, positions,
     )
     part_other = swapped(part, 2)
     texts, hidden = lax.optimization_barrier((texts, hidden))
     texts_sib = swapped(texts, 1)
-    image_unit, inverse, packed = pairs(
+    image_unit, inverse, packed, image_rows = pairs(
         part, part_other, texts, texts_sib, place, scale, shift
     )
     packed_other = swapped(packed, 2)
-    unit_other = mirrored(image_unit)
-    packed_other, unit_other = lax.optimization_barrier((packed_other, unit_other))
+    packed, both, slope_sib, hidden = lax.optimization_barrier((packed, both, slope_sib, hidden))
+    both_sib, slope_back, hidden_sib = swapped(both, 1), swapped(slope_sib, 1), swapped(hidden, 1)
     losses, const, grad, own_grad, across_grad = slopes_of(
         packed, packed_other, image_unit, inverse, projection, layer_scale,
-        down_weight, down_sib, up_weight, up_sib, slope, slope_sib, images.shape[1] * images.shape[2],
-    )
-    grad, both, slope_sib, hidden = lax.optimization_barrier((grad, both, slope_sib, hidden))
-    both_sib, slope_back, hidden_sib = swapped(both, 1), swapped(slope_sib, 1), swapped(hidden, 1)
-    across_grad, image_unit, unit_other = lax.optimization_barrier((across_grad, image_unit, unit_other))
+        down_weight, down_sib, up_weight, up_sib, slope, slope_sib, positions,
+    )
+    across_grad, image_rows = lax.optimization_barrier((across_grad, image_rows))
     other_grad = swapped(across_grad, 2)
-    image_units = spread_out(spread_pair(image_unit, unit_other, peers))
+    image_units = spread_out(image_rows)
     up_grad, down_grad = last_grads(
         both, both_sib, slope, slope_back, grad, swapped(grad, 1), hidden, hidden_sib
     )
-    image_units, up_grad = lax.optimization_barrier((image_units, up_grad))
+    other_grad, up_grad = lax.optimization_barrier((other_grad, up_grad))
+    input_grad = back(own_grad, other_grad, both, rstd, dw_kernel, gain, const, images.shape[1])
+    image_units, input_grad = lax.optimization_barrier((image_units, input_grad))
     steps = columns_of(image_units, (text_embed,) + group_texts, place, scale, shift)
-    input_grad = back(own_grad, other_grad, both, rstd, dw_kernel, gain, const, images.shape[1])
-    first_step, input_grad = lax.optimization_barrier((steps[0], input_grad))
+    first_step = steps[0]
     text_grad = text_grads(
-        text_embed, (first_step,) + tuple(swapped(steps[k], k) for k in (1, 2, 3))
+        text_embed, (first_step, swapped(steps[1], 1), mirrored(steps[2]), cornered(steps[3]))
     )
     return (
         input_grad.reshape(images.shape),

time: 87.9 us -> 83.9 us (0.954)
  starting transfers between devices: 44 us -> 38.6 us
  waiting for transfers between devices: 7.88 us -> 8.96 us
    ppermute x18 -> x15, starting transfers between devices: 21.4 us -> 12.9 us  [swapped(): return lax.ppermute(value, 'fsdp', [(i, i ^ by) for i in range(peers)])]
    ppermute x2, starting transfers between devices: 1.83 us -> 5.41 us  [mirrored(): return lax.ppermute(value, 'dp', [(i, i ^ 1) for i in range(peers)])]
    ppermute x2, waiting for transfers between devices: 3.19 us -> 0.75 us  [mirrored(): return lax.ppermute(value, 'dp', [(i, i ^ 1) for i in range(peers)])]
    ppermute x0 -> x1, waiting for transfers between devices: none -> 2.3 us  [cornered(): return lax.ppermute(value, ('dp', 'fsdp'), moves)]
    all_to_all x2, starting transfers between devices: 20.8 us -> 18.9 us  [spread_out(): lax.all_to_all(rows, 'dp', 0, 0, axis_index_groups=groups, tiled=True)]
    ppermute x0 -> x1, starting transfers between devices: none -> 1.49 us  [cornered(): return lax.ppermute(value, ('dp', 'fsdp'), moves)]
    ppermute x18 -> x15, waiting for transfers between devices: 2.56 us -> 3.97 us  [swapped(): return lax.ppermute(value, 'fsdp', [(i, i ^ by) for i in range(peers)])]
    pallas_call x1, Pallas kernels: 4.69 us -> 5.69 us  [slopes_of(): call(slope_kernel, [(1, LANES), (1, channels), (4, channels), (positions,...]
  transfers between devices with their start and end apart: 22 -> 20, of which waited for: 6 -> 9; matrix products, arithmetic and copies ran while one was open for 0% -> 0% of each run, Pallas kernels for 28% -> 35%
where the time goes in v3:
time: 83.9 us; the launch traced here: 83.4 us
  starting transfers between devices  38.6 us (46%)
  Pallas kernels  31.2 us (37%)
  waiting for transfers between devices  8.96 us (11%)
  local copies, waits for them, and re-layouts  2.51 us (3%)
  between operations  2.13 us (3%)
    all_to_all x2, starting transfers between devices, spread_out(): lax.all_to_all(rows, 'dp', 0, 0, axis_index_groups=groups, tiled=True)  18.9 us
    ppermute x15, starting transfers between devices, swapped(): return lax.ppermute(value, 'fsdp', [(i, i ^ by) for i in range(peers)])  12.9 us
    pallas_call x1, Pallas kernels, mlp(): call(functools.partial(mlp_kernel, positions=positions), [(rows, channels...  6.31 us
    pallas_call x1, Pallas kernels, slopes_of(): call(slope_kernel, [(1, LANES), (1, channels), (4, channels), (positions,...  5.69 us
    pallas_call x1, Pallas kernels, last_grads(): call(last_kernel, [(channels, width), (width, channels)], [VMEM] * 8, us=...  5.65 us
    pallas_call x1, Pallas kernels, front(): call(front_kernel, [(pl.cdiv(side * side, 8) * 8, channels), (side, 16, L...  5.52 us
    ppermute x2, starting transfers between devices, mirrored(): return lax.ppermute(value, 'dp', [(i, i ^ 1) for i in range(peers)])  5.41 us
    pallas_call x1, Pallas kernels, back(): call(back_kernel, [(side * side * tiles, LANES)], [VMEM, ANY] + [VMEM] *...  5.02 us
  transfers between devices with their start and end apart: 20, of which 9 were waited for; matrix products, arithmetic and copies ran while one was open for 0% of the time, Pallas kernels for 35%

profile of v3, /device:TPU:1, one launch (start us, length us, event | category | flops | bytes accessed | tf_op | source)
XLA Modules:
  0.0 83.4 jit_solution(17238320545245289496)
XLA Ops:
  0.6 3.7 %collective-permute-start = (f32[1,1152]{1,0:T(1,128)}, f32[1,1152]{1,0:T(1,128)S(1)}, u32[]{:S(2)}, u32[]{:S(2)}) collective-permute-start(f32[1,1152]{1,0:T(1,128)} %text_ref.1), channel_id=1, source_target_pairs={{0,4},{4,0},{8,12},{12,8},{16,20},{20,16},{24,28},{28,24},{32,36},... | collective-permute-start | bytes 13832 | tf_op jit(solution)/shard_map/ppermute | solution.py:500
  4.3 5.5 %shard_map.146 = (f32[200,768]{1,0:T(8,128)}, f32[14,16,128]{2,1,0:T(8,128)}, f32[1,768]{1,0:T(1,128)}, f32[1,768]{1,0:T(1,128)}) custom-call(f32[1176,128]{1,0:T(8,128)} %bitcast.22, f32[7,7,768]{2,1,0:T(8,128)} %w_ref.1, f32[768]{0:T(1024)} %gain_any.1), custom_call_target="tpu_custom_call" | custom-call | flops 4600000000 | bytes 12000000 | tf_op jit(solution)/shard_map/pallas_call | solution.py:153
  9.9 1.0 %collective-permute-start.4 = (f32[768,384]{1,0:T(8,128)S(1)}, f32[768,384]{1,0:T(8,128)}, u32[]{:S(2)}, u32[]{:S(2)}) collective-permute-start(f32[768,384]{1,0:T(8,128)S(1)} %copy-done.4), channel_id=1, source_target_pairs={{0,1},{1,0},{2,3},{3,2},{4,5},{5,4},{6,7},{7,6},{8,9},{9,8},{10,11... | collective-permute-start | bytes 3538952 | tf_op jit(solution)/shard_map/ppermute | solution.py:495
  11.3 0.7 shard_map.148
  12.1 11.2 %all-to-all-start = ((f32[32,1,2304]{2,1,0:T(1,128)}), f32[32,1,2304]{2,1,0:T(1,128)S(1)}, u32[]{:S(2)}, u32[]{:S(2)}) async-start(f32[32,1,2304]{2,1,0:T(1,128)} %bitcast.1), calls=%async_computation | async-start | bytes 589824 | tf_op jit(solution)/shard_map/all_to_all | solution.py:515
  23.3 1.0 %collective-permute-start.2 = (f32[1,1152]{1,0:T(1,128)S(1)}, f32[1,1152]{1,0:T(1,128)S(1)}, u32[]{:S(2)}, u32[]{:S(2)}) collective-permute-start(f32[1,1152]{1,0:T(1,128)S(1)} %copy-done.10), channel_id=1, source_target_pairs={{0,1},{1,0},{2,3},{3,2},{4,5},{5,4},{6,7},{7,6},{8,9},{9,8},{10,11... | collective-permute-start | bytes 13832 | tf_op jit(solution)/shard_map/ppermute | solution.py:495
  24.4 0.7 collective-permute-done.2.t1_ref
  25.5 0.8 collective-permute-done.1.across_any
  26.3 0.8 copy-done.16
  27.1 6.3 %shard_map.147 = (f32[400,768]{1,0:T(8,128)}, f32[400,384]{1,0:T(8,128)}, f32[400,384]{1,0:T(8,128)}, f32[2,768]{1,0:T(2,128)}, f32[2,1152]{1,0:T(2,128)}) custom-call(f32[200,768]{1,0:T(8,128)} %get-tuple-element.51.own_any, f32[200,768]{1,0:T(8,128)} %copy-done.16, f32[768,384]{1,0:T(8,128)} %up_ref.1, ...), custom_call_target="tpu_custom_call" | custom-call | flops 5750000128 | bytes 15000000 | tf_op jit(solution)/shard_map/pallas_call | solution.py:249
  33.4 1.9 %all-to-all-done = f32[32,1,2304]{2,1,0:T(1,128)S(1)} async-done(((f32[32,1,2304]{2,1,0:T(1,128)}), f32[32,1,2304]{2,1,0:T(1,128)S(1)}, u32[]{:S(2)}, u32[]{:S(2)}) %all-to-all-start) | async-done | bytes 294944 | tf_op jit(solution)/shard_map/all_to_all | solution.py:515
  35.3 2.2 %collective-permute-start.8 = (f32[576,128]{1,0:T(8,128)S(1)}, f32[576,128]{1,0:T(8,128)S(1)}, u32[]{:S(2)}, u32[]{:S(2)}) collective-permute-start(f32[576,128]{1,0:T(8,128)S(1)} %bitcast.17), channel_id=1, source_target_pairs={{0,1},{1,0},{2,3},{3,2},{4,5},{5,4},{6,7},{7,6},{8,9},{9,8},{10,11... | collective-permute-start | bytes 884744 | tf_op jit(solution)/shard_map/ppermute | solution.py:495
  37.6 1.2 %collective-permute-start.7 = (f32[2,1152]{1,0:T(2,128)}, f32[2,1152]{1,0:T(2,128)S(1)}, u32[]{:S(2)}, u32[]{:S(2)}) collective-permute-start(f32[2,1152]{1,0:T(2,128)} %get-tuple-element.58.mine_ref), channel_id=1, source_target_pairs={{0,2},{1,3},{2,0},{3,1},{4,6},{5,7},{6,4},{7,5},{8,10},{9,11},{10,... | collective-permute-start | bytes 27656 | tf_op jit(solution)/shard_map/ppermute | solution.py:495
  40.3 0.7 copy-done.9
  41.0 1.1 %shard_map.149 = (f32[2,1152]{1,0:T(2,128)S(1)}, f32[2,128]{1,0:T(2,128)S(1)}, f32[2,1280]{1,0:T(2,128)S(1)}, f32[576,128]{1,0:T(8,128)}) custom-call(f32[2,1152]{1,0:T(2,128)S(1)} %copy-done.9, f32[2,1152]{1,0:T(2,128)S(1)} %collective-permute-done.7.other_ref, f32[576,128]{1,0:T(8,128)S(1)} %bitcast.18, ...), custom_call_target="tpu_custom_call" | custom-call | flops 6899999744 | bytes 18000000 | tf_op jit(solution)/shard_map/pallas_call | solution.py:315
  42.3 1.2 %collective-permute-start.11 = (f32[400,768]{1,0:T(8,128)S(1)}, f32[400,768]{1,0:T(8,128)S(1)}, u32[]{:S(2)}, u32[]{:S(2)}) collective-permute-start(f32[400,768]{1,0:T(8,128)S(1)} %copy-done), channel_id=1, source_target_pairs={{0,1},{1,0},{2,3},{3,2},{4,5},{5,4},{6,7},{7,6},{8,9},{9,8},{10,11... | collective-permute-start | bytes 3686408 | tf_op jit(solution)/shard_map/ppermute | solution.py:495
  43.4 1.2 %collective-permute-start.9 = (f32[2,1280]{1,0:T(2,128)S(1)}, f32[2,1280]{1,0:T(2,128)S(1)}, u32[]{:S(2)}, u32[]{:S(2)}) collective-permute-start(f32[2,1280]{1,0:T(2,128)S(1)} %get-tuple-element.65.packed_ref), channel_id=1, source_target_pairs={{0,2},{1,3},{2,0},{3,1},{4,6},{5,7},{6,4},{7,5},{8,10},{9,11},{10,... | collective-permute-start | bytes 30728 | tf_op jit(solution)/shard_map/ppermute | solution.py:495
  44.9 1.1 %collective-permute-done.9.other_ref = f32[2,1280]{1,0:T(2,128)S(1)} collective-permute-done((f32[2,1280]{1,0:T(2,128)S(1)}, f32[2,1280]{1,0:T(2,128)S(1)}, u32[]{:S(2)}, u32[]{:S(2)}) %collective-permute-start.9) | collective-permute-done | bytes 10272 | tf_op jit(solution)/shard_map/ppermute | solution.py:495
  46.0 5.7 %shard_map.150 = (f32[1,128]{1,0:T(1,128)}, f32[1,768]{1,0:T(1,128)S(1)}, f32[4,768]{1,0:T(4,128)S(1)}, f32[196,768]{1,0:T(8,128)S(1)}, f32[196,768]{1,0:T(8,128)}) custom-call(f32[2,1280]{1,0:T(2,128)S(1)} %get-tuple-element.65.packed_ref, f32[2,1280]{1,0:T(2,128)S(1)} %collective-permute-done.9.other_ref, f32[2,1152]{1,0:T(2,128)S(1)} %get-tuple-element.66.unit_ref, ...), custom_call_target="tpu_custom_call" | custom-call | flops 4600000000 | bytes 12000000 | tf_op jit(solution)/shard_map/pallas_call | solution.py:364
  51.7 0.8 copy-done.11
  52.5 1.2 %collective-permute-start.10 = (f32[196,768]{1,0:T(8,128)}, f32[196,768]{1,0:T(8,128)}, u32[]{:S(2)}, u32[]{:S(2)}) collective-permute-start(f32[196,768]{1,0:T(8,128)} %get-tuple-element.74), channel_id=1, source_target_pairs={{0,2},{1,3},{2,0},{3,1},{4,6},{5,7},{6,4},{7,5},{8,10},{9,11},{10,... | collective-permute-start | bytes 1806344 | tf_op jit(solution)/shard_map/ppermute | solution.py:495
  53.6 7.6 %all-to-all-start.1 = ((f32[32,1,2304]{2,1,0:T(1,128)}), f32[32,1,2304]{2,1,0:T(1,128)S(1)}, u32[]{:S(2)}, u32[]{:S(2)}) async-start(f32[32,1,2304]{2,1,0:T(1,128)} %bitcast.6), calls=%async_computation.1 | async-start | bytes 589824 | tf_op jit(solution)/shard_map/all_to_all | solution.py:515
  61.3 1.8 %collective-permute-start.13 = (f32[4,768]{1,0:T(4,128)S(1)}, f32[4,768]{1,0:T(4,128)S(1)}, u32[]{:S(2)}, u32[]{:S(2)}) collective-permute-start(f32[4,768]{1,0:T(4,128)S(1)} %get-tuple-element.76.grad_ref), channel_id=1, source_target_pairs={{0,1},{1,0},{2,3},{3,2},{4,5},{5,4},{6,7},{7,6},{8,9},{9,8},{10,11... | collective-permute-start | bytes 36872 | tf_op jit(solution)/shard_map/ppermute | solution.py:495
  63.3 1.1 %collective-permute-done.14.hidden_sib_ref = f32[2,768]{1,0:T(2,128)S(1)} collective-permute-done((f32[2,768]{1,0:T(2,128)S(1)}, f32[2,768]{1,0:T(2,128)S(1)}, u32[]{:S(2)}, u32[]{:S(2)}) %collective-permute-start.14) | collective-permute-done | bytes 6176 | tf_op jit(solution)/shard_map/ppermute | solution.py:495
  64.3 5.7 %shard_map.151 = (f32[768,384]{1,0:T(8,128)}, f32[384,768]{1,0:T(8,128)}) custom-call(f32[400,768]{1,0:T(8,128)S(1)} %copy-done, f32[400,768]{1,0:T(8,128)S(1)} %collective-permute-done.11.both_sib_ref, f32[400,384]{1,0:T(8,128)S(1)} %copy-done.1, f32[400,384]{1,0:T(8,128)} %collective-permute-done.12.slope_sib_ref, ...), custom_call_target="tpu_custom_call" | custom-call | flops 230000000 | bytes 600000 | tf_op jit(solution)/shard_map/pallas_call | solution.py:389
  70.0 5.0 %shard_map.152 = f32[1176,128]{1,0:T(8,128)} custom-call(f32[196,768]{1,0:T(8,128)S(1)} %copy-done.12, f32[196,768]{1,0:T(8,128)} %collective-permute-done.10.other_any, f32[400,768]{1,0:T(8,128)S(1)} %copy-done, f32[14,16,128]{2,1,0:T(8,128)S(1)} %copy-done.13, f32[7,7,768]{2,1,0:T(8,128)S(1)} %copy-done.8, f32[1,768]{1,0:T(1,128)S(1)} %copy-done.14, ...), custom_call_target="tpu_custom_call" | custom-call | flops 4600000000 | bytes 12000000 | tf_op jit(solution)/shard_map/pallas_call | solution.py:442
  75.4 0.9 %collective-permute-start.15 = (f32[1,1152]{1,0:T(1,128)S(1)}, f32[1,1152]{1,0:T(1,128)S(1)}, u32[]{:S(2)}, u32[]{:S(2)}) collective-permute-start(f32[1,1152]{1,0:T(1,128)S(1)} %get-tuple-element.91), channel_id=1, source_target_pairs={{0,1},{1,0},{2,3},{3,2},{4,5},{5,4},{6,7},{7,6},{8,9},{9,8},{10,11... | collective-permute-start | bytes 13832 | tf_op jit(solution)/shard_map/ppermute | solution.py:495
  76.3 1.7 %collective-permute-start.16 = (f32[1,1152]{1,0:T(1,128)S(1)}, f32[1,1152]{1,0:T(1,128)S(1)}, u32[]{:S(2)}, u32[]{:S(2)}) collective-permute-start(f32[1,1152]{1,0:T(1,128)S(1)} %get-tuple-element.92), channel_id=1, source_target_pairs={{0,4},{4,0},{8,12},{12,8},{16,20},{20,16},{24,28},{28,24},{32,36},... | collective-permute-start | bytes 13832 | tf_op jit(solution)/shard_map/ppermute | solution.py:500
  78.1 1.5 %collective-permute-start.17 = (f32[1,1152]{1,0:T(1,128)S(1)}, f32[1,1152]{1,0:T(1,128)S(1)}, u32[]{:S(2)}, u32[]{:S(2)}) collective-permute-start(f32[1,1152]{1,0:T(1,128)S(1)} %get-tuple-element.93), channel_id=1, source_target_pairs={{0,5},{1,4},{2,7},{3,6},{4,1},{5,0},{6,3},{7,2},{8,13},{9,12},{10,... | collective-permute-start | bytes 13832 | tf_op jit(solution)/shard_map/ppermute | solution.py:508
  79.6 0.7 collective-permute-done.16.c_ref
  80.3 2.3 %collective-permute-done.17.d_ref = f32[1,1152]{1,0:T(1,128)S(1)} collective-permute-done((f32[1,1152]{1,0:T(1,128)S(1)}, f32[1,1152]{1,0:T(1,128)S(1)}, u32[]{:S(2)}, u32[]{:S(2)}) %collective-permute-start.17) | collective-permute-done | bytes 4640 | tf_op jit(solution)/shard_map/ppermute | solution.py:508
  82.6 0.8 shard_map.154
  (56 shorter events, 2.2 us)
Async XLA Ops:
  0.6 9.2 %collective-permute-start = (f32[1,1152]{1,0:T(1,128)}, f32[1,1152]{1,0:T(1,128)S(1)}, u32[]{:S(2)}, u32[]{:S(2)}) collective-permute-start(f32[1,1152]{1,0:T(1,128)} %text_ref.1), channel_id=1, source_target_pairs={{0,4},{4,0},{8,12},{12,8},{16,20},{20,16},{24,28},{28,24},{32,36},... | collective-permute-start | bytes 13832 | tf_op jit(solution)/shard_map/ppermute | solution.py:500
  4.3 5.5 %copy-start.4 = (f32[768,384]{1,0:T(8,128)S(1)}, f32[768,384]{1,0:T(8,128)}, u32[]{:S(2)}) copy-start(f32[768,384]{1,0:T(8,128)} %up_ref.1) | copy-start | bytes 3538948
  4.3 6.6 %copy-start.6 = (f32[384,768]{1,0:T(8,128)S(1)}, f32[384,768]{1,0:T(8,128)}, u32[]{:S(2)}) copy-start(f32[384,768]{1,0:T(8,128)} %down_ref.1) | copy-start | bytes 3538948
  4.3 7.0 %copy-start.10 = (f32[1,1152]{1,0:T(1,128)S(1)}, f32[1,1152]{1,0:T(1,128)}, u32[]{:S(2)}) copy-start(f32[1,1152]{1,0:T(1,128)} %text_ref.1) | copy-start | bytes 13828
  9.8 15.3 %copy-start.17 = (f32[384]{0:T(512)S(1)}, f32[384]{0:T(512)}, u32[]{:S(2)}) copy-start(f32[384]{0:T(512)} %bias_any.1) | copy-start | bytes 4612
  9.9 16.5 %collective-permute-start.4 = (f32[768,384]{1,0:T(8,128)S(1)}, f32[768,384]{1,0:T(8,128)}, u32[]{:S(2)}, u32[]{:S(2)}) collective-permute-start(f32[768,384]{1,0:T(8,128)S(1)} %copy-done.4), channel_id=1, source_target_pairs={{0,1},{1,0},{2,3},{3,2},{4,5},{5,4},{6,7},{7,6},{8,9},{9,8},{10,11... | collective-permute-start | bytes 3538952 | tf_op jit(solution)/shard_map/ppermute | solution.py:495
  10.9 15.4 %collective-permute-start.6 = (f32[384,768]{1,0:T(8,128)S(1)}, f32[384,768]{1,0:T(8,128)}, u32[]{:S(2)}, u32[]{:S(2)}) collective-permute-start(f32[384,768]{1,0:T(8,128)S(1)} %copy-done.6), channel_id=1, source_target_pairs={{0,1},{1,0},{2,3},{3,2},{4,5},{5,4},{6,7},{7,6},{8,9},{9,8},{10,11... | collective-permute-start | bytes 3538952 | tf_op jit(solution)/shard_map/ppermute | solution.py:495
  11.0 15.2 %collective-permute-start.1 = (f32[200,768]{1,0:T(8,128)}, f32[200,768]{1,0:T(8,128)S(1)}, u32[]{:S(2)}, u32[]{:S(2)}) collective-permute-start(f32[200,768]{1,0:T(8,128)} %get-tuple-element.51.own_any), channel_id=1, source_target_pairs={{0,2},{1,3},{2,0},{3,1},{4,6},{5,7},{6,4},{7,5},{8,10},{9,11},{10,... | collective-permute-start | bytes 1843208 | tf_op jit(solution)/shard_map/ppermute | solution.py:495
  12.1 23.3 %all-to-all-start = ((f32[32,1,2304]{2,1,0:T(1,128)}), f32[32,1,2304]{2,1,0:T(1,128)S(1)}, u32[]{:S(2)}, u32[]{:S(2)}) async-start(f32[32,1,2304]{2,1,0:T(1,128)} %bitcast.1), calls=%async_computation | async-start | bytes 589824 | tf_op jit(solution)/shard_map/all_to_all | solution.py:515
  23.3 1.9 %collective-permute-start.2 = (f32[1,1152]{1,0:T(1,128)S(1)}, f32[1,1152]{1,0:T(1,128)S(1)}, u32[]{:S(2)}, u32[]{:S(2)}) collective-permute-start(f32[1,1152]{1,0:T(1,128)S(1)} %copy-done.10), channel_id=1, source_target_pairs={{0,1},{1,0},{2,3},{3,2},{4,5},{5,4},{6,7},{7,6},{8,9},{9,8},{10,11... | collective-permute-start | bytes 13832 | tf_op jit(solution)/shard_map/ppermute | solution.py:495
  24.3 1.2 %collective-permute-start.3 = (f32[1,1152]{1,0:T(1,128)S(1)}, f32[1,1152]{1,0:T(1,128)S(1)}, u32[]{:S(2)}, u32[]{:S(2)}) collective-permute-start(f32[1,1152]{1,0:T(1,128)S(1)} %collective-permute-done.other_ref.t2_ref), channel_id=1, source_target_pairs={{0,1},{1,0},{2,3},{3,2},{4,5},{5,4},{6,7},{7,6},{8,9},{9,8},{10,11... | collective-permute-start | bytes 13832 | tf_op jit(solution)/shard_map/ppermute | solution.py:495
  25.2 1.2 %collective-permute-start.5 = (f32[384]{0:T(512)S(1)}, f32[384]{0:T(512)S(1)}, u32[]{:S(2)}, u32[]{:S(2)}) collective-permute-start(f32[384]{0:T(512)S(1)} %copy-done.17), channel_id=1, source_target_pairs={{0,1},{1,0},{2,3},{3,2},{4,5},{5,4},{6,7},{7,6},{8,9},{9,8},{10,11... | collective-permute-start | bytes 4616 | tf_op jit(solution)/shard_map/ppermute | solution.py:495
  35.3 4.9 %collective-permute-start.8 = (f32[576,128]{1,0:T(8,128)S(1)}, f32[576,128]{1,0:T(8,128)S(1)}, u32[]{:S(2)}, u32[]{:S(2)}) collective-permute-start(f32[576,128]{1,0:T(8,128)S(1)} %bitcast.17), channel_id=1, source_target_pairs={{0,1},{1,0},{2,3},{3,2},{4,5},{5,4},{6,7},{7,6},{8,9},{9,8},{10,11... | collective-permute-start | bytes 884744 | tf_op jit(solution)/shard_map/ppermute | solution.py:495
  37.6 2.7 %collective-permute-start.7 = (f32[2,1152]{1,0:T(2,128)}, f32[2,1152]{1,0:T(2,128)S(1)}, u32[]{:S(2)}, u32[]{:S(2)}) collective-permute-start(f32[2,1152]{1,0:T(2,128)} %get-tuple-element.58.mine_ref), channel_id=1, source_target_pairs={{0,2},{1,3},{2,0},{3,1},{4,6},{5,7},{6,4},{7,5},{8,10},{9,11},{10,... | collective-permute-start | bytes 27656 | tf_op jit(solution)/shard_map/ppermute | solution.py:495
  41.0 5.0 %copy-start.1 = (f32[400,384]{1,0:T(8,128)S(1)}, f32[400,384]{1,0:T(8,128)}, u32[]{:S(2)}) copy-start(f32[400,384]{1,0:T(8,128)} %get-tuple-element.68.slope_ref) | copy-start | bytes 1843204
  41.0 5.0 %copy-start.3 = (f32[768,1152]{1,0:T(8,128)S(1)}, f32[768,1152]{1,0:T(8,128)}, u32[]{:S(2)}) copy-start(f32[768,1152]{1,0:T(8,128)} %proj_ref.1) | copy-start | bytes 10616836
  41.0 5.0 %copy-start.5 = (f32[768,384]{1,0:T(8,128)S(1)}, f32[768,384]{1,0:T(8,128)}, u32[]{:S(2)}) copy-start(f32[768,384]{1,0:T(8,128)} %up_ref.1) | copy-start | bytes 3538948
  42.3 22.1 %collective-permute-start.11 = (f32[400,768]{1,0:T(8,128)S(1)}, f32[400,768]{1,0:T(8,128)S(1)}, u32[]{:S(2)}, u32[]{:S(2)}) collective-permute-start(f32[400,768]{1,0:T(8,128)S(1)} %copy-done), channel_id=1, source_target_pairs={{0,1},{1,0},{2,3},{3,2},{4,5},{5,4},{6,7},{7,6},{8,9},{9,8},{10,11... | collective-permute-start | bytes 3686408 | tf_op jit(solution)/shard_map/ppermute | solution.py:495
  43.4 2.5 %collective-permute-start.9 = (f32[2,1280]{1,0:T(2,128)S(1)}, f32[2,1280]{1,0:T(2,128)S(1)}, u32[]{:S(2)}, u32[]{:S(2)}) collective-permute-start(f32[2,1280]{1,0:T(2,128)S(1)} %get-tuple-element.65.packed_ref), channel_id=1, source_target_pairs={{0,2},{1,3},{2,0},{3,1},{4,6},{5,7},{6,4},{7,5},{8,10},{9,11},{10,... | collective-permute-start | bytes 30728 | tf_op jit(solution)/shard_map/ppermute | solution.py:495
  44.6 19.7 %collective-permute-start.12 = (f32[400,384]{1,0:T(8,128)}, f32[400,384]{1,0:T(8,128)}, u32[]{:S(2)}, u32[]{:S(2)}) collective-permute-start(f32[400,384]{1,0:T(8,128)} %get-tuple-element.69.slope_sib_ref), channel_id=1, source_target_pairs={{0,1},{1,0},{2,3},{3,2},{4,5},{5,4},{6,7},{7,6},{8,9},{9,8},{10,11... | collective-permute-start | bytes 1843208 | tf_op jit(solution)/shard_map/ppermute | solution.py:495
  46.0 17.2 %copy-start.2 = (f32[2,768]{1,0:T(2,128)S(1)}, f32[2,768]{1,0:T(2,128)}, u32[]{:S(2)}) copy-start(f32[2,768]{1,0:T(2,128)} %get-tuple-element.77.hidden_ref) | copy-start | bytes 18436
  52.5 17.5 %collective-permute-start.10 = (f32[196,768]{1,0:T(8,128)}, f32[196,768]{1,0:T(8,128)}, u32[]{:S(2)}, u32[]{:S(2)}) collective-permute-start(f32[196,768]{1,0:T(8,128)} %get-tuple-element.74), channel_id=1, source_target_pairs={{0,2},{1,3},{2,0},{3,1},{4,6},{5,7},{6,4},{7,5},{8,10},{9,11},{10,... | collective-permute-start | bytes 1806344 | tf_op jit(solution)/shard_map/ppermute | solution.py:495
  53.6 21.4 %all-to-all-start.1 = ((f32[32,1,2304]{2,1,0:T(1,128)}), f32[32,1,2304]{2,1,0:T(1,128)S(1)}, u32[]{:S(2)}, u32[]{:S(2)}) async-start(f32[32,1,2304]{2,1,0:T(1,128)} %bitcast.6), calls=%async_computation.1 | async-start | bytes 589824 | tf_op jit(solution)/shard_map/all_to_all | solution.py:515
  61.3 8.7 %copy-start.8 = (f32[7,7,768]{2,1,0:T(8,128)S(1)}, f32[7,7,768]{2,1,0:T(8,128)}, u32[]{:S(2)}) copy-start(f32[7,7,768]{2,1,0:T(8,128)} %w_ref.1) | copy-start | bytes 451588
  61.3 8.7 %copy-start.12 = (f32[196,768]{1,0:T(8,128)S(1)}, f32[196,768]{1,0:T(8,128)}, u32[]{:S(2)}) copy-start(f32[196,768]{1,0:T(8,128)} %copy-done.11) | copy-start | bytes 1806340
  61.3 8.7 %copy-start.13 = (f32[14,16,128]{2,1,0:T(8,128)S(1)}, f32[14,16,128]{2,1,0:T(8,128)}, u32[]{:S(2)}) copy-start(f32[14,16,128]{2,1,0:T(8,128)} %get-tuple-element.80.rstd_ref) | copy-start | bytes 344068
  61.3 8.7 %copy-start.14 = (f32[1,768]{1,0:T(1,128)S(1)}, f32[1,768]{1,0:T(1,128)}, u32[]{:S(2)}) copy-start(f32[1,768]{1,0:T(1,128)} %get-tuple-element.81.gain_ref) | copy-start | bytes 9220
  61.3 3.0 %collective-permute-start.13 = (f32[4,768]{1,0:T(4,128)S(1)}, f32[4,768]{1,0:T(4,128)S(1)}, u32[]{:S(2)}, u32[]{:S(2)}) collective-permute-start(f32[4,768]{1,0:T(4,128)S(1)} %get-tuple-element.76.grad_ref), channel_id=1, source_target_pairs={{0,1},{1,0},{2,3},{3,2},{4,5},{5,4},{6,7},{7,6},{8,9},{9,8},{10,11... | collective-permute-start | bytes 36872 | tf_op jit(solution)/shard_map/ppermute | solution.py:495
  63.1 1.2 %collective-permute-start.14 = (f32[2,768]{1,0:T(2,128)S(1)}, f32[2,768]{1,0:T(2,128)S(1)}, u32[]{:S(2)}, u32[]{:S(2)}) collective-permute-start(f32[2,768]{1,0:T(2,128)S(1)} %copy-done.2), channel_id=1, source_target_pairs={{0,1},{1,0},{2,3},{3,2},{4,5},{5,4},{6,7},{7,6},{8,9},{9,8},{10,11... | collective-permute-start | bytes 18440 | tf_op jit(solution)/shard_map/ppermute | solution.py:495
  75.4 4.1 %collective-permute-start.15 = (f32[1,1152]{1,0:T(1,128)S(1)}, f32[1,1152]{1,0:T(1,128)S(1)}, u32[]{:S(2)}, u32[]{:S(2)}) collective-permute-start(f32[1,1152]{1,0:T(1,128)S(1)} %get-tuple-element.91), channel_id=1, source_target_pairs={{0,1},{1,0},{2,3},{3,2},{4,5},{5,4},{6,7},{7,6},{8,9},{9,8},{10,11... | collective-permute-start | bytes 13832 | tf_op jit(solution)/shard_map/ppermute | solution.py:495
  76.3 4.0 %collective-permute-start.16 = (f32[1,1152]{1,0:T(1,128)S(1)}, f32[1,1152]{1,0:T(1,128)S(1)}, u32[]{:S(2)}, u32[]{:S(2)}) collective-permute-start(f32[1,1152]{1,0:T(1,128)S(1)} %get-tuple-element.92), channel_id=1, source_target_pairs={{0,4},{4,0},{8,12},{12,8},{16,20},{20,16},{24,28},{28,24},{32,36},... | collective-permute-start | bytes 13832 | tf_op jit(solution)/shard_map/ppermute | solution.py:500
  78.1 4.5 %collective-permute-start.17 = (f32[1,1152]{1,0:T(1,128)S(1)}, f32[1,1152]{1,0:T(1,128)S(1)}, u32[]{:S(2)}, u32[]{:S(2)}) collective-permute-start(f32[1,1152]{1,0:T(1,128)S(1)} %get-tuple-element.93), channel_id=1, source_target_pairs={{0,5},{1,4},{2,7},{3,6},{4,1},{5,0},{6,3},{7,2},{8,13},{9,12},{10,... | collective-permute-start | bytes 13832 | tf_op jit(solution)/shard_map/ppermute | solution.py:508
  (7 other events, 13.0 us)

commit v4 on v3

--- a/solution.py
+++ b/solution.py
@@ -13,7 +13,7 @@
 SMEM = pl.BlockSpec(memory_space=pltpu.SMEM)
 ANY = pl.BlockSpec(memory_space=pl.ANY)
 F32 = jnp.float32
-WIDE = 58
+WIDE = 55
 
 
 def call(kernel, outs, specs, scratch=(), us=1.0, mib=12):
@@ -321,7 +321,7 @@
             pltpu.VMEM((count, embed), F32),
             pltpu.VMEM((count, embed), F32),
         ],
-        us=6.0,
+        us=14.0,
     )(mine, other, texts, texts_sib, dp, scale, shift)
 
 
@@ -332,7 +332,7 @@
 
 def slope_kernel(
     packed_ref, other_ref, unit_ref, inverse_ref, proj_ref, scale_ref, down_ref, down_sib_ref, up_ref, up_sib_ref,
-    slope_ref, slope_sib_ref, loss_ref, const_ref, grad_ref, own_ref, across_ref, sums,
+    slope_ref, slope_sib_ref, hidden_ref, loss_ref, const_ref, grad_ref, own_ref, across_ref, sums,
 ):
     embed = unit_ref.shape[1]
     width = down_ref.shape[0]
@@ -349,6 +349,7 @@
     for k in range(2):
         grad_ref[pl.ds(2 + k, 1), :] = rows[k] * scale_ref[...]
     branch = grad_ref[2:4, :]
+    grad_ref[4:6, :] = hidden_ref[...]
     for s, weight in enumerate((down_ref, down_sib_ref)):
         for k, row in enumerate(row_dots(weight, (branch[0:1], branch[1:2]))):
             grad_ref[pl.ds(k, 1), s * width : (s + 1) * width] = row
@@ -359,36 +360,36 @@
     across_ref[...] = total[offset : offset + positions]
 
 
-def slopes_of(packed, other, unit, inverse, projection, scale, down, down_sib, up, up_sib, slope, slope_sib, positions):
+def slopes_of(packed, other, unit, inverse, projection, scale, down, down_sib, up, up_sib, slope, slope_sib, hidden, positions):
     channels = up.shape[0]
     return call(
         slope_kernel,
-        [(1, LANES), (1, channels), (4, channels), (positions, channels), (positions, channels)],
-        [VMEM] * 12,
+        [(1, LANES), (1, channels), (6, channels), (positions, channels), (positions, channels)],
+        [VMEM] * 13,
         [pltpu.VMEM(packed.shape, F32)],
         us=4.0,
         mib=16,
-    )(packed, other, unit, inverse, projection, scale[None], down, down_sib, up, up_sib, slope, slope_sib)
+    )(packed, other, unit, inverse, projection, scale[None], down, down_sib, up, up_sib, slope, slope_sib, hidden)
 
 
 def last_kernel(
-    both_ref, both_sib_ref, slope_ref, slope_sib_ref, grad_ref, grad_sib_ref, hidden_ref, hidden_sib_ref,
+    both_ref, both_sib_ref, slope_ref, slope_sib_ref, grad_ref, grad_sib_ref,
     up_out, down_out,
 ):
     width = up_out.shape[1]
     rows, rows_sib = grad_ref[...], grad_sib_ref[...]
     up_out[...] = dot(both_ref[...], scaled(slope_ref, rows[:, :width]), ((0,), (0,)))
     up_out[...] += dot(both_sib_ref[...], scaled(slope_sib_ref, rows_sib[:, width:]), ((0,), (0,)))
-    down_out[...] = dot(hidden_ref[:, :width], rows[2:4], ((0,), (0,))) + dot(
-        hidden_sib_ref[:, width:], rows_sib[2:4], ((0,), (0,))
-    )
-
-
-def last_grads(both, both_sib, slope, slope_sib, grad, grad_sib, hidden, hidden_sib):
+    down_out[...] = dot(rows[4:6, :width], rows[2:4], ((0,), (0,))) + dot(
+        rows_sib[4:6, width:], rows_sib[2:4], ((0,), (0,))
+    )
+
+
+def last_grads(both, both_sib, slope, slope_sib, grad, grad_sib):
     channels, width = both.shape[1], slope.shape[1]
     return call(
-        last_kernel, [(channels, width), (width, channels)], [VMEM] * 8, us=0.2, mib=16
-    )(both, both_sib, slope, slope_sib, grad, grad_sib, hidden, hidden_sib)
+        last_kernel, [(channels, width), (width, channels)], [VMEM] * 6, us=0.2, mib=16
+    )(both, both_sib, slope, slope_sib, grad, grad_sib)
 
 
 def back_kernel(
@@ -556,17 +557,18 @@
         part, part_other, texts, texts_sib, place, scale, shift
     )
     packed_other = swapped(packed, 2)
-    packed, both, slope_sib, hidden = lax.optimization_barrier((packed, both, slope_sib, hidden))
-    both_sib, slope_back, hidden_sib = swapped(both, 1), swapped(slope_sib, 1), swapped(hidden, 1)
+    both_sib = swapped(both, 1)
+    packed, slope_sib = lax.optimization_barrier((packed, slope_sib))
+    slope_back = swapped(slope_sib, 1)
     losses, const, grad, own_grad, across_grad = slopes_of(
         packed, packed_other, image_unit, inverse, projection, layer_scale,
-        down_weight, down_sib, up_weight, up_sib, slope, slope_sib, positions,
+        down_weight, down_sib, up_weight, up_sib, slope, slope_sib, hidden, positions,
     )
     across_grad, image_rows = lax.optimization_barrier((across_grad, image_rows))
     other_grad = swapped(across_grad, 2)
     image_units = spread_out(image_rows)
     up_grad, down_grad = last_grads(
-        both, both_sib, slope, slope_back, grad, swapped(grad, 1), hidden, hidden_sib
+        both, both_sib, slope, slope_back, grad, swapped(grad, 1)
     )
     other_grad, up_grad = lax.optimization_barrier((other_grad, up_grad))
     input_grad = back(own_grad, other_grad, both, rstd, dw_kernel, gain, const, images.shape[1])

time: 83.9 us -> 83 us (0.989)
  waiting for transfers between devices: 8.96 us -> 7.42 us
    ppermute x15 -> x14, waiting for transfers between devices: 3.97 us -> 2.45 us  [swapped(): return lax.ppermute(value, 'fsdp', [(i, i ^ by) for i in range(peers)])]
    ppermute x15 -> x14, starting transfers between devices: 12.9 us -> 13.5 us  [swapped(): return lax.ppermute(value, 'fsdp', [(i, i ^ by) for i in range(peers)])]
  transfers between devices with their start and end apart: 20 -> 19, of which waited for: 9 -> 7; matrix products, arithmetic and copies ran while one was open for 0% -> 0% of each run, Pallas kernels for 35% -> 36%
where the time goes in v4:
time: 83 us; the launch traced here: 82.6 us
  starting transfers between devices  39.4 us (47%)
  Pallas kernels  31.2 us (38%)
  waiting for transfers between devices  7.42 us (9%)
  local copies, waits for them, and re-layouts  2.36 us (3%)
  between operations  2.14 us (3%)
    all_to_all x2, starting transfers between devices, spread_out(): lax.all_to_all(rows, 'dp', 0, 0, axis_index_groups=groups, tiled=True)  18.9 us
    ppermute x14, starting transfers between devices, swapped(): return lax.ppermute(value, 'fsdp', [(i, i ^ by) for i in range(peers)])  13.5 us
    pallas_call x1, Pallas kernels, mlp(): call(functools.partial(mlp_kernel, positions=positions), [(rows, channels...  6.29 us
    pallas_call x1, Pallas kernels, slopes_of(): call(slope_kernel, [(1, LANES), (1, channels), (6, channels), (positions,...  5.74 us
    pallas_call x1, Pallas kernels, last_grads(): call(last_kernel, [(channels, width), (width, channels)], [VMEM] * 6, us=...  5.65 us
    pallas_call x1, Pallas kernels, front(): call(front_kernel, [(pl.cdiv(side * side, 8) * 8, channels), (side, 16, L...  5.52 us
    ppermute x2, starting transfers between devices, mirrored(): return lax.ppermute(value, 'dp', [(i, i ^ 1) for i in range(peers)])  5.39 us
    pallas_call x1, Pallas kernels, back(): call(back_kernel, [(side * side * tiles, LANES)], [VMEM, ANY] + [VMEM] *...  5.05 us
  transfers between devices with their start and end apart: 19, of which 7 were waited for; matrix products, arithmetic and copies ran while one was open for 0% of the time, Pallas kernels for 36%

profile of v4, /device:TPU:1, one launch (start us, length us, event | category | flops | bytes accessed | tf_op | source)
XLA Modules:
  0.0 82.6 jit_solution(17656155630632232660)
XLA Ops:
  0.6 3.7 %collective-permute-start = (f32[1,1152]{1,0:T(1,128)}, f32[1,1152]{1,0:T(1,128)S(1)}, u32[]{:S(2)}, u32[]{:S(2)}) collective-permute-start(f32[1,1152]{1,0:T(1,128)} %text_ref.1), channel_id=1, source_target_pairs={{0,4},{4,0},{8,12},{12,8},{16,20},{20,16},{24,28},{28,24},{32,36},... | collective-permute-start | bytes 13832 | tf_op jit(solution)/shard_map/ppermute | solution.py:501
  4.3 5.5 %shard_map.146 = (f32[200,768]{1,0:T(8,128)}, f32[14,16,128]{2,1,0:T(8,128)}, f32[1,768]{1,0:T(1,128)}, f32[1,768]{1,0:T(1,128)}) custom-call(f32[1176,128]{1,0:T(8,128)} %bitcast.22, f32[7,7,768]{2,1,0:T(8,128)} %w_ref.1, f32[768]{0:T(1024)} %gain_any.1), custom_call_target="tpu_custom_call" | custom-call | flops 4600000000 | bytes 12000000 | tf_op jit(solution)/shard_map/pallas_call | solution.py:153
  9.9 1.0 %collective-permute-start.4 = (f32[768,384]{1,0:T(8,128)S(1)}, f32[768,384]{1,0:T(8,128)}, u32[]{:S(2)}, u32[]{:S(2)}) collective-permute-start(f32[768,384]{1,0:T(8,128)S(1)} %copy-done.3), channel_id=1, source_target_pairs={{0,1},{1,0},{2,3},{3,2},{4,5},{5,4},{6,7},{7,6},{8,9},{9,8},{10,11... | collective-permute-start | bytes 3538952 | tf_op jit(solution)/shard_map/ppermute | solution.py:496
  11.3 0.7 shard_map.148
  12.1 11.2 %all-to-all-start = ((f32[32,1,2304]{2,1,0:T(1,128)}), f32[32,1,2304]{2,1,0:T(1,128)S(1)}, u32[]{:S(2)}, u32[]{:S(2)}) async-start(f32[32,1,2304]{2,1,0:T(1,128)} %bitcast.1), calls=%async_computation | async-start | bytes 589824 | tf_op jit(solution)/shard_map/all_to_all | solution.py:516
  23.3 1.0 %collective-permute-start.2 = (f32[1,1152]{1,0:T(1,128)S(1)}, f32[1,1152]{1,0:T(1,128)S(1)}, u32[]{:S(2)}, u32[]{:S(2)}) collective-permute-start(f32[1,1152]{1,0:T(1,128)S(1)} %copy-done.9), channel_id=1, source_target_pairs={{0,1},{1,0},{2,3},{3,2},{4,5},{5,4},{6,7},{7,6},{8,9},{9,8},{10,11... | collective-permute-start | bytes 13832 | tf_op jit(solution)/shard_map/ppermute | solution.py:496
  24.4 0.7 collective-permute-done.2.t1_ref
  25.5 0.8 collective-permute-done.1.across_any
  26.3 0.8 copy-done.16
  27.1 6.3 %shard_map.147 = (f32[400,768]{1,0:T(8,128)}, f32[400,384]{1,0:T(8,128)}, f32[400,384]{1,0:T(8,128)}, f32[2,768]{1,0:T(2,128)}, f32[2,1152]{1,0:T(2,128)}) custom-call(f32[200,768]{1,0:T(8,128)} %get-tuple-element.49.own_any, f32[200,768]{1,0:T(8,128)} %copy-done.16, f32[768,384]{1,0:T(8,128)} %up_ref.1, ...), custom_call_target="tpu_custom_call" | custom-call | flops 5750000128 | bytes 15000000 | tf_op jit(solution)/shard_map/pallas_call | solution.py:249
  33.4 2.0 %all-to-all-done = f32[32,1,2304]{2,1,0:T(1,128)S(1)} async-done(((f32[32,1,2304]{2,1,0:T(1,128)}), f32[32,1,2304]{2,1,0:T(1,128)S(1)}, u32[]{:S(2)}, u32[]{:S(2)}) %all-to-all-start) | async-done | bytes 294944 | tf_op jit(solution)/shard_map/all_to_all | solution.py:516
  35.3 2.2 %collective-permute-start.8 = (f32[576,128]{1,0:T(8,128)S(1)}, f32[576,128]{1,0:T(8,128)S(1)}, u32[]{:S(2)}, u32[]{:S(2)}) collective-permute-start(f32[576,128]{1,0:T(8,128)S(1)} %bitcast.17), channel_id=1, source_target_pairs={{0,1},{1,0},{2,3},{3,2},{4,5},{5,4},{6,7},{7,6},{8,9},{9,8},{10,11... | collective-permute-start | bytes 884744 | tf_op jit(solution)/shard_map/ppermute | solution.py:496
  37.6 1.2 %collective-permute-start.7 = (f32[2,1152]{1,0:T(2,128)}, f32[2,1152]{1,0:T(2,128)S(1)}, u32[]{:S(2)}, u32[]{:S(2)}) collective-permute-start(f32[2,1152]{1,0:T(2,128)} %get-tuple-element.56.mine_ref), channel_id=1, source_target_pairs={{0,2},{1,3},{2,0},{3,1},{4,6},{5,7},{6,4},{7,5},{8,10},{9,11},{10,... | collective-permute-start | bytes 27656 | tf_op jit(solution)/shard_map/ppermute | solution.py:496
  40.0 0.4 collective-permute-start.11
  40.4 0.7 copy-done.8
  41.1 1.1 %shard_map.149 = (f32[2,1152]{1,0:T(2,128)S(1)}, f32[2,128]{1,0:T(2,128)S(1)}, f32[2,1280]{1,0:T(2,128)S(1)}, f32[576,128]{1,0:T(8,128)}) custom-call(f32[2,1152]{1,0:T(2,128)S(1)} %copy-done.8, f32[2,1152]{1,0:T(2,128)S(1)} %collective-permute-done.7.other_ref, f32[576,128]{1,0:T(8,128)S(1)} %bitcast.18, ...), custom_call_target="tpu_custom_call" | custom-call | flops 16099999744 | bytes 42000000 | tf_op jit(solution)/shard_map/pallas_call | solution.py:315
  42.2 1.0 %collective-permute-start.9 = (f32[2,1280]{1,0:T(2,128)S(1)}, f32[2,1280]{1,0:T(2,128)S(1)}, u32[]{:S(2)}, u32[]{:S(2)}) collective-permute-start(f32[2,1280]{1,0:T(2,128)S(1)} %get-tuple-element.61.packed_ref), channel_id=1, source_target_pairs={{0,2},{1,3},{2,0},{3,1},{4,6},{5,7},{6,4},{7,5},{8,10},{9,11},{10,... | collective-permute-start | bytes 30728 | tf_op jit(solution)/shard_map/ppermute | solution.py:496
  43.3 1.4 %collective-permute-start.12 = (f32[400,384]{1,0:T(8,128)}, f32[400,384]{1,0:T(8,128)}, u32[]{:S(2)}, u32[]{:S(2)}) collective-permute-start(f32[400,384]{1,0:T(8,128)} %get-tuple-element.65.slope_sib_ref), channel_id=1, source_target_pairs={{0,1},{1,0},{2,3},{3,2},{4,5},{5,4},{6,7},{7,6},{8,9},{9,8},{10,11... | collective-permute-start | bytes 1843208 | tf_op jit(solution)/shard_map/ppermute | solution.py:496
  44.8 5.7 %shard_map.150 = (f32[1,128]{1,0:T(1,128)}, f32[1,768]{1,0:T(1,128)S(1)}, f32[6,768]{1,0:T(8,128)S(1)}, f32[196,768]{1,0:T(8,128)S(1)}, f32[196,768]{1,0:T(8,128)}) custom-call(f32[2,1280]{1,0:T(2,128)S(1)} %get-tuple-element.61.packed_ref, f32[2,1280]{1,0:T(2,128)S(1)} %collective-permute-done.9.other_ref, f32[2,1152]{1,0:T(2,128)S(1)} %get-tuple-element.62.unit_ref, ...), custom_call_target="tpu_custom_call" | custom-call | flops 4600000000 | bytes 12000000 | tf_op jit(solution)/shard_map/pallas_call | solution.py:365
  50.5 0.8 %copy-done.10 = f32[196,768]{1,0:T(8,128)} copy-done((f32[196,768]{1,0:T(8,128)}, f32[196,768]{1,0:T(8,128)S(1)}, u32[]{:S(2)}) %copy-start.10) | copy-done | bytes 602136
  51.4 1.0 %collective-permute-start.10 = (f32[196,768]{1,0:T(8,128)}, f32[196,768]{1,0:T(8,128)}, u32[]{:S(2)}, u32[]{:S(2)}) collective-permute-start(f32[196,768]{1,0:T(8,128)} %get-tuple-element.71), channel_id=1, source_target_pairs={{0,2},{1,3},{2,0},{3,1},{4,6},{5,7},{6,4},{7,5},{8,10},{9,11},{10,... | collective-permute-start | bytes 1806344 | tf_op jit(solution)/shard_map/ppermute | solution.py:496
  52.4 7.7 %all-to-all-start.1 = ((f32[32,1,2304]{2,1,0:T(1,128)}), f32[32,1,2304]{2,1,0:T(1,128)S(1)}, u32[]{:S(2)}, u32[]{:S(2)}) async-start(f32[32,1,2304]{2,1,0:T(1,128)} %bitcast.6), calls=%async_computation.1 | async-start | bytes 589824 | tf_op jit(solution)/shard_map/all_to_all | solution.py:516
  60.2 2.8 %collective-permute-start.13 = (f32[6,768]{1,0:T(8,128)S(1)}, f32[6,768]{1,0:T(8,128)S(1)}, u32[]{:S(2)}, u32[]{:S(2)}) collective-permute-start(f32[6,768]{1,0:T(8,128)S(1)} %get-tuple-element.73.grad_ref), channel_id=1, source_target_pairs={{0,1},{1,0},{2,3},{3,2},{4,5},{5,4},{6,7},{7,6},{8,9},{9,8},{10,11... | collective-permute-start | bytes 55304 | tf_op jit(solution)/shard_map/ppermute | solution.py:496
  63.0 0.8 %collective-permute-done.13.grad_sib_ref = f32[6,768]{1,0:T(8,128)S(1)} collective-permute-done((f32[6,768]{1,0:T(8,128)S(1)}, f32[6,768]{1,0:T(8,128)S(1)}, u32[]{:S(2)}, u32[]{:S(2)}) %collective-permute-start.13) | collective-permute-done | bytes 18464 | tf_op jit(solution)/shard_map/ppermute | solution.py:496
  63.9 5.7 %shard_map.151 = (f32[768,384]{1,0:T(8,128)}, f32[384,768]{1,0:T(8,128)}) custom-call(f32[400,768]{1,0:T(8,128)S(1)} %copy-done, f32[400,768]{1,0:T(8,128)S(1)} %collective-permute-done.11.both_sib_ref, f32[400,384]{1,0:T(8,128)S(1)} %copy-done.1, f32[400,384]{1,0:T(8,128)} %collective-permute-done.12.slope_sib_ref, ...), custom_call_target="tpu_custom_call" | custom-call | flops 230000000 | bytes 600000 | tf_op jit(solution)/shard_map/pallas_call | solution.py:390
  69.6 5.0 %shard_map.152 = f32[1176,128]{1,0:T(8,128)} custom-call(f32[196,768]{1,0:T(8,128)S(1)} %copy-done.11, f32[196,768]{1,0:T(8,128)} %collective-permute-done.10.other_any, f32[400,768]{1,0:T(8,128)S(1)} %copy-done, f32[14,16,128]{2,1,0:T(8,128)S(1)} %copy-done.12, f32[7,7,768]{2,1,0:T(8,128)S(1)} %copy-done.7, f32[1,768]{1,0:T(1,128)S(1)} %copy-done.14, ...), custom_call_target="tpu_custom_call" | custom-call | flops 4600000000 | bytes 12000000 | tf_op jit(solution)/shard_map/pallas_call | solution.py:443
  75.0 0.4 collective-permute-start.14
  75.5 1.7 %collective-permute-start.15 = (f32[1,1152]{1,0:T(1,128)S(1)}, f32[1,1152]{1,0:T(1,128)S(1)}, u32[]{:S(2)}, u32[]{:S(2)}) collective-permute-start(f32[1,1152]{1,0:T(1,128)S(1)} %get-tuple-element.88), channel_id=1, source_target_pairs={{0,4},{4,0},{8,12},{12,8},{16,20},{20,16},{24,28},{28,24},{32,36},... | collective-permute-start | bytes 13832 | tf_op jit(solution)/shard_map/ppermute | solution.py:501
  77.2 1.6 %collective-permute-start.16 = (f32[1,1152]{1,0:T(1,128)S(1)}, f32[1,1152]{1,0:T(1,128)S(1)}, u32[]{:S(2)}, u32[]{:S(2)}) collective-permute-start(f32[1,1152]{1,0:T(1,128)S(1)} %get-tuple-element.89), channel_id=1, source_target_pairs={{0,5},{1,4},{2,7},{3,6},{4,1},{5,0},{6,3},{7,2},{8,13},{9,12},{10,... | collective-permute-start | bytes 13832 | tf_op jit(solution)/shard_map/ppermute | solution.py:509
  78.8 0.7 collective-permute-done.15.c_ref
  79.4 2.3 %collective-permute-done.16.d_ref = f32[1,1152]{1,0:T(1,128)S(1)} collective-permute-done((f32[1,1152]{1,0:T(1,128)S(1)}, f32[1,1152]{1,0:T(1,128)S(1)}, u32[]{:S(2)}, u32[]{:S(2)}) %collective-permute-start.16) | collective-permute-done | bytes 4640 | tf_op jit(solution)/shard_map/ppermute | solution.py:509
  81.8 0.8 shard_map.154
  (54 shorter events, 1.4 us)
Async XLA Ops:
  0.6 9.2 %collective-permute-start = (f32[1,1152]{1,0:T(1,128)}, f32[1,1152]{1,0:T(1,128)S(1)}, u32[]{:S(2)}, u32[]{:S(2)}) collective-permute-start(f32[1,1152]{1,0:T(1,128)} %text_ref.1), channel_id=1, source_target_pairs={{0,4},{4,0},{8,12},{12,8},{16,20},{20,16},{24,28},{28,24},{32,36},... | collective-permute-start | bytes 13832 | tf_op jit(solution)/shard_map/ppermute | solution.py:501
  4.3 5.5 %copy-start.3 = (f32[768,384]{1,0:T(8,128)S(1)}, f32[768,384]{1,0:T(8,128)}, u32[]{:S(2)}) copy-start(f32[768,384]{1,0:T(8,128)} %up_ref.1) | copy-start | bytes 3538948
  4.3 6.6 %copy-start.5 = (f32[384,768]{1,0:T(8,128)S(1)}, f32[384,768]{1,0:T(8,128)}, u32[]{:S(2)}) copy-start(f32[384,768]{1,0:T(8,128)} %down_ref.1) | copy-start | bytes 3538948
  4.3 7.0 %copy-start.9 = (f32[1,1152]{1,0:T(1,128)S(1)}, f32[1,1152]{1,0:T(1,128)}, u32[]{:S(2)}) copy-start(f32[1,1152]{1,0:T(1,128)} %text_ref.1) | copy-start | bytes 13828
  9.8 15.3 %copy-start.17 = (f32[384]{0:T(512)S(1)}, f32[384]{0:T(512)}, u32[]{:S(2)}) copy-start(f32[384]{0:T(512)} %bias_any.1) | copy-start | bytes 4612
  9.9 16.5 %collective-permute-start.4 = (f32[768,384]{1,0:T(8,128)S(1)}, f32[768,384]{1,0:T(8,128)}, u32[]{:S(2)}, u32[]{:S(2)}) collective-permute-start(f32[768,384]{1,0:T(8,128)S(1)} %copy-done.3), channel_id=1, source_target_pairs={{0,1},{1,0},{2,3},{3,2},{4,5},{5,4},{6,7},{7,6},{8,9},{9,8},{10,11... | collective-permute-start | bytes 3538952 | tf_op jit(solution)/shard_map/ppermute | solution.py:496
  10.9 15.4 %collective-permute-start.6 = (f32[384,768]{1,0:T(8,128)S(1)}, f32[384,768]{1,0:T(8,128)}, u32[]{:S(2)}, u32[]{:S(2)}) collective-permute-start(f32[384,768]{1,0:T(8,128)S(1)} %copy-done.5), channel_id=1, source_target_pairs={{0,1},{1,0},{2,3},{3,2},{4,5},{5,4},{6,7},{7,6},{8,9},{9,8},{10,11... | collective-permute-start | bytes 3538952 | tf_op jit(solution)/shard_map/ppermute | solution.py:496
  11.0 15.2 %collective-permute-start.1 = (f32[200,768]{1,0:T(8,128)}, f32[200,768]{1,0:T(8,128)S(1)}, u32[]{:S(2)}, u32[]{:S(2)}) collective-permute-start(f32[200,768]{1,0:T(8,128)} %get-tuple-element.49.own_any), channel_id=1, source_target_pairs={{0,2},{1,3},{2,0},{3,1},{4,6},{5,7},{6,4},{7,5},{8,10},{9,11},{10,... | collective-permute-start | bytes 1843208 | tf_op jit(solution)/shard_map/ppermute | solution.py:496
  12.1 23.3 %all-to-all-start = ((f32[32,1,2304]{2,1,0:T(1,128)}), f32[32,1,2304]{2,1,0:T(1,128)S(1)}, u32[]{:S(2)}, u32[]{:S(2)}) async-start(f32[32,1,2304]{2,1,0:T(1,128)} %bitcast.1), calls=%async_computation | async-start | bytes 589824 | tf_op jit(solution)/shard_map/all_to_all | solution.py:516
  23.3 1.9 %collective-permute-start.2 = (f32[1,1152]{1,0:T(1,128)S(1)}, f32[1,1152]{1,0:T(1,128)S(1)}, u32[]{:S(2)}, u32[]{:S(2)}) collective-permute-start(f32[1,1152]{1,0:T(1,128)S(1)} %copy-done.9), channel_id=1, source_target_pairs={{0,1},{1,0},{2,3},{3,2},{4,5},{5,4},{6,7},{7,6},{8,9},{9,8},{10,11... | collective-permute-start | bytes 13832 | tf_op jit(solution)/shard_map/ppermute | solution.py:496
  24.3 1.2 %collective-permute-start.3 = (f32[1,1152]{1,0:T(1,128)S(1)}, f32[1,1152]{1,0:T(1,128)S(1)}, u32[]{:S(2)}, u32[]{:S(2)}) collective-permute-start(f32[1,1152]{1,0:T(1,128)S(1)} %collective-permute-done.other_ref.t2_ref), channel_id=1, source_target_pairs={{0,1},{1,0},{2,3},{3,2},{4,5},{5,4},{6,7},{7,6},{8,9},{9,8},{10,11... | collective-permute-start | bytes 13832 | tf_op jit(solution)/shard_map/ppermute | solution.py:496
  25.2 1.2 %collective-permute-start.5 = (f32[384]{0:T(512)S(1)}, f32[384]{0:T(512)S(1)}, u32[]{:S(2)}, u32[]{:S(2)}) collective-permute-start(f32[384]{0:T(512)S(1)} %copy-done.17), channel_id=1, source_target_pairs={{0,1},{1,0},{2,3},{3,2},{4,5},{5,4},{6,7},{7,6},{8,9},{9,8},{10,11... | collective-permute-start | bytes 4616 | tf_op jit(solution)/shard_map/ppermute | solution.py:496
  35.3 5.1 %collective-permute-start.8 = (f32[576,128]{1,0:T(8,128)S(1)}, f32[576,128]{1,0:T(8,128)S(1)}, u32[]{:S(2)}, u32[]{:S(2)}) collective-permute-start(f32[576,128]{1,0:T(8,128)S(1)} %bitcast.17), channel_id=1, source_target_pairs={{0,1},{1,0},{2,3},{3,2},{4,5},{5,4},{6,7},{7,6},{8,9},{9,8},{10,11... | collective-permute-start | bytes 884744 | tf_op jit(solution)/shard_map/ppermute | solution.py:496
  37.6 2.8 %collective-permute-start.7 = (f32[2,1152]{1,0:T(2,128)}, f32[2,1152]{1,0:T(2,128)S(1)}, u32[]{:S(2)}, u32[]{:S(2)}) collective-permute-start(f32[2,1152]{1,0:T(2,128)} %get-tuple-element.56.mine_ref), channel_id=1, source_target_pairs={{0,2},{1,3},{2,0},{3,1},{4,6},{5,7},{6,4},{7,5},{8,10},{9,11},{10,... | collective-permute-start | bytes 27656 | tf_op jit(solution)/shard_map/ppermute | solution.py:496
  40.0 23.9 %collective-permute-start.11 = (f32[400,768]{1,0:T(8,128)}, f32[400,768]{1,0:T(8,128)S(1)}, u32[]{:S(2)}, u32[]{:S(2)}) collective-permute-start(f32[400,768]{1,0:T(8,128)} %get-tuple-element.72.both_ref), channel_id=1, source_target_pairs={{0,1},{1,0},{2,3},{3,2},{4,5},{5,4},{6,7},{7,6},{8,9},{9,8},{10,11... | collective-permute-start | bytes 3686408 | tf_op jit(solution)/shard_map/ppermute | solution.py:496
  41.1 3.7 %copy-start.1 = (f32[400,384]{1,0:T(8,128)S(1)}, f32[400,384]{1,0:T(8,128)}, u32[]{:S(2)}) copy-start(f32[400,384]{1,0:T(8,128)} %get-tuple-element.64.slope_ref) | copy-start | bytes 1843204
  41.1 3.7 %copy-start.2 = (f32[768,1152]{1,0:T(8,128)S(1)}, f32[768,1152]{1,0:T(8,128)}, u32[]{:S(2)}) copy-start(f32[768,1152]{1,0:T(8,128)} %proj_ref.1) | copy-start | bytes 10616836
  41.1 3.7 %copy-start.4 = (f32[768,384]{1,0:T(8,128)S(1)}, f32[768,384]{1,0:T(8,128)}, u32[]{:S(2)}) copy-start(f32[768,384]{1,0:T(8,128)} %up_ref.1) | copy-start | bytes 3538948
  41.1 3.7 %copy-start.6 = (f32[384,768]{1,0:T(8,128)S(1)}, f32[384,768]{1,0:T(8,128)}, u32[]{:S(2)}) copy-start(f32[384,768]{1,0:T(8,128)} %down_ref.1) | copy-start | bytes 3538948
  42.2 2.5 %collective-permute-start.9 = (f32[2,1280]{1,0:T(2,128)S(1)}, f32[2,1280]{1,0:T(2,128)S(1)}, u32[]{:S(2)}, u32[]{:S(2)}) collective-permute-start(f32[2,1280]{1,0:T(2,128)S(1)} %get-tuple-element.61.packed_ref), channel_id=1, source_target_pairs={{0,2},{1,3},{2,0},{3,1},{4,6},{5,7},{6,4},{7,5},{8,10},{9,11},{10,... | collective-permute-start | bytes 30728 | tf_op jit(solution)/shard_map/ppermute | solution.py:496
  43.3 20.6 %collective-permute-start.12 = (f32[400,384]{1,0:T(8,128)}, f32[400,384]{1,0:T(8,128)}, u32[]{:S(2)}, u32[]{:S(2)}) collective-permute-start(f32[400,384]{1,0:T(8,128)} %get-tuple-element.65.slope_sib_ref), channel_id=1, source_target_pairs={{0,1},{1,0},{2,3},{3,2},{4,5},{5,4},{6,7},{7,6},{8,9},{9,8},{10,11... | collective-permute-start | bytes 1843208 | tf_op jit(solution)/shard_map/ppermute | solution.py:496
  44.8 19.1 %copy-start = (f32[400,768]{1,0:T(8,128)S(1)}, f32[400,768]{1,0:T(8,128)}, u32[]{:S(2)}) copy-start(f32[400,768]{1,0:T(8,128)} %get-tuple-element.72.both_ref) | copy-start | bytes 3686404
  51.4 18.2 %collective-permute-start.10 = (f32[196,768]{1,0:T(8,128)}, f32[196,768]{1,0:T(8,128)}, u32[]{:S(2)}, u32[]{:S(2)}) collective-permute-start(f32[196,768]{1,0:T(8,128)} %get-tuple-element.71), channel_id=1, source_target_pairs={{0,2},{1,3},{2,0},{3,1},{4,6},{5,7},{6,4},{7,5},{8,10},{9,11},{10,... | collective-permute-start | bytes 1806344 | tf_op jit(solution)/shard_map/ppermute | solution.py:496
  52.4 22.2 %all-to-all-start.1 = ((f32[32,1,2304]{2,1,0:T(1,128)}), f32[32,1,2304]{2,1,0:T(1,128)S(1)}, u32[]{:S(2)}, u32[]{:S(2)}) async-start(f32[32,1,2304]{2,1,0:T(1,128)} %bitcast.6), calls=%async_computation.1 | async-start | bytes 589824 | tf_op jit(solution)/shard_map/all_to_all | solution.py:516
  60.2 9.4 %copy-start.7 = (f32[7,7,768]{2,1,0:T(8,128)S(1)}, f32[7,7,768]{2,1,0:T(8,128)}, u32[]{:S(2)}) copy-start(f32[7,7,768]{2,1,0:T(8,128)} %w_ref.1) | copy-start | bytes 451588
  60.2 9.4 %copy-start.11 = (f32[196,768]{1,0:T(8,128)S(1)}, f32[196,768]{1,0:T(8,128)}, u32[]{:S(2)}) copy-start(f32[196,768]{1,0:T(8,128)} %copy-done.10) | copy-start | bytes 1806340
  60.2 9.4 %copy-start.12 = (f32[14,16,128]{2,1,0:T(8,128)S(1)}, f32[14,16,128]{2,1,0:T(8,128)}, u32[]{:S(2)}) copy-start(f32[14,16,128]{2,1,0:T(8,128)} %get-tuple-element.76.rstd_ref) | copy-start | bytes 344068
  60.2 9.4 %copy-start.14 = (f32[1,768]{1,0:T(1,128)S(1)}, f32[1,768]{1,0:T(1,128)}, u32[]{:S(2)}) copy-start(f32[1,768]{1,0:T(1,128)} %get-tuple-element.77.gain_ref) | copy-start | bytes 9220
  60.2 3.7 %collective-permute-start.13 = (f32[6,768]{1,0:T(8,128)S(1)}, f32[6,768]{1,0:T(8,128)S(1)}, u32[]{:S(2)}, u32[]{:S(2)}) collective-permute-start(f32[6,768]{1,0:T(8,128)S(1)} %get-tuple-element.73.grad_ref), channel_id=1, source_target_pairs={{0,1},{1,0},{2,3},{3,2},{4,5},{5,4},{6,7},{7,6},{8,9},{9,8},{10,11... | collective-permute-start | bytes 55304 | tf_op jit(solution)/shard_map/ppermute | solution.py:496
  75.0 3.7 %collective-permute-start.14 = (f32[1,1152]{1,0:T(1,128)S(1)}, f32[1,1152]{1,0:T(1,128)S(1)}, u32[]{:S(2)}, u32[]{:S(2)}) collective-permute-start(f32[1,1152]{1,0:T(1,128)S(1)} %get-tuple-element.87), channel_id=1, source_target_pairs={{0,1},{1,0},{2,3},{3,2},{4,5},{5,4},{6,7},{7,6},{8,9},{9,8},{10,11... | collective-permute-start | bytes 13832 | tf_op jit(solution)/shard_map/ppermute | solution.py:496
  75.5 4.0 %collective-permute-start.15 = (f32[1,1152]{1,0:T(1,128)S(1)}, f32[1,1152]{1,0:T(1,128)S(1)}, u32[]{:S(2)}, u32[]{:S(2)}) collective-permute-start(f32[1,1152]{1,0:T(1,128)S(1)} %get-tuple-element.88), channel_id=1, source_target_pairs={{0,4},{4,0},{8,12},{12,8},{16,20},{20,16},{24,28},{28,24},{32,36},... | collective-permute-start | bytes 13832 | tf_op jit(solution)/shard_map/ppermute | solution.py:501
  77.2 4.6 %collective-permute-start.16 = (f32[1,1152]{1,0:T(1,128)S(1)}, f32[1,1152]{1,0:T(1,128)S(1)}, u32[]{:S(2)}, u32[]{:S(2)}) collective-permute-start(f32[1,1152]{1,0:T(1,128)S(1)} %get-tuple-element.89), channel_id=1, source_target_pairs={{0,5},{1,4},{2,7},{3,6},{4,1},{5,0},{6,3},{7,2},{8,13},{9,12},{10,... | collective-permute-start | bytes 13832 | tf_op jit(solution)/shard_map/ppermute | solution.py:509
  (6 other events, 9.0 us)
